TPU v7x, 256 devices: a whole 4x4x8 slice. The times are simulated.
256 devices in a mesh: loop: 32 (over x, y, z_hi), team: 8 (over z_lo, core).
Axes of the slice: x: 4, y: 4, z: 8 (z_hi: 2, z_lo: 4; z = z_hi * 4 + z_lo), core: 2. Of those that a mesh axis runs over, the one named last changes fastest.
Arguments:
- features: bfloat16 [32768, 256], P(('loop', 'team')), may hold values from -6 to 6
- weight: bfloat16 [256, 256], replicated, may hold values from -0.375 to 0.375
- bias: float32 [256], replicated, may hold values from -1 to 1
- node_scale: float32 [32768], P(('loop', 'team')), may hold values from 0.1 to 1
- cotangent: bfloat16 [32768, 256], P(('loop', 'team')), may hold values from -6 to 6
- edge_slot: int32 [32, 8, 32, 96], P('loop', 'team'), may hold values from 0 to 4, as said below
- edge_row: int32 [32, 8, 32, 96], P('loop', 'team'), may hold values from 0 to 127
- edge_col: int32 [32, 8, 32, 96], P('loop', 'team'), may hold values from 0 to 127
- tile_row: int32 [32, 8, 32, 4], P('loop', 'team'), may hold values from 0 to 7
Outputs:
- output: bfloat16 [32768, 256], P(('loop', 'team'))
- feature_grad: bfloat16 [32768, 256], P(('loop', 'team'))
- weight_grad: float32 [256, 256], replicated
- bias_grad: float32 [256], replicated
Inputs may be any that keep to these rules, and one draw needn't show every extreme that they name: `edge_slot`: unused edge slots hold 4 and come after the used ones of each column block; in every device's lists one column block has all 96 edge slots used and another only its first one. Repeated edges count with their multiplicity.
All inputs are finite; a program needn't handle non-finite values.
Results may differ from a plain program's by a relative error of at most 0.01.
Values may be sent and summed in bfloat16 or wider, within the bound.
No kernel may reach another device: no remote copies, remote signals or barrier semaphores. Data moves between devices by JAX's collectives and lax.ppermute only.
A program may use at most 64 MiB of HBM per device.

v0:
```python
from functools import partial
import math

import jax
import jax.numpy as jnp
from jax import lax
from jax.sharding import PartitionSpec as P


def activation_grad(preact, upstream):
    return jax.vjp(partial(jax.nn.gelu, approximate=True), preact)[1](upstream)[0]


def per_device(
    features, weight, bias, node_scale, cotangent, edge_slot, edge_row, edge_col, tile_row
):
    loop_size = lax.axis_size("loop")
    team_size = lax.axis_size("team")
    tile_size = features.shape[0]
    feat_size = features.shape[1]
    block_rows = team_size * tile_size
    slot_count = tile_row.shape[-1]
    edge_count = edge_slot.shape[-1]
    slot_ids = edge_slot.reshape(loop_size, edge_count)
    row_ids = edge_row.reshape(loop_size, edge_count)
    col_ids = edge_col.reshape(loop_size, edge_count)
    tile_rows = tile_row.reshape(loop_size, slot_count)
    clamped = jnp.minimum(slot_ids, slot_count - 1)
    targets = jnp.take_along_axis(tile_rows, clamped, axis=1) * tile_size + row_ids
    active = (slot_ids < slot_count).astype(jnp.bfloat16)

    def column_matrix(number):
        block_ids = jnp.arange(number, dtype=jnp.int32)[:, None]
        matrix = jnp.zeros((number, block_rows, tile_size), jnp.bfloat16)
        return matrix.at[block_ids, targets, col_ids].add(active)

    product = jnp.dot(features, weight, preferred_element_type=jnp.float32)
    scaled = (node_scale[:, None] * product).astype(jnp.bfloat16)
    own_offset = lax.axis_index("team") * tile_size
    initial = lax.dynamic_update_slice_in_dim(
        jnp.zeros((block_rows, feat_size), jnp.float32), scaled.astype(jnp.float32), own_offset, 0
    )
    arrived = lax.all_gather(scaled, "loop", axis=0, tiled=True)
    number = arrived.shape[0] // tile_size
    blocks = arrived.reshape(number, tile_size, feat_size)
    partial_sum = initial + jnp.einsum(
        "bkc,bcf->kf", column_matrix(number), blocks, preferred_element_type=jnp.float32
    )
    summed = lax.psum_scatter(partial_sum, "team", scatter_dimension=0, tiled=True)
    preact = node_scale[:, None] * summed + bias
    grad_act = activation_grad(preact, cotangent.astype(jnp.float32))
    own_scaled = (node_scale[:, None] * grad_act).astype(jnp.bfloat16)
    grad_block = lax.all_gather(own_scaled, "team", axis=0, tiled=True)
    output = jax.nn.gelu(preact, approximate=True).astype(jnp.bfloat16)
    number = tile_size * lax.axis_size("loop") // tile_size
    term = jnp.einsum(
        "bkc,kf->bcf", column_matrix(number), grad_block, preferred_element_type=jnp.float32
    )
    back_total = lax.psum_scatter(
        term.reshape(tile_size * lax.axis_size("loop"), feat_size),
        "loop",
        scatter_dimension=0,
        tiled=True,
    )
    grad_xw = (node_scale[:, None] * (back_total + own_scaled.astype(jnp.float32))).astype(
        jnp.bfloat16
    )
    feature_grad = lax.dot_general(
        grad_xw, weight, (((1,), (1,)), ((), ())), preferred_element_type=jnp.float32
    ).astype(jnp.bfloat16)
    weight_local = lax.dot_general(
        features, grad_xw, (((0,), (0,)), ((), ())), preferred_element_type=jnp.float32
    )
    bias_local = jnp.sum(grad_act, axis=0)
    weight_total, bias_total = lax.psum((weight_local, bias_local), ("loop", "team"))
    factor = 1.0 / math.sqrt(loop_size * team_size * tile_size)
    return (output, feature_grad, weight_total * factor, bias_total * factor)


def solution(mesh):
    placed = (
        P(("loop", "team"), None),
        P(),
        P(),
        P(("loop", "team")),
        P(("loop", "team"), None),
        P("loop", "team", None, None),
        P("loop", "team", None, None),
        P("loop", "team", None, None),
        P("loop", "team", None, None),
    )
    return jax.shard_map(
        per_device,
        mesh=mesh,
        in_specs=placed,
        out_specs=(P(("loop", "team"), None), P(("loop", "team"), None), P(), P()),
        check_vma=False,
    )
```

profile of v0, /device:TPU:1, one launch (start us, length us, event | category | flops | bytes accessed | tf_op | source)
XLA Modules:
  0.0 691.9 jit_solution(145950152087800610)
XLA Ops:
  7.2 0.8 copy-done
  8.1 1.6 fusion.2
  9.7 0.0 reduce-scatter.3.cloned.1.call-start
  9.8 0.7 compare_convert_fusion
  10.5 0.1 reshape.149
  10.6 0.7 shift-left_or_fusion
  11.3 0.1 reshape.141
  11.5 25.5 %gather_fusion = s32[3072]{0:T(1024)S(1)} fusion(s32[32,4]{0,1:T(4,128)S(1)} %bitcast.36, s32[3072]{0:T(1024)S(1)} %reshape.141), kind=kCustom, calls=%fused_computation | custom fusion | bytes 49152 | tf_op jit(solution)/shard_map/jit(take_along_axis)/gather | solution.py:29
  37.0 0.1 gather.7
  37.1 0.1 multiply_reduce_fusion
  37.2 0.1 and_reduce_fusion
  37.3 0.1 reshape.147
  37.4 26.7 %scatter_custom_fusion = bf16[4194304]{0:T(1024)(128)(2,1)} fusion(s32[3072]{0:T(1024)S(1)} %reshape.147, bf16[3072]{0:T(1024)(128)(2,1)S(1)} %reshape.149, bf16[]{:T(256)} %constant.16.clone.1), kind=kCustom, calls=%fused_computation.2 | custom fusion | flops 3072 | bytes 8388610
  64.0 42.1 %all-gather.2.cloned.1.call-done = bf16[4096,256]{1,0:T(8,128)(2,1)} async-done(((bf16[128,256]{1,0:T(8,128)(2,1)}), bf16[4096,256]{1,0:T(8,128)(2,1)}) %all-gather.2.cloned.1.call-update) | async-done | bytes 2097168 | tf_op jit(solution)/shard_map/all_gather | solution.py:43
  106.1 5.4 convolution_bitcast_fusion
  111.6 1.0 copy-done.2
  112.7 0.0 reduce-scatter.5.cloned.1.call-start
  112.8 30.0 %reduce-scatter.3.cloned.1.call-done = f32[128,256]{1,0:T(8,128)} async-done(((f32[1024,256]{1,0:T(8,128)}), f32[128,256]{1,0:T(8,128)}) %reduce-scatter.3.cloned.1.call-update) | async-done | bytes 131088 | tf_op jit(solution)/shard_map/reduce_scatter | solution.py:49
  142.8 1.7 fusion.14
  144.5 0.1 multiply_convert_fusion.1
  144.6 18.9 %all_gather.7 = bf16[1024,256]{1,0:T(8,128)(2,1)S(1)} all-gather(bf16[128,256]{1,0:T(8,128)(2,1)S(1)} %multiply_convert_fusion.1), channel_id=1, replica_groups=mesh['loop'=32,'team'=8] {'team'}, dimensions={0}, use_global_device_ids=true | all-gather | bytes 589824 | tf_op jit(solution)/shard_map/all_gather | solution.py:53
  163.5 7.7 %fusion.3 = f32[32,128,256]{2,1,0:T(8,128)} fusion(bf16[32,1024,128]{2,1,0:T(8,128)(2,1)} %bitcast.38, bf16[1024,256]{1,0:T(8,128)(2,1)S(1)} %all_gather.7), kind=kOutput, calls=%fused_computation.9 | convolution fusion | flops 2147483648 | bytes 13107200 | tf_op jit(solution)/shard_map/bkc,kf->bcf/dot_general | solution.py:56
  171.2 0.0 all-reduce.2.cloned.1.call-start
  171.3 100.2 %psum.15 = f32[256]{0:T(256)S(1)} all-reduce(f32[256]{0:T(256)S(1)} %get-tuple-element.12), channel_id=1, replica_groups=mesh['loop'=32,'team'=8] {'loop','team'}, use_global_device_ids=true, to_apply=%region_5.6 | all-reduce | flops 256 | bytes 2048 | tf_op jit(solution)/shard_map/psum | solution.py:75
  271.4 0.6 broadcast_multiply_fusion.1
  272.0 134.2 %reduce-scatter.5.cloned.1.call-done = f32[128,256]{1,0:T(8,128)} async-done(((f32[4096,256]{1,0:T(8,128)}), f32[128,256]{1,0:T(8,128)}) %reduce-scatter.5.cloned.1.call-update) | async-done | bytes 131088 | tf_op jit(solution)/shard_map/reduce_scatter | solution.py:59
  406.2 1.0 multiply_convert_fusion
  407.2 0.9 convolution_bitcast_fusion.1
  408.2 0.8 convolution_convert_fusion
  409.0 274.6 %all-reduce.2.cloned.1.call-done = f32[256,256]{0,1:T(8,128)} async-done(((f32[256,256]{0,1:T(8,128)}), f32[256,256]{0,1:T(8,128)}) %all-reduce.2.cloned.1.call-update) | async-done | bytes 262160 | tf_op jit(solution)/shard_map/psum | solution.py:75
  683.6 1.0 broadcast_multiply_fusion
  684.6 0.8 copy.16
  (33 shorter events, 0.2 us)
Async XLA Ops:
  7.2 0.9 copy-start
  7.2 4.2 copy-start.1
  7.2 98.9 %all-gather.2.cloned.1.call-start = ((), (), s32[]{:S(2)}) async-start(), calls=%async_computation.2 | async-start | bytes 2162688 | tf_op jit(solution)/shard_map/all_gather | solution.py:43
  9.7 133.1 %reduce-scatter.3.cloned.1.call-start = ((), (), s32[]{:S(2)}) async-start(), calls=%async_computation.3 | async-start | bytes 1179648 | tf_op jit(solution)/shard_map/reduce_scatter | solution.py:49
  11.4 25.7 %copy-start.5 = (s32[1,1,32,96]{3,2,1,0:T(8,128)S(1)}, s32[1,1,32,96]{3,2,1,0:T(8,128)}, u32[]{:S(2)}) copy-start(s32[1,1,32,96]{3,2,1,0:T(8,128)} %param.14) | copy-start | bytes 36868
  11.4 25.7 %copy-start.7 = (s32[1,1,32,96]{3,2,1,0:T(8,128)S(1)}, s32[1,1,32,96]{3,2,1,0:T(8,128)}, u32[]{:S(2)}) copy-start(s32[1,1,32,96]{3,2,1,0:T(8,128)} %param.16) | copy-start | bytes 36868
  11.4 25.6 %copy-start.8 = (s32[1,1,32,96]{3,2,1,0:T(8,128)S(1)}, s32[1,1,32,96]{3,2,1,0:T(8,128)}, u32[]{:S(2)}) copy-start(s32[1,1,32,96]{3,2,1,0:T(8,128)} %param.15) | copy-start | bytes 36868
  11.4 25.7 %copy-start.12 = (s32[3]{0:T(128)S(1)}, s32[3]{0:T(128)}, u32[]{:S(2)}) copy-start(s32[3]{0:T(128)} %constant.60) | copy-start | bytes 40
  11.4 25.8 %copy-start.11 = (s32[3]{0:T(128)S(1)}, s32[3]{0:T(128)}, u32[]{:S(2)}) copy-start(s32[3]{0:T(128)} %constant.63) | copy-start | bytes 40
  106.1 5.5 copy-start.3
  106.1 36.7 %copy-start.6 = (bf16[128,256]{1,0:T(8,128)(2,1)S(1)}, bf16[128,256]{1,0:T(8,128)(2,1)}, u32[]{:S(2)}) copy-start(bf16[128,256]{1,0:T(8,128)(2,1)} %param.13) | copy-start | bytes 196612
  106.1 36.7 %copy-start.9 = (f32[128]{0:T(128)S(1)}, f32[128]{0:T(128)}, u32[]{:S(2)}) copy-start(f32[128]{0:T(128)} %param.12) | copy-start | bytes 1540
  106.1 36.7 %copy-start.10 = (f32[256]{0:T(256)S(1)}, f32[256]{0:T(256)}, u32[]{:S(2)}) copy-start(f32[256]{0:T(256)} %param.11) | copy-start | bytes 3076
  111.6 1.1 copy-start.2
  112.7 293.5 %reduce-scatter.5.cloned.1.call-start = ((), (), s32[]{:S(2)}) async-start(), calls=%async_computation.4 | async-start | bytes 4325376 | tf_op jit(solution)/shard_map/reduce_scatter | solution.py:59
  171.2 236.0 %copy-start.4 = (bf16[128,256]{1,0:T(8,128)(2,1)S(1)}, bf16[128,256]{1,0:T(8,128)(2,1)}, u32[]{:S(2)}) copy-start(bf16[128,256]{1,0:T(8,128)(2,1)} %param.9) | copy-start | bytes 196612
  171.2 512.4 %all-reduce.2.cloned.1.call-start = ((), (), s32[]{:S(2)}) async-start(), calls=%async_computation.5 | async-start | bytes 524288 | tf_op jit(solution)/shard_map/psum | solution.py:75
Sparse Core Ops, SparseCore 0:
  12.0 94.0 all-gather.1
  112.8 29.9 reduce-scatter.2
  171.3 234.8 reduce-scatter.4
  412.1 271.4 all-reduce.1
where the time goes:
time: 693 us; the launch traced here: 692 us
  waiting for transfers between devices  481 us (69%)
  blocking collectives  119 us (17%)
  other arithmetic  32.6 us (5%)
  local copies, waits for them, and re-layouts  28.6 us (4%)
  matrix products  16.5 us (2%)
  between operations  13.9 us (2%)
    psum x1, waiting for transfers between devices, per_device(): lax.psum((weight_local, bias_local), ('loop', 'team'))  275 us
    reduce_scatter x1, waiting for transfers between devices, per_device(): lax.psum_scatter(term.reshape(tile_size * lax.axis_size('loop'), feat_siz...  134 us
    psum x1, blocking collectives, per_device(): lax.psum((weight_local, bias_local), ('loop', 'team'))  100 us
    all_gather x1, waiting for transfers between devices, per_device(): arrived = lax.all_gather(scaled, 'loop', axis=0, tiled=True)  42.1 us
    reduce_scatter x1, waiting for transfers between devices, per_device(): lax.psum_scatter(partial_sum, 'team', scatter_dimension=0, tiled=True)  30 us
    unnamed x4, other arithmetic  26.8 us
    gather x3, local copies, waits for them, and re-layouts, per_device(): jnp.take_along_axis(tile_rows, clamped, axis=1) * tile_size + row_ids  25.7 us
    all_gather x1, blocking collectives, per_device(): grad_block = lax.all_gather(own_scaled, 'team', axis=0, tiled=True)  18.9 us
  transfers between devices with their start and end apart: 4, of which 4 were waited for; matrix products, arithmetic and copies ran while one was open for 8% of the time, Pallas kernels for 0%

commit v1 on v0

v1 whole, which is shorter than its diff:
```python
import math

import jax
import jax.numpy as jnp
from jax import lax
from jax.experimental import pallas as pl
from jax.experimental.pallas import tpu as pltpu
from jax.sharding import Mesh, PartitionSpec as P

X, Y, H, L, C = 4, 4, 2, 4, 2
XY, ZN = X * Y, H * L
TILE, F, SLOTS, EDGES = 128, 256, 4, 96
HALF = L * TILE
ROWS = C * HALF
E_ALL = XY * EDGES
WZ, WC, BB = F // ZN, F // (ZN * C), 16
ZCHUNK = TILE + WZ + BB
XCHUNK = TILE + WC + BB
F32, BF16, I32 = jnp.float32, jnp.bfloat16, jnp.int32
K0, K1 = math.sqrt(2.0 / math.pi), 0.044715
ALL = ("x", "y", "h", "l", "c")
PARAMS = pltpu.CompilerParams(vmem_limit_bytes=40 * 1024 * 1024)


def dot(a, b):
    return jnp.dot(a, b, preferred_element_type=F32)


def one_hot(index, shape, axis, base=0):
    return (index == lax.broadcasted_iota(I32, shape, axis) + base).astype(F32).astype(BF16)


def split_rows(row):
    high = row.astype(BF16).astype(F32)
    at = lax.broadcasted_iota(I32, (BB, F), 0)
    return jnp.where(at == 0, high, jnp.where(at == 1, row - high, 0.0)).astype(BF16)


def forward_kernel(x_ref, lane_ref, sub_ref, mine_ref, send_ref, gathered):
    for b in range(H):
        for j in range(XY):
            rows = pl.ds(j * EDGES, EDGES)
            pick = one_hot(sub_ref[rows, H + b : H + b + 1], (EDGES, TILE), 1)
            gathered[b, rows, :] = dot(pick, x_ref[j]).astype(BF16)
    step = 256
    for b in range(H):
        for m in range(ROWS // step):
            place = one_hot(lane_ref[b : b + 1, :], (step, E_ALL), 0, m * step)
            total = dot(place, gathered[b])
            if m * step < HALF:
                mine_ref[b, pl.ds(m * step, step), :] = total
            else:
                send_ref[b, pl.ds(m * step - HALF, step), :] = total.astype(BF16)


def middle_kernel(part_ref, x_ref, s_ref, w_ref, bias_ref, ct_ref, out_ref, g_ref, pay_ref):
    s = s_ref[...]
    z = s * x_ref[...].astype(F32)
    for k in range(ZN):
        z += part_ref[k].astype(F32)
    z_high = z.astype(BF16)
    z_low = (z - z_high.astype(F32)).astype(BF16)
    w = w_ref[...]
    p = s * (dot(z_high, w) + dot(z_low, w)) + bias_ref[...]
    square = p * p
    th = jnp.tanh(K0 * (p + K1 * (p * square)))
    out_ref[...] = (0.5 * p * (1.0 + th)).astype(BF16)
    slope = 0.5 * (1.0 + th) + 0.5 * p * (1.0 - th * th) * (K0 * (1.0 + 3.0 * K1 * square))
    grad = ct_ref[...].astype(F32) * slope
    g = (s * grad).astype(BF16)
    g_ref[...] = g
    first = (((0,), (0,)), ((), ()))
    wg = lax.dot_general(z_high, g, first, preferred_element_type=F32)
    wg += lax.dot_general(z_low, g, first, preferred_element_type=F32)
    bias_rows = split_rows(jnp.sum(grad, axis=0, keepdims=True))
    for k in range(ZN):
        pay_ref[k, pl.ds(0, TILE), :] = g
        pay_ref[k, pl.ds(TILE, WZ), :] = wg[k * WZ : (k + 1) * WZ].astype(BF16)
        pay_ref[k, pl.ds(TILE + WZ, BB), :] = bias_rows


def backward_kernel(core_ref, mine_ref, other_ref, sub_ref, col_ref, pay_ref, grads, picked):
    for b in range(H):
        for k in range(L):
            grads[b, pl.ds(k * TILE, TILE), :] = mine_ref[b * L + k, pl.ds(0, TILE), :]
            grads[b, pl.ds(HALF + k * TILE, TILE), :] = other_ref[b * L + k, pl.ds(0, TILE), :]
    wg = jnp.zeros((WZ, F), F32)
    bias_mine = jnp.zeros((BB, F), F32)
    bias_other = jnp.zeros((BB, F), F32)
    for k in range(ZN):
        rows = pl.ds(TILE, WZ)
        wg += mine_ref[k, rows, :].astype(F32) + other_ref[k, rows, :].astype(F32)
        rows = pl.ds(TILE + WZ, BB)
        bias_mine += mine_ref[k, rows, :].astype(F32)
        bias_other += other_ref[k, rows, :].astype(F32)
    bias_rows = split_rows(jnp.sum(bias_mine + bias_other, axis=0, keepdims=True))
    own = jnp.where(core_ref[0] == 0, wg[:WC], wg[WC:]).astype(BF16)
    step = 256
    for b in range(H):
        for m in range(E_ALL // step):
            rows = pl.ds(m * step, step)
            pick = one_hot(sub_ref[rows, b : b + 1], (step, ROWS), 1)
            picked[b, rows, :] = dot(pick, grads[b]).astype(BF16)
    for j in range(XY):
        total = jnp.zeros((TILE, F), F32)
        for b in range(H):
            at = b * XY + j
            place = one_hot(col_ref[at : at + 1, :], (TILE, EDGES), 0)
            total += dot(place, picked[b, pl.ds(j * EDGES, EDGES), :])
        pay_ref[j, pl.ds(0, TILE), :] = total.astype(BF16)
        pay_ref[j, pl.ds(TILE, WC), :] = own
        pay_ref[j, pl.ds(TILE + WC, BB), :] = bias_rows


def final_kernel(part_ref, g_ref, s_ref, w_ref, fg_ref, wrow_ref, bias_ref):
    factor = 1.0 / math.sqrt(XY * ZN * C * TILE)
    back = g_ref[...].astype(F32)
    tail = jnp.zeros((WC + BB, F), F32)
    for k in range(XY):
        back += part_ref[k, pl.ds(0, TILE), :].astype(F32)
        tail += part_ref[k, pl.ds(TILE, WC + BB), :].astype(F32)
    grad_xw = (s_ref[...] * back).astype(BF16)
    fg_ref[...] = lax.dot_general(
        grad_xw, w_ref[...], (((1,), (1,)), ((), ())), preferred_element_type=F32
    ).astype(BF16)
    wrow_ref[...] = tail[:WC] * factor
    bias_ref[...] = jnp.sum(tail[WC:], axis=0, keepdims=True) * factor


def call(kernel, outs, scratch=(), smem=0):
    def run(*args):
        specs = [
            pl.BlockSpec(memory_space=pltpu.SMEM if k < smem else pltpu.VMEM)
            for k in range(len(args))
        ]
        return pl.pallas_call(
            kernel,
            out_shape=[jax.ShapeDtypeStruct(shape, dtype) for shape, dtype in outs],
            in_specs=specs,
            out_specs=[pl.BlockSpec(memory_space=pltpu.VMEM)] * len(outs),
            scratch_shapes=[pltpu.VMEM(shape, dtype) for shape, dtype in scratch],
            compiler_params=PARAMS,
        )(*args)

    return run


def exchange(array, axes):
    return lax.all_to_all(array, axes, 0, 0, tiled=True)


def swap(array, axis):
    return lax.ppermute(array, axis, [(0, 1), (1, 0)])


def per_device(
    features, weight, bias, node_scale, cotangent, edge_slot, edge_row, edge_col, tile_row
):
    h, c = lax.axis_index("h"), lax.axis_index("c")
    s = node_scale[:, None]
    bias = bias[None, :]

    slot = edge_slot.reshape(XY * H, EDGES)
    tiles = tile_row.reshape(XY * H, SLOTS)
    tile = sum(jnp.where(slot == k, tiles[:, k : k + 1], 0) for k in range(SLOTS))
    target = ((tile & 1) ^ c) * HALF + (tile >> 1) * TILE + edge_row.reshape(slot.shape)
    target = jnp.where(slot < SLOTS, target, -1)
    edges = jnp.stack([target, edge_col.reshape(slot.shape)]).reshape(2, XY, H, EDGES)
    kept = lax.dynamic_index_in_dim(edges, h, 2, keepdims=False)
    came = swap(lax.dynamic_index_in_dim(edges, 1 - h, 2, keepdims=False), "h")

    scaled = (s * features.astype(F32)).astype(BF16)
    sources = exchange(jnp.broadcast_to(scaled[None], (XY, TILE, F)), ("x", "y"))

    pairs = jnp.stack([jnp.where(h == 0, kept, came), jnp.where(h == 0, came, kept)], axis=1)
    lane = pairs.reshape(2 * H, E_ALL)
    sub = lane.T
    columns = pairs[1].reshape(H * XY, EDGES)

    mine, send = call(
        forward_kernel,
        [((H, HALF, F), F32), ((H, HALF, F), BF16)],
        [((H, E_ALL, F), BF16)],
    )(sources, lane, sub)
    partial = (mine + swap(send, "c").astype(F32)).astype(BF16).reshape(ZN, TILE, F)
    partial = exchange(partial, ("h", "l"))
    output, g, pay = call(
        middle_kernel,
        [((TILE, F), BF16), ((TILE, F), BF16), ((ZN, ZCHUNK, F), BF16)],
    )(partial, features, s, weight, bias, cotangent)
    around = exchange(pay, ("h", "l"))
    other = swap(around, "c")
    (terms,) = call(
        backward_kernel,
        [((XY, XCHUNK, F), BF16)],
        [((H, ROWS, F), BF16), ((H, E_ALL, F), BF16)],
        smem=1,
    )(c.astype(I32)[None], around, other, sub, columns)
    terms = exchange(terms, ("x", "y"))
    feature_grad, w_rows, bias_grad = call(
        final_kernel,
        [((TILE, F), BF16), ((WC, F), F32), ((1, F), F32)],
    )(terms, g, s, weight)
    w_other = swap(w_rows, "c")
    w_pair = jnp.where(
        c == 0, jnp.concatenate([w_rows, w_other]), jnp.concatenate([w_other, w_rows])
    )
    w_grad = exchange(jnp.broadcast_to(w_pair[None], (ZN, WZ, F)), ("h", "l"))
    return output, feature_grad, w_grad.reshape(F, F), bias_grad.reshape(F)


def solution(mesh):
    fine = Mesh(mesh.devices.reshape(X, Y, H, L, C), ALL)
    rows, edges = P(ALL, None), P(("x", "y", "h"), ("l", "c"), None, None)
    return jax.shard_map(
        per_device,
        mesh=fine,
        in_specs=(rows, P(), P(), P(ALL), rows, edges, edges, edges, edges),
        out_specs=(rows, rows, P(), P()),
        check_vma=False,
    )
```

time: 693 us -> 132 us (0.19)
  waiting for transfers between devices: 481 us -> 29.4 us
  blocking collectives: 119 us -> 60.9 us
  other arithmetic: 32.6 us -> 2.08 us
  starting transfers between devices: 0.16 us -> 28.6 us
  local copies, waits for them, and re-layouts: 28.6 us -> 2.79 us
  matrix products: 16.5 us -> 0 us
  between operations: 13.9 us -> 0.8 us
    psum x1 -> x0, waiting for transfers between devices: 275 us -> none  [per_device(): lax.psum((weight_local, bias_local), ('loop', 'team'))]
    reduce_scatter x2 -> x0, waiting for transfers between devices: 164 us -> none  [the longest x1 134 us: per_device(): lax.psum_scatter(term.reshape(tile_size * lax.axis_size('loop'), feat_siz...]
    psum x1 -> x0, blocking collectives: 100 us -> none  [per_device(): lax.psum((weight_local, bias_local), ('loop', 'team'))]
    all_to_all x0 -> x3, blocking collectives: none -> 60.9 us  [exchange(): return lax.all_to_all(array, axes, 0, 0, tiled=True)]
    all_gather x1 -> x0, waiting for transfers between devices: 42.1 us -> none  [per_device(): arrived = lax.all_gather(scaled, 'loop', axis=0, tiled=True)]
    unnamed x4 -> x0, other arithmetic: 26.8 us -> none
    gather x3 -> x0, local copies, waits for them, and re-layouts: 25.7 us -> none  [per_device(): jnp.take_along_axis(tile_rows, clamped, axis=1) * tile_size + row_ids]
    all_to_all x0 -> x2, waiting for transfers between devices: none -> 24 us  [exchange(): return lax.all_to_all(array, axes, 0, 0, tiled=True)]
  transfers between devices with their start and end apart: 4 -> 6, of which waited for: 4 -> 6; matrix products, arithmetic and copies ran while one was open for 8% -> 1% of each run, Pallas kernels for 0% -> 0%
where the time goes in v1:
time: 132 us; the launch traced here: 131 us
  blocking collectives  60.9 us (46%)
  waiting for transfers between devices  29.4 us (22%)
  starting transfers between devices  28.6 us (22%)
  Pallas kernels  6.69 us (5%)
  local copies, waits for them, and re-layouts  2.79 us (2%)
  other arithmetic  2.08 us (2%)
    all_to_all x3, blocking collectives, exchange(): return lax.all_to_all(array, axes, 0, 0, tiled=True)  60.9 us
    all_to_all x2, waiting for transfers between devices, exchange(): return lax.all_to_all(array, axes, 0, 0, tiled=True)  24 us
    all_to_all x2, starting transfers between devices, exchange(): return lax.all_to_all(array, axes, 0, 0, tiled=True)  15.9 us
    ppermute x4, starting transfers between devices, swap(): return lax.ppermute(array, axis, [(0, 1), (1, 0)])  12.6 us
    pallas_call x4, Pallas kernels, run(): pl.pallas_call(kernel, out_shape=[jax.ShapeDtypeStruct(shape, dtype) for...  6.69 us
    ppermute x4, waiting for transfers between devices, swap(): return lax.ppermute(array, axis, [(0, 1), (1, 0)])  5.32 us
  transfers between devices with their start and end apart: 6, of which 6 were waited for; matrix products, arithmetic and copies ran while one was open for 1% of the time, Pallas kernels for 0%

profile of v1, /device:TPU:1, one launch (start us, length us, event | category | flops | bytes accessed | tf_op | source)
XLA Modules:
  0.0 131.2 jit_solution(213208275614028317)
XLA Ops:
  0.6 0.9 multiply_convert_fusion
  1.6 1.1 broadcast_in_dim.61
  2.7 7.7 %all-to-all-start = ((bf16[16,128,256]{2,1,0:T(8,128)(2,1)}), bf16[16,128,256]{2,1,0:T(8,128)(2,1)S(1)}, u32[]{:S(2)}, u32[]{:S(2)}) async-start(bf16[16,128,256]{2,1,0:T(8,128)(2,1)} %broadcast_in_dim.61), calls=%async_computation | async-start | bytes 2097152 | tf_op jit(solution)/shard_map/all_to_all | solution.py:149
  10.6 0.1 broadcast_in_dim.62
  10.6 0.1 broadcast_in_dim.64
  10.7 0.1 broadcast_in_dim.66
  10.8 0.1 broadcast_in_dim.68
  10.9 0.1 add_select_fusion
  11.1 0.1 fusion.1
  11.1 7.0 %collective-permute-start = (s32[2,16,96]{2,1,0:T(8,128)S(1)}, s32[2,16,96]{2,1,0:T(8,128)S(1)}, u32[]{:S(2)}, u32[]{:S(2)}) collective-permute-start(s32[2,16,96]{2,1,0:T(8,128)S(1)} %bitcast.39), channel_id=1, source_target_pairs={{0,8},{8,0},{1,9},{9,1},{2,10},{10,2},{3,11},{11,3},{4,12},{12,4},... | collective-permute-start | bytes 36872 | tf_op jit(solution)/shard_map/ppermute | solution.py:153
  18.1 1.1 collective-permute-done
  19.3 0.1 reshape.206.lane_ref
  19.4 0.3 copy.19
  19.7 6.2 %all-to-all-done.x_ref = bf16[16,128,256]{2,1,0:T(8,128)(2,1)S(1)} async-done(((bf16[16,128,256]{2,1,0:T(8,128)(2,1)}), bf16[16,128,256]{2,1,0:T(8,128)(2,1)S(1)}, u32[]{:S(2)}, u32[]{:S(2)}) %all-to-all-start) | async-done | bytes 1048608 | tf_op jit(solution)/shard_map/all_to_all | solution.py:149
  25.9 2.3 %shard_map.120 = (f32[2,512,256]{2,1,0:T(8,128)S(1)}, bf16[2,512,256]{2,1,0:T(8,128)(2,1)S(1)}) custom-call(bf16[16,128,256]{2,1,0:T(8,128)(2,1)S(1)} %all-to-all-done.x_ref, s32[4,1536]{1,0:T(4,128)S(1)} %reshape.206.lane_ref, s32[1536,4]{1,0:T(8,128)S(1)} %bitcast.31), custom_call_target="tpu_custom_call" | custom-call | tf_op jit(solution)/shard_map/pallas_call | solution.py:136
  28.2 3.2 %collective-permute-start.1 = (bf16[2,512,256]{2,1,0:T(8,128)(2,1)S(1)}, bf16[2,512,256]{2,1,0:T(8,128)(2,1)S(1)}, u32[]{:S(2)}, u32[]{:S(2)}) collective-permute-start(bf16[2,512,256]{2,1,0:T(8,128)(2,1)S(1)} %get-tuple-element.13), channel_id=1, source_target_pairs={{0,1},{1,0},{2,3},{3,2},{4,5},{5,4},{6,7},{7,6},{8,9},{9,8},{10,11... | collective-permute-start | bytes 1572872 | tf_op jit(solution)/shard_map/ppermute | solution.py:153
  31.4 1.5 %collective-permute-done.1 = bf16[2,512,256]{2,1,0:T(8,128)(2,1)S(1)} collective-permute-done((bf16[2,512,256]{2,1,0:T(8,128)(2,1)S(1)}, bf16[2,512,256]{2,1,0:T(8,128)(2,1)S(1)}, u32[]{:S(2)}, u32[]{:S(2)}) %collective-permute-start.1) | collective-permute-done | bytes 524320 | tf_op jit(solution)/shard_map/ppermute | solution.py:153
  33.0 0.9 add_convert_fusion
  33.9 8.2 %all-to-all-start.1 = ((bf16[8,128,256]{2,1,0:T(8,128)(2,1)}), bf16[8,128,256]{2,1,0:T(8,128)(2,1)S(1)}, u32[]{:S(2)}, u32[]{:S(2)}) async-start(bf16[8,128,256]{2,1,0:T(8,128)(2,1)} %bitcast.9), calls=%async_computation.1 | async-start | bytes 1048576 | tf_op jit(solution)/shard_map/all_to_all | solution.py:149
  42.1 0.1 copy.20.s_ref
  42.2 17.8 %all-to-all-done.1.part_ref = bf16[8,128,256]{2,1,0:T(8,128)(2,1)S(1)} async-done(((bf16[8,128,256]{2,1,0:T(8,128)(2,1)}), bf16[8,128,256]{2,1,0:T(8,128)(2,1)S(1)}, u32[]{:S(2)}, u32[]{:S(2)}) %all-to-all-start.1) | async-done | bytes 524320 | tf_op jit(solution)/shard_map/all_to_all | solution.py:149
  60.0 1.0 shard_map.121
  61.1 24.4 %all_to_all.25.mine_ref = bf16[8,176,256]{2,1,0:T(8,128)(2,1)S(1)} all-to-all(bf16[8,176,256]{2,1,0:T(8,128)(2,1)S(1)} %get-tuple-element.15), channel_id=1, replica_groups=mesh['x'=4,'y'=4,'h'=2,'l'=4,'c'=2] {'h','l'}, dimensions={0} | all-to-all | bytes 1441792 | tf_op jit(solution)/shard_map/all_to_all | solution.py:149
  85.5 0.6 collective-permute-start.2
  86.1 1.8 %collective-permute-done.2.other_ref = bf16[8,176,256]{2,1,0:T(8,128)(2,1)S(1)} collective-permute-done((bf16[8,176,256]{2,1,0:T(8,128)(2,1)S(1)}, bf16[8,176,256]{2,1,0:T(8,128)(2,1)S(1)}, u32[]{:S(2)}, u32[]{:S(2)}) %collective-permute-start.2) | collective-permute-done | bytes 720928 | tf_op jit(solution)/shard_map/ppermute | solution.py:153
  88.0 2.5 %shard_map.122 = bf16[16,160,256]{2,1,0:T(8,128)(2,1)S(1)} custom-call(s32[1]{0:T(128)} %bitcast.12.core_ref, bf16[8,176,256]{2,1,0:T(8,128)(2,1)S(1)} %all_to_all.25.mine_ref, bf16[8,176,256]{2,1,0:T(8,128)(2,1)S(1)} %collective-permute-done.2.other_ref, s32[1536,4]{1,0:T(8,128)S(1)} %bitcast.32, s32[32,96]{1,0:T(8,128)S(1)} %bitcast.33), custom_call_target="tpu_custom_call" | custom-call | tf_op jit(solution)/shard_map/pallas_call | solution.py:136
  90.4 21.7 %all_to_all.26.part_ref = bf16[16,160,256]{2,1,0:T(8,128)(2,1)S(1)} all-to-all(bf16[16,160,256]{2,1,0:T(8,128)(2,1)S(1)} %shard_map.122), channel_id=1, replica_groups=mesh['x'=4,'y'=4,'h'=2,'l'=4,'c'=2] {'x','y'}, dimensions={0} | all-to-all | bytes 2621440 | tf_op jit(solution)/shard_map/all_to_all | solution.py:149
  112.1 0.9 shard_map.123
  113.0 1.8 %collective-permute-start.3 = (f32[16,256]{1,0:T(8,128)S(1)}, f32[16,256]{1,0:T(8,128)S(1)}, u32[]{:S(2)}, u32[]{:S(2)}) collective-permute-start(f32[16,256]{1,0:T(8,128)S(1)} %get-tuple-element.18), channel_id=1, source_target_pairs={{0,1},{1,0},{2,3},{3,2},{4,5},{5,4},{6,7},{7,6},{8,9},{9,8},{10,11... | collective-permute-start | bytes 49160 | tf_op jit(solution)/shard_map/ppermute | solution.py:153
  114.8 0.8 collective-permute-done.3
  115.7 14.8 %all_to_all.27 = f32[8,32,256]{2,1,0:T(8,128)S(1)} all-to-all(f32[8,32,256]{2,1,0:T(8,128)S(1)} %broadcast_in_dim.74), channel_id=1, replica_groups=mesh['x'=4,'y'=4,'h'=2,'l'=4,'c'=2] {'h','l'}, dimensions={0} | all-to-all | bytes 524288 | tf_op jit(solution)/shard_map/all_to_all | solution.py:149
  130.5 0.7 copy.23
  (30 shorter events, 0.2 us)
Async XLA Ops:
  2.6 7.8 %copy-start.4 = (s32[1,1,32,96]{3,2,1,0:T(8,128)S(1)}, s32[1,1,32,96]{3,2,1,0:T(8,128)}, u32[]{:S(2)}) copy-start(s32[1,1,32,96]{3,2,1,0:T(8,128)} %param.14) | copy-start | bytes 36868
  2.6 7.9 %copy-start.8 = (s32[1,1,32,4]{2,3,1,0:T(4,128)S(1)}, s32[1,1,32,4]{2,3,1,0:T(4,128)}, u32[]{:S(2)}) copy-start(s32[1,1,32,4]{2,3,1,0:T(4,128)} %param.17) | copy-start | bytes 1540
  2.6 8.3 %copy-start.5 = (s32[1,1,32,96]{3,2,1,0:T(8,128)S(1)}, s32[1,1,32,96]{3,2,1,0:T(8,128)}, u32[]{:S(2)}) copy-start(s32[1,1,32,96]{3,2,1,0:T(8,128)} %param.15) | copy-start | bytes 36868
  2.6 8.4 %copy-start.6 = (s32[1,1,32,96]{3,2,1,0:T(8,128)S(1)}, s32[1,1,32,96]{3,2,1,0:T(8,128)}, u32[]{:S(2)}) copy-start(s32[1,1,32,96]{3,2,1,0:T(8,128)} %param.16) | copy-start | bytes 36868
  2.7 23.2 %all-to-all-start = ((bf16[16,128,256]{2,1,0:T(8,128)(2,1)}), bf16[16,128,256]{2,1,0:T(8,128)(2,1)S(1)}, u32[]{:S(2)}, u32[]{:S(2)}) async-start(bf16[16,128,256]{2,1,0:T(8,128)(2,1)} %broadcast_in_dim.61), calls=%async_computation | async-start | bytes 2097152 | tf_op jit(solution)/shard_map/all_to_all | solution.py:149
  11.1 8.1 %collective-permute-start = (s32[2,16,96]{2,1,0:T(8,128)S(1)}, s32[2,16,96]{2,1,0:T(8,128)S(1)}, u32[]{:S(2)}, u32[]{:S(2)}) collective-permute-start(s32[2,16,96]{2,1,0:T(8,128)S(1)} %bitcast.39), channel_id=1, source_target_pairs={{0,8},{8,0},{1,9},{9,1},{2,10},{10,2},{3,11},{11,3},{4,12},{12,4},... | collective-permute-start | bytes 36872 | tf_op jit(solution)/shard_map/ppermute | solution.py:153
  28.2 4.8 %collective-permute-start.1 = (bf16[2,512,256]{2,1,0:T(8,128)(2,1)S(1)}, bf16[2,512,256]{2,1,0:T(8,128)(2,1)S(1)}, u32[]{:S(2)}, u32[]{:S(2)}) collective-permute-start(bf16[2,512,256]{2,1,0:T(8,128)(2,1)S(1)} %get-tuple-element.13), channel_id=1, source_target_pairs={{0,1},{1,0},{2,3},{3,2},{4,5},{5,4},{6,7},{7,6},{8,9},{9,8},{10,11... | collective-permute-start | bytes 1572872 | tf_op jit(solution)/shard_map/ppermute | solution.py:153
  32.9 9.1 %copy-start.7 = (f32[128]{0:T(128)S(1)}, f32[128]{0:T(128)}, u32[]{:S(2)}) copy-start(f32[128]{0:T(128)} %param.12) | copy-start | bytes 1540
  32.9 27.1 %copy-start = (bf16[256,256]{1,0:T(8,128)(2,1)S(1)}, bf16[256,256]{1,0:T(8,128)(2,1)}, u32[]{:S(2)}) copy-start(bf16[256,256]{1,0:T(8,128)(2,1)} %w_ref.3) | copy-start | bytes 393220
  32.9 27.1 %copy-start.1 = (bf16[128,256]{1,0:T(8,128)(2,1)S(1)}, bf16[128,256]{1,0:T(8,128)(2,1)}, u32[]{:S(2)}) copy-start(bf16[128,256]{1,0:T(8,128)(2,1)} %x_ref.1) | copy-start | bytes 196612
  32.9 27.1 %copy-start.2 = (bf16[128,256]{1,0:T(8,128)(2,1)S(1)}, bf16[128,256]{1,0:T(8,128)(2,1)}, u32[]{:S(2)}) copy-start(bf16[128,256]{1,0:T(8,128)(2,1)} %ct_ref.1) | copy-start | bytes 196612
  32.9 27.1 %copy-start.3 = (f32[256]{0:T(256)S(1)}, f32[256]{0:T(256)}, u32[]{:S(2)}) copy-start(f32[256]{0:T(256)} %param.11) | copy-start | bytes 3076
  33.9 26.1 %all-to-all-start.1 = ((bf16[8,128,256]{2,1,0:T(8,128)(2,1)}), bf16[8,128,256]{2,1,0:T(8,128)(2,1)S(1)}, u32[]{:S(2)}, u32[]{:S(2)}) async-start(bf16[8,128,256]{2,1,0:T(8,128)(2,1)} %bitcast.9), calls=%async_computation.1 | async-start | bytes 1048576 | tf_op jit(solution)/shard_map/all_to_all | solution.py:149
  85.5 2.4 %collective-permute-start.2 = (bf16[8,176,256]{2,1,0:T(8,128)(2,1)S(1)}, bf16[8,176,256]{2,1,0:T(8,128)(2,1)S(1)}, u32[]{:S(2)}, u32[]{:S(2)}) collective-permute-start(bf16[8,176,256]{2,1,0:T(8,128)(2,1)S(1)} %all_to_all.25.mine_ref), channel_id=1, source_target_pairs={{0,1},{1,0},{2,3},{3,2},{4,5},{5,4},{6,7},{7,6},{8,9},{9,8},{10,11... | collective-permute-start | bytes 2162696 | tf_op jit(solution)/shard_map/ppermute | solution.py:153
  113.0 2.6 %collective-permute-start.3 = (f32[16,256]{1,0:T(8,128)S(1)}, f32[16,256]{1,0:T(8,128)S(1)}, u32[]{:S(2)}, u32[]{:S(2)}) collective-permute-start(f32[16,256]{1,0:T(8,128)S(1)} %get-tuple-element.18), channel_id=1, source_target_pairs={{0,1},{1,0},{2,3},{3,2},{4,5},{5,4},{6,7},{7,6},{8,9},{9,8},{10,11... | collective-permute-start | bytes 49160 | tf_op jit(solution)/shard_map/ppermute | solution.py:153

commit v2 on v1

--- a/solution.py
+++ b/solution.py
@@ -13,9 +13,9 @@
 HALF = L * TILE
 ROWS = C * HALF
 E_ALL = XY * EDGES
-WZ, WC, BB = F // ZN, F // (ZN * C), 16
-ZCHUNK = TILE + WZ + BB
-XCHUNK = TILE + WC + BB
+WR, BB = F // XY, 16
+ZCHUNK = TILE + WR + BB
+XCHUNK = TILE + WR
 F32, BF16, I32 = jnp.float32, jnp.bfloat16, jnp.int32
 K0, K1 = math.sqrt(2.0 / math.pi), 0.044715
 ALL = ("x", "y", "h", "l", "c")
@@ -53,7 +53,7 @@
                 send_ref[b, pl.ds(m * step - HALF, step), :] = total.astype(BF16)
 
 
-def middle_kernel(part_ref, x_ref, s_ref, w_ref, bias_ref, ct_ref, out_ref, g_ref, pay_ref):
+def middle_kernel(part_ref, x_ref, s_ref, w_ref, bias_ref, ct_ref, out_ref, g_ref, wp_ref):
     s = s_ref[...]
     z = s * x_ref[...].astype(F32)
     for k in range(ZN):
@@ -73,28 +73,39 @@
     wg = lax.dot_general(z_high, g, first, preferred_element_type=F32)
     wg += lax.dot_general(z_low, g, first, preferred_element_type=F32)
     bias_rows = split_rows(jnp.sum(grad, axis=0, keepdims=True))
+    for k in range(XY):
+        wp_ref[k, pl.ds(0, WR), :] = wg[k * WR : (k + 1) * WR].astype(BF16)
+        wp_ref[k, pl.ds(WR, BB), :] = bias_rows
+
+
+def load_kernel(w_ref, g_ref, pay_ref):
+    tail = jnp.zeros((WR + BB, F), F32)
+    for k in range(XY):
+        tail += w_ref[k].astype(F32)
+    own = tail[:WR].astype(BF16)
+    bias_rows = split_rows(jnp.sum(tail[WR:], axis=0, keepdims=True))
+    g = g_ref[...]
     for k in range(ZN):
         pay_ref[k, pl.ds(0, TILE), :] = g
-        pay_ref[k, pl.ds(TILE, WZ), :] = wg[k * WZ : (k + 1) * WZ].astype(BF16)
-        pay_ref[k, pl.ds(TILE + WZ, BB), :] = bias_rows
-
-
-def backward_kernel(core_ref, mine_ref, other_ref, sub_ref, col_ref, pay_ref, grads, picked):
+        pay_ref[k, pl.ds(TILE, WR), :] = own
+        pay_ref[k, pl.ds(TILE + WR, BB), :] = bias_rows
+
+
+def backward_kernel(mine_ref, other_ref, sub_ref, col_ref, pay_ref, bias_ref, grads, picked):
     for b in range(H):
         for k in range(L):
             grads[b, pl.ds(k * TILE, TILE), :] = mine_ref[b * L + k, pl.ds(0, TILE), :]
             grads[b, pl.ds(HALF + k * TILE, TILE), :] = other_ref[b * L + k, pl.ds(0, TILE), :]
-    wg = jnp.zeros((WZ, F), F32)
-    bias_mine = jnp.zeros((BB, F), F32)
-    bias_other = jnp.zeros((BB, F), F32)
+    factor = 1.0 / math.sqrt(XY * ZN * C * TILE)
+    tail_mine = jnp.zeros((WR + BB, F), F32)
+    tail_other = jnp.zeros((WR + BB, F), F32)
     for k in range(ZN):
-        rows = pl.ds(TILE, WZ)
-        wg += mine_ref[k, rows, :].astype(F32) + other_ref[k, rows, :].astype(F32)
-        rows = pl.ds(TILE + WZ, BB)
-        bias_mine += mine_ref[k, rows, :].astype(F32)
-        bias_other += other_ref[k, rows, :].astype(F32)
-    bias_rows = split_rows(jnp.sum(bias_mine + bias_other, axis=0, keepdims=True))
-    own = jnp.where(core_ref[0] == 0, wg[:WC], wg[WC:]).astype(BF16)
+        rows = pl.ds(TILE, WR + BB)
+        tail_mine += mine_ref[k, rows, :].astype(F32)
+        tail_other += other_ref[k, rows, :].astype(F32)
+    tail = (tail_mine + tail_other) * factor
+    own = tail[:WR].astype(BF16)
+    bias_ref[...] = jnp.sum(tail[WR:], axis=0, keepdims=True)
     step = 256
     for b in range(H):
         for m in range(E_ALL // step):
@@ -108,41 +119,28 @@
             place = one_hot(col_ref[at : at + 1, :], (TILE, EDGES), 0)
             total += dot(place, picked[b, pl.ds(j * EDGES, EDGES), :])
         pay_ref[j, pl.ds(0, TILE), :] = total.astype(BF16)
-        pay_ref[j, pl.ds(TILE, WC), :] = own
-        pay_ref[j, pl.ds(TILE + WC, BB), :] = bias_rows
-
-
-def final_kernel(part_ref, g_ref, s_ref, w_ref, fg_ref, wrow_ref, bias_ref):
-    factor = 1.0 / math.sqrt(XY * ZN * C * TILE)
+        pay_ref[j, pl.ds(TILE, WR), :] = own
+
+
+def final_kernel(part_ref, g_ref, s_ref, w_ref, fg_ref, wg_ref):
     back = g_ref[...].astype(F32)
-    tail = jnp.zeros((WC + BB, F), F32)
     for k in range(XY):
         back += part_ref[k, pl.ds(0, TILE), :].astype(F32)
-        tail += part_ref[k, pl.ds(TILE, WC + BB), :].astype(F32)
+        wg_ref[pl.ds(k * WR, WR), :] = part_ref[k, pl.ds(TILE, WR), :].astype(F32)
     grad_xw = (s_ref[...] * back).astype(BF16)
     fg_ref[...] = lax.dot_general(
         grad_xw, w_ref[...], (((1,), (1,)), ((), ())), preferred_element_type=F32
     ).astype(BF16)
-    wrow_ref[...] = tail[:WC] * factor
-    bias_ref[...] = jnp.sum(tail[WC:], axis=0, keepdims=True) * factor
-
-
-def call(kernel, outs, scratch=(), smem=0):
-    def run(*args):
-        specs = [
-            pl.BlockSpec(memory_space=pltpu.SMEM if k < smem else pltpu.VMEM)
-            for k in range(len(args))
-        ]
-        return pl.pallas_call(
-            kernel,
-            out_shape=[jax.ShapeDtypeStruct(shape, dtype) for shape, dtype in outs],
-            in_specs=specs,
-            out_specs=[pl.BlockSpec(memory_space=pltpu.VMEM)] * len(outs),
-            scratch_shapes=[pltpu.VMEM(shape, dtype) for shape, dtype in scratch],
-            compiler_params=PARAMS,
-        )(*args)
-
-    return run
+
+
+def call(kernel, outs, scratch=()):
+    return pl.pallas_call(
+        kernel,
+        out_shape=[jax.ShapeDtypeStruct(shape, dtype) for shape, dtype in outs],
+        out_specs=[pl.BlockSpec(memory_space=pltpu.VMEM)] * len(outs),
+        scratch_shapes=[pltpu.VMEM(shape, dtype) for shape, dtype in scratch],
+        compiler_params=PARAMS,
+    )
 
 
 def exchange(array, axes):
@@ -184,29 +182,24 @@
     )(sources, lane, sub)
     partial = (mine + swap(send, "c").astype(F32)).astype(BF16).reshape(ZN, TILE, F)
     partial = exchange(partial, ("h", "l"))
-    output, g, pay = call(
+    output, g, w_parts = call(
         middle_kernel,
-        [((TILE, F), BF16), ((TILE, F), BF16), ((ZN, ZCHUNK, F), BF16)],
+        [((TILE, F), BF16), ((TILE, F), BF16), ((XY, WR + BB, F), BF16)],
     )(partial, features, s, weight, bias, cotangent)
+    w_parts = exchange(w_parts, ("x", "y"))
+    (pay,) = call(load_kernel, [((ZN, ZCHUNK, F), BF16)])(w_parts, g)
     around = exchange(pay, ("h", "l"))
     other = swap(around, "c")
-    (terms,) = call(
+    terms, bias_grad = call(
         backward_kernel,
-        [((XY, XCHUNK, F), BF16)],
+        [((XY, XCHUNK, F), BF16), ((1, F), F32)],
         [((H, ROWS, F), BF16), ((H, E_ALL, F), BF16)],
-        smem=1,
-    )(c.astype(I32)[None], around, other, sub, columns)
+    )(around, other, sub, columns)
     terms = exchange(terms, ("x", "y"))
-    feature_grad, w_rows, bias_grad = call(
-        final_kernel,
-        [((TILE, F), BF16), ((WC, F), F32), ((1, F), F32)],
+    feature_grad, weight_grad = call(
+        final_kernel, [((TILE, F), BF16), ((F, F), F32)]
     )(terms, g, s, weight)
-    w_other = swap(w_rows, "c")
-    w_pair = jnp.where(
-        c == 0, jnp.concatenate([w_rows, w_other]), jnp.concatenate([w_other, w_rows])
-    )
-    w_grad = exchange(jnp.broadcast_to(w_pair[None], (ZN, WZ, F)), ("h", "l"))
-    return output, feature_grad, w_grad.reshape(F, F), bias_grad.reshape(F)
+    return output, feature_grad, weight_grad, bias_grad.reshape(F)
 
 
 def solution(mesh):

time: 132 us -> 122 us (0.924)
  blocking collectives: 60.9 us -> 51.1 us
  starting transfers between devices: 28.6 us -> 30 us
    all_to_all x3, blocking collectives: 60.9 us -> 51.1 us  [exchange(): return lax.all_to_all(array, axes, 0, 0, tiled=True)]
    ppermute x4 -> x3, starting transfers between devices: 12.6 us -> 14.1 us  [swap(): return lax.ppermute(array, axis, [(0, 1), (1, 0)])]
    ppermute x4 -> x3, waiting for transfers between devices: 5.32 us -> 4.38 us  [swap(): return lax.ppermute(array, axis, [(0, 1), (1, 0)])]
    pallas_call x4 -> x5, Pallas kernels: 6.69 us -> 7.2 us  [the longest x1 2.91 us: per_device(): call(backward_kernel, [((XY, XCHUNK, F), BF16), ((1, F), F32)], [((H, ROW...]
  transfers between devices with their start and end apart: 6 -> 5, of which waited for: 6 -> 5; matrix products, arithmetic and copies ran while one was open for 1% -> 1% of each run, Pallas kernels for 0% -> 0%
where the time goes in v2:
time: 122 us
  blocking collectives  51.1 us (42%)
  starting transfers between devices  30 us (25%)
  waiting for transfers between devices  28.4 us (23%)
  Pallas kernels  7.2 us (6%)
  other arithmetic  2.08 us (2%)
  local copies, waits for them, and re-layouts  2.07 us (2%)
    all_to_all x3, blocking collectives, exchange(): return lax.all_to_all(array, axes, 0, 0, tiled=True)  51.1 us
    all_to_all x2, waiting for transfers between devices, exchange(): return lax.all_to_all(array, axes, 0, 0, tiled=True)  24 us
    all_to_all x2, starting transfers between devices, exchange(): return lax.all_to_all(array, axes, 0, 0, tiled=True)  15.9 us
    ppermute x3, starting transfers between devices, swap(): return lax.ppermute(array, axis, [(0, 1), (1, 0)])  14.1 us
    ppermute x3, waiting for transfers between devices, swap(): return lax.ppermute(array, axis, [(0, 1), (1, 0)])  4.38 us
    pallas_call x1, Pallas kernels, per_device(): call(backward_kernel, [((XY, XCHUNK, F), BF16), ((1, F), F32)], [((H, ROW...  2.91 us
  transfers between devices with their start and end apart: 5, of which 5 were waited for; matrix products, arithmetic and copies ran while one was open for 1% of the time, Pallas kernels for 0%

profile of v2, /device:TPU:1, one launch (start us, length us, event | category | flops | bytes accessed | tf_op | source)
XLA Modules:
  0.0 121.7 jit_solution(11511379754521608696)
XLA Ops:
  0.6 0.9 multiply_convert_fusion
  1.6 1.1 broadcast_in_dim.52
  2.7 7.7 %all-to-all-start = ((bf16[16,128,256]{2,1,0:T(8,128)(2,1)}), bf16[16,128,256]{2,1,0:T(8,128)(2,1)S(1)}, u32[]{:S(2)}, u32[]{:S(2)}) async-start(bf16[16,128,256]{2,1,0:T(8,128)(2,1)} %broadcast_in_dim.52), calls=%async_computation | async-start | bytes 2097152 | tf_op jit(solution)/shard_map/all_to_all | solution.py:147
  10.6 0.1 broadcast_in_dim.59
  10.6 0.1 broadcast_in_dim.57
  10.7 0.1 broadcast_in_dim.55
  10.8 0.1 broadcast_in_dim.53
  10.9 0.0 copy-done.5
  10.9 0.1 add_select_fusion
  11.1 0.0 copy-done.6
  11.1 0.1 fusion.1
  11.1 7.0 %collective-permute-start = (s32[2,16,96]{2,1,0:T(8,128)S(1)}, s32[2,16,96]{2,1,0:T(8,128)S(1)}, u32[]{:S(2)}, u32[]{:S(2)}) collective-permute-start(s32[2,16,96]{2,1,0:T(8,128)S(1)} %bitcast.36), channel_id=1, source_target_pairs={{0,8},{8,0},{1,9},{9,1},{2,10},{10,2},{3,11},{11,3},{4,12},{12,4},... | collective-permute-start | bytes 36872 | tf_op jit(solution)/shard_map/ppermute | solution.py:151
  18.1 1.1 collective-permute-done
  19.3 0.1 reshape.174.lane_ref
  19.4 0.3 copy.19
  19.7 6.2 %all-to-all-done.x_ref = bf16[16,128,256]{2,1,0:T(8,128)(2,1)S(1)} async-done(((bf16[16,128,256]{2,1,0:T(8,128)(2,1)}), bf16[16,128,256]{2,1,0:T(8,128)(2,1)S(1)}, u32[]{:S(2)}, u32[]{:S(2)}) %all-to-all-start) | async-done | bytes 1048608 | tf_op jit(solution)/shard_map/all_to_all | solution.py:147
  25.9 2.3 %shard_map.120 = (f32[2,512,256]{2,1,0:T(8,128)S(1)}, bf16[2,512,256]{2,1,0:T(8,128)(2,1)S(1)}) custom-call(bf16[16,128,256]{2,1,0:T(8,128)(2,1)S(1)} %all-to-all-done.x_ref, s32[4,1536]{1,0:T(4,128)S(1)} %reshape.174.lane_ref, s32[1536,4]{1,0:T(8,128)S(1)} %bitcast.29), custom_call_target="tpu_custom_call" | custom-call | tf_op jit(solution)/shard_map/pallas_call | solution.py:178
  28.2 3.2 %collective-permute-start.1 = (bf16[2,512,256]{2,1,0:T(8,128)(2,1)S(1)}, bf16[2,512,256]{2,1,0:T(8,128)(2,1)S(1)}, u32[]{:S(2)}, u32[]{:S(2)}) collective-permute-start(bf16[2,512,256]{2,1,0:T(8,128)(2,1)S(1)} %get-tuple-element.14), channel_id=1, source_target_pairs={{0,1},{1,0},{2,3},{3,2},{4,5},{5,4},{6,7},{7,6},{8,9},{9,8},{10,11... | collective-permute-start | bytes 1572872 | tf_op jit(solution)/shard_map/ppermute | solution.py:151
  31.4 1.5 %collective-permute-done.1 = bf16[2,512,256]{2,1,0:T(8,128)(2,1)S(1)} collective-permute-done((bf16[2,512,256]{2,1,0:T(8,128)(2,1)S(1)}, bf16[2,512,256]{2,1,0:T(8,128)(2,1)S(1)}, u32[]{:S(2)}, u32[]{:S(2)}) %collective-permute-start.1) | collective-permute-done | bytes 524320 | tf_op jit(solution)/shard_map/ppermute | solution.py:151
  33.0 0.9 add_convert_fusion
  33.9 8.2 %all-to-all-start.1 = ((bf16[8,128,256]{2,1,0:T(8,128)(2,1)}), bf16[8,128,256]{2,1,0:T(8,128)(2,1)S(1)}, u32[]{:S(2)}, u32[]{:S(2)}) async-start(bf16[8,128,256]{2,1,0:T(8,128)(2,1)} %bitcast.9), calls=%async_computation.1 | async-start | bytes 1048576 | tf_op jit(solution)/shard_map/all_to_all | solution.py:147
  42.1 0.1 copy.20.s_ref
  42.2 17.8 %all-to-all-done.1.part_ref = bf16[8,128,256]{2,1,0:T(8,128)(2,1)S(1)} async-done(((bf16[8,128,256]{2,1,0:T(8,128)(2,1)}), bf16[8,128,256]{2,1,0:T(8,128)(2,1)S(1)}, u32[]{:S(2)}, u32[]{:S(2)}) %all-to-all-start.1) | async-done | bytes 524320 | tf_op jit(solution)/shard_map/all_to_all | solution.py:147
  60.0 1.0 shard_map.121
  61.1 10.3 %all_to_all.25.w_ref = bf16[16,32,256]{2,1,0:T(8,128)(2,1)S(1)} all-to-all(bf16[16,32,256]{2,1,0:T(8,128)(2,1)S(1)} %get-tuple-element.16), channel_id=1, replica_groups=mesh['x'=4,'y'=4,'h'=2,'l'=4,'c'=2] {'x','y'}, dimensions={0} | all-to-all | bytes 524288 | tf_op jit(solution)/shard_map/all_to_all | solution.py:147
  71.3 0.1 shard_map.122
  71.4 19.8 %all_to_all.26.mine_ref = bf16[8,160,256]{2,1,0:T(8,128)(2,1)S(1)} all-to-all(bf16[8,160,256]{2,1,0:T(8,128)(2,1)S(1)} %shard_map.122), channel_id=1, replica_groups=mesh['x'=4,'y'=4,'h'=2,'l'=4,'c'=2] {'h','l'}, dimensions={0} | all-to-all | bytes 1310720 | tf_op jit(solution)/shard_map/all_to_all | solution.py:147
  91.2 3.9 %collective-permute-start.2 = (bf16[8,160,256]{2,1,0:T(8,128)(2,1)S(1)}, bf16[8,160,256]{2,1,0:T(8,128)(2,1)S(1)}, u32[]{:S(2)}, u32[]{:S(2)}) collective-permute-start(bf16[8,160,256]{2,1,0:T(8,128)(2,1)S(1)} %all_to_all.26.mine_ref), channel_id=1, source_target_pairs={{0,1},{1,0},{2,3},{3,2},{4,5},{5,4},{6,7},{7,6},{8,9},{9,8},{10,11... | collective-permute-start | bytes 1966088 | tf_op jit(solution)/shard_map/ppermute | solution.py:151
  95.0 1.7 %collective-permute-done.2.other_ref = bf16[8,160,256]{2,1,0:T(8,128)(2,1)S(1)} collective-permute-done((bf16[8,160,256]{2,1,0:T(8,128)(2,1)S(1)}, bf16[8,160,256]{2,1,0:T(8,128)(2,1)S(1)}, u32[]{:S(2)}, u32[]{:S(2)}) %collective-permute-start.2) | collective-permute-done | bytes 655392 | tf_op jit(solution)/shard_map/ppermute | solution.py:151
  96.8 2.9 %shard_map.123 = (bf16[16,144,256]{2,1,0:T(8,128)(2,1)S(1)}, f32[1,256]{1,0:T(1,128)}) custom-call(bf16[8,160,256]{2,1,0:T(8,128)(2,1)S(1)} %all_to_all.26.mine_ref, bf16[8,160,256]{2,1,0:T(8,128)(2,1)S(1)} %collective-permute-done.2.other_ref, s32[1536,4]{1,0:T(8,128)S(1)} %bitcast.30, s32[32,96]{1,0:T(8,128)S(1)} %bitcast.31), custom_call_target="tpu_custom_call" | custom-call | tf_op jit(solution)/shard_map/pallas_call | solution.py:193
  99.7 21.1 %all_to_all.27.part_ref = bf16[16,144,256]{2,1,0:T(8,128)(2,1)S(1)} all-to-all(bf16[16,144,256]{2,1,0:T(8,128)(2,1)S(1)} %get-tuple-element.18), channel_id=1, replica_groups=mesh['x'=4,'y'=4,'h'=2,'l'=4,'c'=2] {'x','y'}, dimensions={0} | all-to-all | bytes 2359296 | tf_op jit(solution)/shard_map/all_to_all | solution.py:147
  120.7 0.9 shard_map.124
  (26 shorter events, 0.2 us)
Async XLA Ops:
  2.6 7.8 %copy-start.4 = (s32[1,1,32,96]{3,2,1,0:T(8,128)S(1)}, s32[1,1,32,96]{3,2,1,0:T(8,128)}, u32[]{:S(2)}) copy-start(s32[1,1,32,96]{3,2,1,0:T(8,128)} %param.14) | copy-start | bytes 36868
  2.6 7.9 %copy-start.8 = (s32[1,1,32,4]{2,3,1,0:T(4,128)S(1)}, s32[1,1,32,4]{2,3,1,0:T(4,128)}, u32[]{:S(2)}) copy-start(s32[1,1,32,4]{2,3,1,0:T(4,128)} %param.17) | copy-start | bytes 1540
  2.6 8.3 %copy-start.5 = (s32[1,1,32,96]{3,2,1,0:T(8,128)S(1)}, s32[1,1,32,96]{3,2,1,0:T(8,128)}, u32[]{:S(2)}) copy-start(s32[1,1,32,96]{3,2,1,0:T(8,128)} %param.15) | copy-start | bytes 36868
  2.6 8.4 %copy-start.6 = (s32[1,1,32,96]{3,2,1,0:T(8,128)S(1)}, s32[1,1,32,96]{3,2,1,0:T(8,128)}, u32[]{:S(2)}) copy-start(s32[1,1,32,96]{3,2,1,0:T(8,128)} %param.16) | copy-start | bytes 36868
  2.7 23.2 %all-to-all-start = ((bf16[16,128,256]{2,1,0:T(8,128)(2,1)}), bf16[16,128,256]{2,1,0:T(8,128)(2,1)S(1)}, u32[]{:S(2)}, u32[]{:S(2)}) async-start(bf16[16,128,256]{2,1,0:T(8,128)(2,1)} %broadcast_in_dim.52), calls=%async_computation | async-start | bytes 2097152 | tf_op jit(solution)/shard_map/all_to_all | solution.py:147
  11.1 8.1 %collective-permute-start = (s32[2,16,96]{2,1,0:T(8,128)S(1)}, s32[2,16,96]{2,1,0:T(8,128)S(1)}, u32[]{:S(2)}, u32[]{:S(2)}) collective-permute-start(s32[2,16,96]{2,1,0:T(8,128)S(1)} %bitcast.36), channel_id=1, source_target_pairs={{0,8},{8,0},{1,9},{9,1},{2,10},{10,2},{3,11},{11,3},{4,12},{12,4},... | collective-permute-start | bytes 36872 | tf_op jit(solution)/shard_map/ppermute | solution.py:151
  28.2 4.8 %collective-permute-start.1 = (bf16[2,512,256]{2,1,0:T(8,128)(2,1)S(1)}, bf16[2,512,256]{2,1,0:T(8,128)(2,1)S(1)}, u32[]{:S(2)}, u32[]{:S(2)}) collective-permute-start(bf16[2,512,256]{2,1,0:T(8,128)(2,1)S(1)} %get-tuple-element.14), channel_id=1, source_target_pairs={{0,1},{1,0},{2,3},{3,2},{4,5},{5,4},{6,7},{7,6},{8,9},{9,8},{10,11... | collective-permute-start | bytes 1572872 | tf_op jit(solution)/shard_map/ppermute | solution.py:151
  32.9 9.1 %copy-start.7 = (f32[128]{0:T(128)S(1)}, f32[128]{0:T(128)}, u32[]{:S(2)}) copy-start(f32[128]{0:T(128)} %param.12) | copy-start | bytes 1540
  32.9 27.1 %copy-start = (bf16[256,256]{1,0:T(8,128)(2,1)S(1)}, bf16[256,256]{1,0:T(8,128)(2,1)}, u32[]{:S(2)}) copy-start(bf16[256,256]{1,0:T(8,128)(2,1)} %w_ref.3) | copy-start | bytes 393220
  32.9 27.1 %copy-start.1 = (bf16[128,256]{1,0:T(8,128)(2,1)S(1)}, bf16[128,256]{1,0:T(8,128)(2,1)}, u32[]{:S(2)}) copy-start(bf16[128,256]{1,0:T(8,128)(2,1)} %x_ref.1) | copy-start | bytes 196612
  32.9 27.1 %copy-start.2 = (bf16[128,256]{1,0:T(8,128)(2,1)S(1)}, bf16[128,256]{1,0:T(8,128)(2,1)}, u32[]{:S(2)}) copy-start(bf16[128,256]{1,0:T(8,128)(2,1)} %ct_ref.1) | copy-start | bytes 196612
  32.9 27.1 %copy-start.3 = (f32[256]{0:T(256)S(1)}, f32[256]{0:T(256)}, u32[]{:S(2)}) copy-start(f32[256]{0:T(256)} %param.11) | copy-start | bytes 3076
  33.9 26.1 %all-to-all-start.1 = ((bf16[8,128,256]{2,1,0:T(8,128)(2,1)}), bf16[8,128,256]{2,1,0:T(8,128)(2,1)S(1)}, u32[]{:S(2)}, u32[]{:S(2)}) async-start(bf16[8,128,256]{2,1,0:T(8,128)(2,1)} %bitcast.9), calls=%async_computation.1 | async-start | bytes 1048576 | tf_op jit(solution)/shard_map/all_to_all | solution.py:147
  91.2 5.6 %collective-permute-start.2 = (bf16[8,160,256]{2,1,0:T(8,128)(2,1)S(1)}, bf16[8,160,256]{2,1,0:T(8,128)(2,1)S(1)}, u32[]{:S(2)}, u32[]{:S(2)}) collective-permute-start(bf16[8,160,256]{2,1,0:T(8,128)(2,1)S(1)} %all_to_all.26.mine_ref), channel_id=1, source_target_pairs={{0,1},{1,0},{2,3},{3,2},{4,5},{5,4},{6,7},{7,6},{8,9},{9,8},{10,11... | collective-permute-start | bytes 1966088 | tf_op jit(solution)/shard_map/ppermute | solution.py:151

commit v3 on v2

--- a/solution.py
+++ b/solution.py
@@ -13,6 +13,7 @@
 HALF = L * TILE
 ROWS = C * HALF
 E_ALL = XY * EDGES
+STEP = 256
 WR, BB = F // XY, 16
 ZCHUNK = TILE + WR + BB
 XCHUNK = TILE + WR
@@ -36,21 +37,36 @@
     return jnp.where(at == 0, high, jnp.where(at == 1, row - high, 0.0)).astype(BF16)
 
 
-def forward_kernel(x_ref, lane_ref, sub_ref, mine_ref, send_ref, gathered):
+def spread_kernel(x_ref, s_ref, out_ref):
+    scale = jnp.transpose(jnp.broadcast_to(s_ref[...], (TILE, TILE)))
+    for k in range(F // TILE):
+        part = pl.ds(k * TILE, TILE)
+        scaled = (scale * x_ref[:, part].astype(F32)).astype(BF16)
+        for j in range(XY):
+            out_ref[j, :, part] = scaled
+
+
+def forward_send_kernel(x_ref, lane_ref, sub_ref, gathered_ref, send_ref):
     for b in range(H):
         for j in range(XY):
             rows = pl.ds(j * EDGES, EDGES)
             pick = one_hot(sub_ref[rows, H + b : H + b + 1], (EDGES, TILE), 1)
-            gathered[b, rows, :] = dot(pick, x_ref[j]).astype(BF16)
-    step = 256
-    for b in range(H):
-        for m in range(ROWS // step):
-            place = one_hot(lane_ref[b : b + 1, :], (step, E_ALL), 0, m * step)
-            total = dot(place, gathered[b])
-            if m * step < HALF:
-                mine_ref[b, pl.ds(m * step, step), :] = total
-            else:
-                send_ref[b, pl.ds(m * step - HALF, step), :] = total.astype(BF16)
+            gathered_ref[b, rows, :] = dot(pick, x_ref[j]).astype(BF16)
+    for b in range(H):
+        for m in range(HALF // STEP):
+            place = one_hot(lane_ref[b : b + 1, :], (STEP, E_ALL), 0, HALF + m * STEP)
+            send_ref[b, pl.ds(m * STEP, STEP), :] = dot(place, gathered_ref[b]).astype(BF16)
+
+
+def forward_keep_kernel(gathered_ref, lane_ref, mine_ref):
+    for b in range(H):
+        for m in range(HALF // STEP):
+            place = one_hot(lane_ref[b : b + 1, :], (STEP, E_ALL), 0, m * STEP)
+            mine_ref[b, pl.ds(m * STEP, STEP), :] = dot(place, gathered_ref[b])
+
+
+def add_kernel(mine_ref, other_ref, out_ref):
+    out_ref[...] = (mine_ref[...] + other_ref[...].astype(F32)).astype(BF16)
 
 
 def middle_kernel(part_ref, x_ref, s_ref, w_ref, bias_ref, ct_ref, out_ref, g_ref, wp_ref):
@@ -91,11 +107,19 @@
         pay_ref[k, pl.ds(TILE + WR, BB), :] = bias_rows
 
 
-def backward_kernel(mine_ref, other_ref, sub_ref, col_ref, pay_ref, bias_ref, grads, picked):
+def backward_mine_kernel(mine_ref, sub_ref, picked_ref, grads):
     for b in range(H):
         for k in range(L):
-            grads[b, pl.ds(k * TILE, TILE), :] = mine_ref[b * L + k, pl.ds(0, TILE), :]
-            grads[b, pl.ds(HALF + k * TILE, TILE), :] = other_ref[b * L + k, pl.ds(0, TILE), :]
+            grads[pl.ds(k * TILE, TILE), :] = mine_ref[b * L + k, pl.ds(0, TILE), :]
+        for m in range(E_ALL // STEP):
+            rows = pl.ds(m * STEP, STEP)
+            pick = one_hot(sub_ref[rows, b : b + 1], (STEP, HALF), 1)
+            picked_ref[b, rows, :] = dot(pick, grads[...]).astype(BF16)
+
+
+def backward_kernel(
+    picked_ref, mine_ref, other_ref, sub_ref, col_ref, pay_ref, bias_ref, grads, picked
+):
     factor = 1.0 / math.sqrt(XY * ZN * C * TILE)
     tail_mine = jnp.zeros((WR + BB, F), F32)
     tail_other = jnp.zeros((WR + BB, F), F32)
@@ -106,12 +130,14 @@
     tail = (tail_mine + tail_other) * factor
     own = tail[:WR].astype(BF16)
     bias_ref[...] = jnp.sum(tail[WR:], axis=0, keepdims=True)
-    step = 256
-    for b in range(H):
-        for m in range(E_ALL // step):
-            rows = pl.ds(m * step, step)
-            pick = one_hot(sub_ref[rows, b : b + 1], (step, ROWS), 1)
-            picked[b, rows, :] = dot(pick, grads[b]).astype(BF16)
+    for b in range(H):
+        for k in range(L):
+            grads[pl.ds(k * TILE, TILE), :] = other_ref[b * L + k, pl.ds(0, TILE), :]
+        for m in range(E_ALL // STEP):
+            rows = pl.ds(m * STEP, STEP)
+            pick = one_hot(sub_ref[rows, b : b + 1], (STEP, HALF), 1, HALF)
+            value = dot(pick, grads[...]) + picked_ref[b, rows, :].astype(F32)
+            picked[b, rows, :] = value.astype(BF16)
     for j in range(XY):
         total = jnp.zeros((TILE, F), F32)
         for b in range(H):
@@ -133,13 +159,16 @@
     ).astype(BF16)
 
 
-def call(kernel, outs, scratch=()):
+def call(kernel, outs, scratch=(), flops=TILE * F * F):
     return pl.pallas_call(
         kernel,
         out_shape=[jax.ShapeDtypeStruct(shape, dtype) for shape, dtype in outs],
         out_specs=[pl.BlockSpec(memory_space=pltpu.VMEM)] * len(outs),
         scratch_shapes=[pltpu.VMEM(shape, dtype) for shape, dtype in scratch],
         compiler_params=PARAMS,
+        cost_estimate=pl.CostEstimate(
+            flops=flops, bytes_accessed=2 * 1024 * 1024, transcendentals=0
+        ),
     )
 
 
@@ -167,20 +196,25 @@
     kept = lax.dynamic_index_in_dim(edges, h, 2, keepdims=False)
     came = swap(lax.dynamic_index_in_dim(edges, 1 - h, 2, keepdims=False), "h")
 
-    scaled = (s * features.astype(F32)).astype(BF16)
-    sources = exchange(jnp.broadcast_to(scaled[None], (XY, TILE, F)), ("x", "y"))
+    (spread,) = call(spread_kernel, [((XY, TILE, F), BF16)])(features, node_scale[None, :])
+    sources = exchange(spread, ("x", "y"))
 
     pairs = jnp.stack([jnp.where(h == 0, kept, came), jnp.where(h == 0, came, kept)], axis=1)
     lane = pairs.reshape(2 * H, E_ALL)
     sub = lane.T
     columns = pairs[1].reshape(H * XY, EDGES)
 
-    mine, send = call(
-        forward_kernel,
-        [((H, HALF, F), F32), ((H, HALF, F), BF16)],
-        [((H, E_ALL, F), BF16)],
+    gathered, send = call(
+        forward_send_kernel,
+        [((H, E_ALL, F), BF16), ((H, HALF, F), BF16)],
+        flops=4 * E_ALL * F * (HALF + TILE),
     )(sources, lane, sub)
-    partial = (mine + swap(send, "c").astype(F32)).astype(BF16).reshape(ZN, TILE, F)
+    other = swap(send, "c")
+    (mine,) = call(
+        forward_keep_kernel, [((H, HALF, F), F32)], flops=4 * E_ALL * F * HALF
+    )(gathered, lane)
+    (partial,) = call(add_kernel, [((H, HALF, F), BF16)])(mine, other)
+    partial = partial.reshape(ZN, TILE, F)
     partial = exchange(partial, ("h", "l"))
     output, g, w_parts = call(
         middle_kernel,
@@ -190,11 +224,18 @@
     (pay,) = call(load_kernel, [((ZN, ZCHUNK, F), BF16)])(w_parts, g)
     around = exchange(pay, ("h", "l"))
     other = swap(around, "c")
+    (picked,) = call(
+        backward_mine_kernel,
+        [((H, E_ALL, F), BF16)],
+        [((HALF, F), BF16)],
+        flops=4 * E_ALL * F * HALF,
+    )(around, sub)
     terms, bias_grad = call(
         backward_kernel,
         [((XY, XCHUNK, F), BF16), ((1, F), F32)],
-        [((H, ROWS, F), BF16), ((H, E_ALL, F), BF16)],
-    )(around, other, sub, columns)
+        [((HALF, F), BF16), ((H, E_ALL, F), BF16)],
+        flops=4 * E_ALL * F * (HALF + TILE),
+    )(picked, around, other, sub, columns)
     terms = exchange(terms, ("x", "y"))
     feature_grad, weight_grad = call(
         final_kernel, [((TILE, F), BF16), ((F, F), F32)]

time: 122 us -> 121 us (level)
  Pallas kernels: 7.2 us -> 9.76 us
  waiting for transfers between devices: 28.4 us -> 26.4 us
  other arithmetic: 2.08 us -> 0.23 us
    pallas_call x2 -> x6, Pallas kernels: 5.18 us -> 7.73 us  [the longest x1 2.15 us: per_device(): call(backward_kernel, [((XY, XCHUNK, F), BF16), ((1, F), F32)], [((HALF,...]
    ppermute x3, waiting for transfers between devices: 4.38 us -> 2.31 us  [swap(): return lax.ppermute(array, axis, [(0, 1), (1, 0)])]
    convert_element_type x2 -> x0, other arithmetic: 1.85 us -> none  [the longest x1 0.93 us: per_device(): scaled = (s * features.astype(F32)).astype(BF16)]
    unnamed x18 -> x22, local copies, waits for them, and re-layouts: 0.04 us -> 1.55 us
  transfers between devices with their start and end apart: 5 -> 5, of which waited for: 5 -> 5; matrix products, arithmetic and copies ran while one was open for 1% -> 1% of each run, Pallas kernels for 0% -> 2%
where the time goes in v3:
time: 121 us
  blocking collectives  51.1 us (42%)
  starting transfers between devices  29.9 us (25%)
  waiting for transfers between devices  26.4 us (22%)
  Pallas kernels  9.76 us (8%)
  local copies, waits for them, and re-layouts  2.5 us (2%)
    all_to_all x3, blocking collectives, exchange(): return lax.all_to_all(array, axes, 0, 0, tiled=True)  51.1 us
    all_to_all x2, waiting for transfers between devices, exchange(): return lax.all_to_all(array, axes, 0, 0, tiled=True)  24 us
    all_to_all x2, starting transfers between devices, exchange(): return lax.all_to_all(array, axes, 0, 0, tiled=True)  15.8 us
    ppermute x3, starting transfers between devices, swap(): return lax.ppermute(array, axis, [(0, 1), (1, 0)])  14.1 us
  transfers between devices with their start and end apart: 5, of which 5 were waited for; matrix products, arithmetic and copies ran while one was open for 1% of the time, Pallas kernels for 2%

profile of v3, /device:TPU:1, one launch (start us, length us, event | category | flops | bytes accessed | tf_op | source)
XLA Modules:
  0.0 120.6 jit_solution(11879202398202401641)
XLA Ops:
  0.6 0.8 copy-done.1
  1.5 0.7 copy-done.4
  2.1 1.3 %shard_map.120 = bf16[16,128,256]{2,1,0:T(8,128)(2,1)} custom-call(bf16[128,256]{1,0:T(8,128)(2,1)S(1)} %copy-done.1, f32[1,128]{1,0:T(1,128)S(1)} %bitcast.34), custom_call_target="tpu_custom_call" | custom-call | flops 8388608 | bytes 2097152 | tf_op jit(solution)/shard_map/pallas_call | solution.py:199
  3.4 7.6 %all-to-all-start = ((bf16[16,128,256]{2,1,0:T(8,128)(2,1)}), bf16[16,128,256]{2,1,0:T(8,128)(2,1)S(1)}, u32[]{:S(2)}, u32[]{:S(2)}) async-start(bf16[16,128,256]{2,1,0:T(8,128)(2,1)} %shard_map.120), calls=%async_computation | async-start | bytes 2097152 | tf_op jit(solution)/shard_map/all_to_all | solution.py:176
  11.0 0.1 broadcast_in_dim.50
  11.1 0.1 broadcast_in_dim.56
  11.2 0.1 broadcast_in_dim.54
  11.3 0.1 broadcast_in_dim.52
  11.5 0.1 add_select_fusion
  11.8 7.0 %collective-permute-start = (s32[2,16,96]{2,1,0:T(8,128)S(1)}, s32[2,16,96]{2,1,0:T(8,128)S(1)}, u32[]{:S(2)}, u32[]{:S(2)}) collective-permute-start(s32[2,16,96]{2,1,0:T(8,128)S(1)} %bitcast.40), channel_id=1, source_target_pairs={{0,8},{8,0},{1,9},{9,1},{2,10},{10,2},{3,11},{11,3},{4,12},{12,4},... | collective-permute-start | bytes 36872 | tf_op jit(solution)/shard_map/ppermute | solution.py:180
  18.7 1.1 collective-permute-done
  19.9 0.1 reshape.172.lane_ref
  20.0 0.3 copy.20
  20.3 6.2 %all-to-all-done.x_ref = bf16[16,128,256]{2,1,0:T(8,128)(2,1)S(1)} async-done(((bf16[16,128,256]{2,1,0:T(8,128)(2,1)}), bf16[16,128,256]{2,1,0:T(8,128)(2,1)S(1)}, u32[]{:S(2)}, u32[]{:S(2)}) %all-to-all-start) | async-done | bytes 1048608 | tf_op jit(solution)/shard_map/all_to_all | solution.py:176
  26.5 1.5 %shard_map.121 = (bf16[2,1536,256]{2,1,0:T(8,128)(2,1)S(1)}, bf16[2,512,256]{2,1,0:T(8,128)(2,1)S(1)}) custom-call(bf16[16,128,256]{2,1,0:T(8,128)(2,1)S(1)} %all-to-all-done.x_ref, s32[4,1536]{1,0:T(4,128)S(1)} %reshape.172.lane_ref, s32[1536,4]{1,0:T(8,128)S(1)} %bitcast.30), custom_call_target="tpu_custom_call" | custom-call | flops 1006632960 | bytes 2097152 | tf_op jit(solution)/shard_map/pallas_call | solution.py:207
  28.0 3.2 %collective-permute-start.1 = (bf16[2,512,256]{2,1,0:T(8,128)(2,1)S(1)}, bf16[2,512,256]{2,1,0:T(8,128)(2,1)S(1)}, u32[]{:S(2)}, u32[]{:S(2)}) collective-permute-start(bf16[2,512,256]{2,1,0:T(8,128)(2,1)S(1)} %get-tuple-element.14), channel_id=1, source_target_pairs={{0,1},{1,0},{2,3},{3,2},{4,5},{5,4},{6,7},{7,6},{8,9},{9,8},{10,11... | collective-permute-start | bytes 1572872 | tf_op jit(solution)/shard_map/ppermute | solution.py:180
  31.2 1.0 shard_map.122.mine_ref
  32.2 0.5 collective-permute-done.1.other_ref
  32.7 0.9 shard_map.123
  33.6 8.2 %all-to-all-start.1 = ((bf16[8,128,256]{2,1,0:T(8,128)(2,1)}), bf16[8,128,256]{2,1,0:T(8,128)(2,1)S(1)}, u32[]{:S(2)}, u32[]{:S(2)}) async-start(bf16[8,128,256]{2,1,0:T(8,128)(2,1)} %bitcast.10), calls=%async_computation.1 | async-start | bytes 1048576 | tf_op jit(solution)/shard_map/all_to_all | solution.py:176
  41.8 0.1 copy.21.s_ref
  41.9 17.8 %all-to-all-done.1.part_ref = bf16[8,128,256]{2,1,0:T(8,128)(2,1)S(1)} async-done(((bf16[8,128,256]{2,1,0:T(8,128)(2,1)}), bf16[8,128,256]{2,1,0:T(8,128)(2,1)S(1)}, u32[]{:S(2)}, u32[]{:S(2)}) %all-to-all-start.1) | async-done | bytes 524320 | tf_op jit(solution)/shard_map/all_to_all | solution.py:176
  59.8 1.0 shard_map.124
  60.8 10.2 %all_to_all.25.w_ref = bf16[16,32,256]{2,1,0:T(8,128)(2,1)S(1)} all-to-all(bf16[16,32,256]{2,1,0:T(8,128)(2,1)S(1)} %get-tuple-element.16), channel_id=1, replica_groups=mesh['x'=4,'y'=4,'h'=2,'l'=4,'c'=2] {'x','y'}, dimensions={0} | all-to-all | bytes 524288 | tf_op jit(solution)/shard_map/all_to_all | solution.py:176
  71.0 0.1 shard_map.125
  71.1 19.8 %all_to_all.26.mine_ref = bf16[8,160,256]{2,1,0:T(8,128)(2,1)S(1)} all-to-all(bf16[8,160,256]{2,1,0:T(8,128)(2,1)S(1)} %shard_map.125), channel_id=1, replica_groups=mesh['x'=4,'y'=4,'h'=2,'l'=4,'c'=2] {'h','l'}, dimensions={0} | all-to-all | bytes 1310720 | tf_op jit(solution)/shard_map/all_to_all | solution.py:176
  90.9 3.9 %collective-permute-start.2 = (bf16[8,160,256]{2,1,0:T(8,128)(2,1)S(1)}, bf16[8,160,256]{2,1,0:T(8,128)(2,1)S(1)}, u32[]{:S(2)}, u32[]{:S(2)}) collective-permute-start(bf16[8,160,256]{2,1,0:T(8,128)(2,1)S(1)} %all_to_all.26.mine_ref), channel_id=1, source_target_pairs={{0,1},{1,0},{2,3},{3,2},{4,5},{5,4},{6,7},{7,6},{8,9},{9,8},{10,11... | collective-permute-start | bytes 1966088 | tf_op jit(solution)/shard_map/ppermute | solution.py:180
  94.8 1.0 shard_map.126.picked_ref
  95.8 0.7 collective-permute-done.2.other_ref
  96.5 2.1 %shard_map.127 = (bf16[16,144,256]{2,1,0:T(8,128)(2,1)S(1)}, f32[1,256]{1,0:T(1,128)}) custom-call(bf16[2,1536,256]{2,1,0:T(8,128)(2,1)S(1)} %shard_map.126.picked_ref, bf16[8,160,256]{2,1,0:T(8,128)(2,1)S(1)} %all_to_all.26.mine_ref, bf16[8,160,256]{2,1,0:T(8,128)(2,1)S(1)} %collective-permute-done.2.other_ref, s32[1536,4]{1,0:T(8,128)S(1)} %bitcast.32, ...), custom_call_target="tpu_custom_call" | custom-call | flops 1006632960 | bytes 2097152 | tf_op jit(solution)/shard_map/pallas_call | solution.py:233
  98.6 21.1 %all_to_all.27.part_ref = bf16[16,144,256]{2,1,0:T(8,128)(2,1)S(1)} all-to-all(bf16[16,144,256]{2,1,0:T(8,128)(2,1)S(1)} %get-tuple-element.18), channel_id=1, replica_groups=mesh['x'=4,'y'=4,'h'=2,'l'=4,'c'=2] {'x','y'}, dimensions={0} | all-to-all | bytes 2359296 | tf_op jit(solution)/shard_map/all_to_all | solution.py:176
  119.7 0.9 shard_map.128
  (31 shorter events, 0.3 us)
Async XLA Ops:
  0.6 0.8 copy-start.1
  1.5 0.7 copy-start.4
  2.1 8.9 %copy-start.10 = (s32[1,1,32,4]{2,3,1,0:T(4,128)S(1)}, s32[1,1,32,4]{2,3,1,0:T(4,128)}, u32[]{:S(2)}) copy-start(s32[1,1,32,4]{2,3,1,0:T(4,128)} %param.17) | copy-start | bytes 1540
  2.1 9.3 %copy-start.7 = (s32[1,1,32,96]{3,2,1,0:T(8,128)S(1)}, s32[1,1,32,96]{3,2,1,0:T(8,128)}, u32[]{:S(2)}) copy-start(s32[1,1,32,96]{3,2,1,0:T(8,128)} %param.14) | copy-start | bytes 36868
  2.1 9.4 %copy-start.8 = (s32[1,1,32,96]{3,2,1,0:T(8,128)S(1)}, s32[1,1,32,96]{3,2,1,0:T(8,128)}, u32[]{:S(2)}) copy-start(s32[1,1,32,96]{3,2,1,0:T(8,128)} %param.15) | copy-start | bytes 36868
  2.1 9.5 %copy-start.9 = (s32[1,1,32,96]{3,2,1,0:T(8,128)S(1)}, s32[1,1,32,96]{3,2,1,0:T(8,128)}, u32[]{:S(2)}) copy-start(s32[1,1,32,96]{3,2,1,0:T(8,128)} %param.16) | copy-start | bytes 36868
  3.4 23.1 %all-to-all-start = ((bf16[16,128,256]{2,1,0:T(8,128)(2,1)}), bf16[16,128,256]{2,1,0:T(8,128)(2,1)S(1)}, u32[]{:S(2)}, u32[]{:S(2)}) async-start(bf16[16,128,256]{2,1,0:T(8,128)(2,1)} %shard_map.120), calls=%async_computation | async-start | bytes 2097152 | tf_op jit(solution)/shard_map/all_to_all | solution.py:176
  11.8 8.1 %collective-permute-start = (s32[2,16,96]{2,1,0:T(8,128)S(1)}, s32[2,16,96]{2,1,0:T(8,128)S(1)}, u32[]{:S(2)}, u32[]{:S(2)}) collective-permute-start(s32[2,16,96]{2,1,0:T(8,128)S(1)} %bitcast.40), channel_id=1, source_target_pairs={{0,8},{8,0},{1,9},{9,1},{2,10},{10,2},{3,11},{11,3},{4,12},{12,4},... | collective-permute-start | bytes 36872 | tf_op jit(solution)/shard_map/ppermute | solution.py:180
  28.0 4.8 %collective-permute-start.1 = (bf16[2,512,256]{2,1,0:T(8,128)(2,1)S(1)}, bf16[2,512,256]{2,1,0:T(8,128)(2,1)S(1)}, u32[]{:S(2)}, u32[]{:S(2)}) collective-permute-start(bf16[2,512,256]{2,1,0:T(8,128)(2,1)S(1)} %get-tuple-element.14), channel_id=1, source_target_pairs={{0,1},{1,0},{2,3},{3,2},{4,5},{5,4},{6,7},{7,6},{8,9},{9,8},{10,11... | collective-permute-start | bytes 1572872 | tf_op jit(solution)/shard_map/ppermute | solution.py:180
  32.2 9.6 %copy-start.5 = (f32[128]{0:T(128)S(1)}, f32[128]{0:T(128)}, u32[]{:S(2)}) copy-start(f32[128]{0:T(128)} %param.12) | copy-start | bytes 1540
  32.2 27.6 %copy-start = (bf16[256,256]{1,0:T(8,128)(2,1)S(1)}, bf16[256,256]{1,0:T(8,128)(2,1)}, u32[]{:S(2)}) copy-start(bf16[256,256]{1,0:T(8,128)(2,1)} %w_ref.3) | copy-start | bytes 393220
  32.2 27.6 %copy-start.2 = (bf16[128,256]{1,0:T(8,128)(2,1)S(1)}, bf16[128,256]{1,0:T(8,128)(2,1)}, u32[]{:S(2)}) copy-start(bf16[128,256]{1,0:T(8,128)(2,1)} %x_ref.3) | copy-start | bytes 196612
  32.2 27.5 %copy-start.3 = (bf16[128,256]{1,0:T(8,128)(2,1)S(1)}, bf16[128,256]{1,0:T(8,128)(2,1)}, u32[]{:S(2)}) copy-start(bf16[128,256]{1,0:T(8,128)(2,1)} %ct_ref.1) | copy-start | bytes 196612
  32.2 27.5 %copy-start.6 = (f32[256]{0:T(256)S(1)}, f32[256]{0:T(256)}, u32[]{:S(2)}) copy-start(f32[256]{0:T(256)} %param.11) | copy-start | bytes 3076
  33.6 26.1 %all-to-all-start.1 = ((bf16[8,128,256]{2,1,0:T(8,128)(2,1)}), bf16[8,128,256]{2,1,0:T(8,128)(2,1)S(1)}, u32[]{:S(2)}, u32[]{:S(2)}) async-start(bf16[8,128,256]{2,1,0:T(8,128)(2,1)} %bitcast.10), calls=%async_computation.1 | async-start | bytes 1048576 | tf_op jit(solution)/shard_map/all_to_all | solution.py:176
  90.9 5.6 %collective-permute-start.2 = (bf16[8,160,256]{2,1,0:T(8,128)(2,1)S(1)}, bf16[8,160,256]{2,1,0:T(8,128)(2,1)S(1)}, u32[]{:S(2)}, u32[]{:S(2)}) collective-permute-start(bf16[8,160,256]{2,1,0:T(8,128)(2,1)S(1)} %all_to_all.26.mine_ref), channel_id=1, source_target_pairs={{0,1},{1,0},{2,3},{3,2},{4,5},{5,4},{6,7},{7,6},{8,9},{9,8},{10,11... | collective-permute-start | bytes 1966088 | tf_op jit(solution)/shard_map/ppermute | solution.py:180

commit v4 on v3

--- a/solution.py
+++ b/solution.py
@@ -1,3 +1,4 @@
+import functools
 import math
 
 import jax
@@ -16,7 +17,6 @@
 STEP = 256
 WR, BB = F // XY, 16
 ZCHUNK = TILE + WR + BB
-XCHUNK = TILE + WR
 F32, BF16, I32 = jnp.float32, jnp.bfloat16, jnp.int32
 K0, K1 = math.sqrt(2.0 / math.pi), 0.044715
 ALL = ("x", "y", "h", "l", "c")
@@ -35,15 +35,6 @@
     high = row.astype(BF16).astype(F32)
     at = lax.broadcasted_iota(I32, (BB, F), 0)
     return jnp.where(at == 0, high, jnp.where(at == 1, row - high, 0.0)).astype(BF16)
-
-
-def spread_kernel(x_ref, s_ref, out_ref):
-    scale = jnp.transpose(jnp.broadcast_to(s_ref[...], (TILE, TILE)))
-    for k in range(F // TILE):
-        part = pl.ds(k * TILE, TILE)
-        scaled = (scale * x_ref[:, part].astype(F32)).astype(BF16)
-        for j in range(XY):
-            out_ref[j, :, part] = scaled
 
 
 def forward_send_kernel(x_ref, lane_ref, sub_ref, gathered_ref, send_ref):
@@ -117,9 +108,7 @@
             picked_ref[b, rows, :] = dot(pick, grads[...]).astype(BF16)
 
 
-def backward_kernel(
-    picked_ref, mine_ref, other_ref, sub_ref, col_ref, pay_ref, bias_ref, grads, picked
-):
+def backward_pick_kernel(picked_ref, mine_ref, other_ref, sub_ref, all_ref, w_ref, bias_ref, grads):
     factor = 1.0 / math.sqrt(XY * ZN * C * TILE)
     tail_mine = jnp.zeros((WR + BB, F), F32)
     tail_other = jnp.zeros((WR + BB, F), F32)
@@ -128,7 +117,7 @@
         tail_mine += mine_ref[k, rows, :].astype(F32)
         tail_other += other_ref[k, rows, :].astype(F32)
     tail = (tail_mine + tail_other) * factor
-    own = tail[:WR].astype(BF16)
+    w_ref[...] = tail[:WR].astype(BF16)
     bias_ref[...] = jnp.sum(tail[WR:], axis=0, keepdims=True)
     for b in range(H):
         for k in range(L):
@@ -137,47 +126,91 @@
             rows = pl.ds(m * STEP, STEP)
             pick = one_hot(sub_ref[rows, b : b + 1], (STEP, HALF), 1, HALF)
             value = dot(pick, grads[...]) + picked_ref[b, rows, :].astype(F32)
-            picked[b, rows, :] = value.astype(BF16)
-    for j in range(XY):
+            all_ref[b, rows, :] = value.astype(BF16)
+
+
+def place_terms(at_x, picked_ref, col_ref, out_ref, dtype):
+    for y in range(Y):
         total = jnp.zeros((TILE, F), F32)
+        j = at_x * Y + y
         for b in range(H):
-            at = b * XY + j
-            place = one_hot(col_ref[at : at + 1, :], (TILE, EDGES), 0)
-            total += dot(place, picked[b, pl.ds(j * EDGES, EDGES), :])
-        pay_ref[j, pl.ds(0, TILE), :] = total.astype(BF16)
-        pay_ref[j, pl.ds(TILE, WR), :] = own
-
-
-def final_kernel(part_ref, g_ref, s_ref, w_ref, fg_ref, wg_ref):
-    back = g_ref[...].astype(F32)
-    for k in range(XY):
-        back += part_ref[k, pl.ds(0, TILE), :].astype(F32)
-        wg_ref[pl.ds(k * WR, WR), :] = part_ref[k, pl.ds(TILE, WR), :].astype(F32)
+            place = one_hot(col_ref[pl.ds(b * XY + j, 1), :], (TILE, EDGES), 0)
+            rows = pl.ds(pl.multiple_of(j * EDGES, 32), EDGES)
+            total += dot(place, picked_ref[b, rows, :])
+        out_ref[pl.ds(y * TILE, TILE), :] = total.astype(dtype)
+
+
+def terms_kernel(step, at_ref, picked_ref, col_ref, w_ref, out_ref):
+    place_terms(lax.rem(at_ref[0] + step, X), picked_ref, col_ref, out_ref, BF16)
+    out_ref[pl.ds(Y * TILE, WR), :] = w_ref[...]
+
+
+def own_terms_kernel(at_ref, picked_ref, col_ref, out_ref):
+    place_terms(at_ref[0], picked_ref, col_ref, out_ref, F32)
+
+
+def x_sum_kernel(at_ref, own_ref, w_ref, first, second, third, one_ref, two_ref, three_ref, keep_ref, total, rows):
+    x, y = at_ref[0], at_ref[1]
+    parts = (first, second, third)
+    value = own_ref[...]
+    for part in parts:
+        value += part[pl.ds(0, Y * TILE), :].astype(F32)
+    total[...] = value
+    rows[pl.ds(pl.multiple_of(x * WR, WR), WR), :] = w_ref[...].astype(F32)
+    for step, part in enumerate(parts, 1):
+        at = pl.multiple_of(lax.rem(x + X - step, X) * WR, WR)
+        rows[pl.ds(at, WR), :] = part[pl.ds(Y * TILE, WR), :].astype(F32)
+    for step, out in enumerate((one_ref, two_ref, three_ref), 1):
+        at = pl.multiple_of(lax.rem(y + step, Y) * TILE, TILE)
+        out[pl.ds(0, TILE), :] = total[pl.ds(at, TILE), :].astype(BF16)
+        out[pl.ds(TILE, X * WR), :] = rows[...].astype(BF16)
+    keep_ref[pl.ds(0, TILE), :] = total[pl.ds(pl.multiple_of(y * TILE, TILE), TILE), :]
+    keep_ref[pl.ds(TILE, X * WR), :] = rows[...]
+
+
+def final_kernel(at_ref, keep_ref, first, second, third, g_ref, s_ref, weight_ref, fg_ref, wg_ref):
+    y = at_ref[1]
+    back = g_ref[...].astype(F32) + keep_ref[pl.ds(0, TILE), :]
+    for step, part in enumerate((keep_ref, first, second, third)):
+        if step:
+            back += part[pl.ds(0, TILE), :].astype(F32)
+        for x in range(X):
+            at = pl.multiple_of((x * Y + lax.rem(y + Y - step, Y)) * WR, WR)
+            wg_ref[pl.ds(at, WR), :] = part[pl.ds(TILE + x * WR, WR), :].astype(F32)
     grad_xw = (s_ref[...] * back).astype(BF16)
     fg_ref[...] = lax.dot_general(
-        grad_xw, w_ref[...], (((1,), (1,)), ((), ())), preferred_element_type=F32
+        grad_xw, weight_ref[...], (((1,), (1,)), ((), ())), preferred_element_type=F32
     ).astype(BF16)
 
 
-def call(kernel, outs, scratch=(), flops=TILE * F * F):
-    return pl.pallas_call(
-        kernel,
-        out_shape=[jax.ShapeDtypeStruct(shape, dtype) for shape, dtype in outs],
-        out_specs=[pl.BlockSpec(memory_space=pltpu.VMEM)] * len(outs),
-        scratch_shapes=[pltpu.VMEM(shape, dtype) for shape, dtype in scratch],
-        compiler_params=PARAMS,
-        cost_estimate=pl.CostEstimate(
-            flops=flops, bytes_accessed=2 * 1024 * 1024, transcendentals=0
-        ),
-    )
+def call(kernel, outs, scratch=(), smem=0, flops=TILE * F * F):
+    def run(*args):
+        spaces = [pltpu.SMEM if k < smem else pltpu.VMEM for k in range(len(args))]
+        return pl.pallas_call(
+            kernel,
+            out_shape=[jax.ShapeDtypeStruct(shape, dtype) for shape, dtype in outs],
+            in_specs=[pl.BlockSpec(memory_space=space) for space in spaces],
+            out_specs=[pl.BlockSpec(memory_space=pltpu.VMEM)] * len(outs),
+            scratch_shapes=[pltpu.VMEM(shape, dtype) for shape, dtype in scratch],
+            compiler_params=PARAMS,
+            cost_estimate=pl.CostEstimate(
+                flops=flops, bytes_accessed=2 * 1024 * 1024, transcendentals=0
+            ),
+        )(*args)
+
+    return run
 
 
 def exchange(array, axes):
     return lax.all_to_all(array, axes, 0, 0, tiled=True)
 
 
+def shift(array, axis, size, step):
+    return lax.ppermute(array, axis, [(k, (k + step) % size) for k in range(size)])
+
+
 def swap(array, axis):
-    return lax.ppermute(array, axis, [(0, 1), (1, 0)])
+    return shift(array, axis, 2, 1)
 
 
 def per_device(
@@ -196,7 +229,8 @@
     kept = lax.dynamic_index_in_dim(edges, h, 2, keepdims=False)
     came = swap(lax.dynamic_index_in_dim(edges, 1 - h, 2, keepdims=False), "h")
 
-    (spread,) = call(spread_kernel, [((XY, TILE, F), BF16)])(features, node_scale[None, :])
+    ones = lax.optimization_barrier(jnp.ones((XY, 1, 1), F32))
+    spread = (ones * s[None] * features.astype(F32)[None]).astype(BF16)
     sources = exchange(spread, ("x", "y"))
 
     pairs = jnp.stack([jnp.where(h == 0, kept, came), jnp.where(h == 0, came, kept)], axis=1)
@@ -230,16 +264,36 @@
         [((HALF, F), BF16)],
         flops=4 * E_ALL * F * HALF,
     )(around, sub)
-    terms, bias_grad = call(
-        backward_kernel,
-        [((XY, XCHUNK, F), BF16), ((1, F), F32)],
-        [((HALF, F), BF16), ((H, E_ALL, F), BF16)],
-        flops=4 * E_ALL * F * (HALF + TILE),
-    )(picked, around, other, sub, columns)
-    terms = exchange(terms, ("x", "y"))
+    at = jnp.stack([lax.axis_index("x"), lax.axis_index("y")]).astype(I32)
+    picked, w_own, bias_grad = call(
+        backward_pick_kernel,
+        [((H, E_ALL, F), BF16), ((WR, F), BF16), ((1, F), F32)],
+        [((HALF, F), BF16)],
+        flops=4 * E_ALL * F * HALF,
+    )(picked, around, other, sub)
+    x_rows, y_rows = Y * TILE + WR, TILE + X * WR
+    came = [None] * X
+    for step in (2, 1, 3):
+        (terms,) = call(
+            functools.partial(terms_kernel, step),
+            [((x_rows, F), BF16)],
+            smem=1,
+            flops=E_ALL * F * TILE,
+        )(at, picked, columns, w_own)
+        came[step] = shift(terms, "x", X, step)
+    (own,) = call(
+        own_terms_kernel, [((Y * TILE, F), F32)], smem=1, flops=E_ALL * F * TILE
+    )(at, picked, columns)
+    *sends, keep = call(
+        x_sum_kernel,
+        [((y_rows, F), BF16)] * 3 + [((y_rows, F), F32)],
+        [((Y * TILE, F), F32), ((X * WR, F), F32)],
+        smem=1,
+    )(at, own, w_own, *came[1:])
+    came = [shift(sends[step - 1], "y", Y, step) for step in (1, 2, 3)]
     feature_grad, weight_grad = call(
-        final_kernel, [((TILE, F), BF16), ((F, F), F32)]
-    )(terms, g, s, weight)
+        final_kernel, [((TILE, F), BF16), ((F, F), F32)], smem=1
+    )(at, keep, *came, g, s, weight)
     return output, feature_grad, weight_grad, bias_grad.reshape(F)
 
 

time: 121 us -> 127 us (1.050); the launches traced: 121 us -> 125 us
  blocking collectives: 51.1 us -> 30 us
  waiting for transfers between devices: 26.4 us -> 40.4 us
  starting transfers between devices: 29.9 us -> 36.6 us
  other arithmetic: 0.23 us -> 3.21 us
  Pallas kernels: 9.76 us -> 12.4 us
  local copies, waits for them, and re-layouts: 2.5 us -> 1.01 us
    all_to_all x3 -> x2, blocking collectives: 51.1 us -> 30 us  [exchange(): return lax.all_to_all(array, axes, 0, 0, tiled=True)]
    ppermute x3 -> x9, waiting for transfers between devices: 2.31 us -> 16.4 us  [shift(): lax.ppermute(array, axis, [(k, (k + step) % size) for k in range(size)])]
    ppermute x3 -> x9, starting transfers between devices: 14.1 us -> 20.8 us  [shift(): lax.ppermute(array, axis, [(k, (k + step) % size) for k in range(size)])]
    pallas_call x9 -> x13, Pallas kernels: 9.76 us -> 12.4 us  [run(): pl.pallas_call(kernel, out_shape=[jax.ShapeDtypeStruct(shape, dtype) for...]
    convert_element_type x0 -> x2, other arithmetic: none -> 2.17 us  [per_device(): spread = (ones * s[None] * features.astype(F32)[None]).astype(BF16)]
    unnamed x22 -> x18, local copies, waits for them, and re-layouts: 1.55 us -> 0.06 us
  transfers between devices with their start and end apart: 5 -> 11, of which waited for: 5 -> 11; matrix products, arithmetic and copies ran while one was open for 1% -> 1% of each run, Pallas kernels for 2% -> 2%
where the time goes in v4:
time: 127 us; the launch traced here: 125 us
  waiting for transfers between devices  40.4 us (32%)
  starting transfers between devices  36.6 us (29%)
  blocking collectives  30 us (24%)
  Pallas kernels  12.4 us (10%)
  other arithmetic  3.21 us (3%)
    all_to_all x2, blocking collectives, exchange(): return lax.all_to_all(array, axes, 0, 0, tiled=True)  30 us
    all_to_all x2, waiting for transfers between devices, exchange(): return lax.all_to_all(array, axes, 0, 0, tiled=True)  24 us
    ppermute x9, starting transfers between devices, shift(): lax.ppermute(array, axis, [(k, (k + step) % size) for k in range(size)])  20.8 us
    ppermute x9, waiting for transfers between devices, shift(): lax.ppermute(array, axis, [(k, (k + step) % size) for k in range(size)])  16.4 us
    all_to_all x2, starting transfers between devices, exchange(): return lax.all_to_all(array, axes, 0, 0, tiled=True)  15.8 us
    pallas_call x13, Pallas kernels, run(): pl.pallas_call(kernel, out_shape=[jax.ShapeDtypeStruct(shape, dtype) for...  12.4 us
  transfers between devices with their start and end apart: 11, of which 11 were waited for; matrix products, arithmetic and copies ran while one was open for 1% of the time, Pallas kernels for 2%

profile of v4, /device:TPU:1, one launch (start us, length us, event | category | flops | bytes accessed | tf_op | source)
XLA Modules:
  0.0 124.6 jit_solution(4518362283916404810)
XLA Ops:
  0.6 0.9 convert_element_type.6
  2.2 1.3 %multiply_convert_fusion = bf16[16,128,256]{2,1,0:T(8,128)(2,1)} fusion(f32[128,256]{1,0:T(8,128)S(1)} %convert_element_type.6, f32[16,128]{1,0:T(8,128)S(1)} %broadcast_multiply_fusion), kind=kLoop, calls=%fused_computation | loop fusion | flops 1048576 | bytes 1187840 | tf_op jit(solution)/shard_map/convert_element_type | solution.py:233
  3.6 7.6 %all-to-all-start = ((bf16[16,128,256]{2,1,0:T(8,128)(2,1)}), bf16[16,128,256]{2,1,0:T(8,128)(2,1)S(1)}, u32[]{:S(2)}, u32[]{:S(2)}) async-start(bf16[16,128,256]{2,1,0:T(8,128)(2,1)} %multiply_convert_fusion), calls=%async_computation | async-start | bytes 2097152 | tf_op jit(solution)/shard_map/all_to_all | solution.py:205
  11.9 7.0 %collective-permute-start = (s32[2,16,96]{2,1,0:T(8,128)S(1)}, s32[2,16,96]{2,1,0:T(8,128)S(1)}, u32[]{:S(2)}, u32[]{:S(2)}) collective-permute-start(s32[2,16,96]{2,1,0:T(8,128)S(1)} %bitcast.43), channel_id=1, source_target_pairs={{0,8},{8,0},{1,9},{9,1},{2,10},{10,2},{3,11},{11,3},{4,12},{12,4},... | collective-permute-start | bytes 36872 | tf_op jit(solution)/shard_map/ppermute | solution.py:209
  18.9 1.1 collective-permute-done
  20.5 6.2 %all-to-all-done.x_ref = bf16[16,128,256]{2,1,0:T(8,128)(2,1)S(1)} async-done(((bf16[16,128,256]{2,1,0:T(8,128)(2,1)}), bf16[16,128,256]{2,1,0:T(8,128)(2,1)S(1)}, u32[]{:S(2)}, u32[]{:S(2)}) %all-to-all-start) | async-done | bytes 1048608 | tf_op jit(solution)/shard_map/all_to_all | solution.py:205
  26.7 1.5 %shard_map.120 = (bf16[2,1536,256]{2,1,0:T(8,128)(2,1)S(1)}, bf16[2,512,256]{2,1,0:T(8,128)(2,1)S(1)}) custom-call(bf16[16,128,256]{2,1,0:T(8,128)(2,1)S(1)} %all-to-all-done.x_ref, s32[4,1536]{1,0:T(4,128)S(1)} %reshape.207.lane_ref, s32[1536,4]{1,0:T(8,128)S(1)} %bitcast.32), custom_call_target="tpu_custom_call" | custom-call | flops 1006632960 | bytes 2097152 | tf_op jit(solution)/shard_map/pallas_call | solution.py:189
  28.1 3.2 %collective-permute-start.1 = (bf16[2,512,256]{2,1,0:T(8,128)(2,1)S(1)}, bf16[2,512,256]{2,1,0:T(8,128)(2,1)S(1)}, u32[]{:S(2)}, u32[]{:S(2)}) collective-permute-start(bf16[2,512,256]{2,1,0:T(8,128)(2,1)S(1)} %get-tuple-element.19), channel_id=1, source_target_pairs={{0,1},{1,0},{2,3},{3,2},{4,5},{5,4},{6,7},{7,6},{8,9},{9,8},{10,11... | collective-permute-start | bytes 1572872 | tf_op jit(solution)/shard_map/ppermute | solution.py:209
  31.4 1.0 shard_map.121.mine_ref
  32.9 0.9 shard_map.122
  33.8 8.2 %all-to-all-start.1 = ((bf16[8,128,256]{2,1,0:T(8,128)(2,1)}), bf16[8,128,256]{2,1,0:T(8,128)(2,1)S(1)}, u32[]{:S(2)}, u32[]{:S(2)}) async-start(bf16[8,128,256]{2,1,0:T(8,128)(2,1)} %bitcast.10), calls=%async_computation.1 | async-start | bytes 1048576 | tf_op jit(solution)/shard_map/all_to_all | solution.py:205
  42.1 17.8 %all-to-all-done.1.part_ref = bf16[8,128,256]{2,1,0:T(8,128)(2,1)S(1)} async-done(((bf16[8,128,256]{2,1,0:T(8,128)(2,1)}), bf16[8,128,256]{2,1,0:T(8,128)(2,1)S(1)}, u32[]{:S(2)}, u32[]{:S(2)}) %all-to-all-start.1) | async-done | bytes 524320 | tf_op jit(solution)/shard_map/all_to_all | solution.py:205
  59.9 1.0 shard_map.123
  61.0 10.2 %all_to_all.20.w_ref = bf16[16,32,256]{2,1,0:T(8,128)(2,1)S(1)} all-to-all(bf16[16,32,256]{2,1,0:T(8,128)(2,1)S(1)} %get-tuple-element.21), channel_id=1, replica_groups=mesh['x'=4,'y'=4,'h'=2,'l'=4,'c'=2] {'x','y'}, dimensions={0} | all-to-all | bytes 524288 | tf_op jit(solution)/shard_map/all_to_all | solution.py:205
  71.3 19.8 %all_to_all.21.mine_ref = bf16[8,160,256]{2,1,0:T(8,128)(2,1)S(1)} all-to-all(bf16[8,160,256]{2,1,0:T(8,128)(2,1)S(1)} %shard_map.124), channel_id=1, replica_groups=mesh['x'=4,'y'=4,'h'=2,'l'=4,'c'=2] {'h','l'}, dimensions={0} | all-to-all | bytes 1310720 | tf_op jit(solution)/shard_map/all_to_all | solution.py:205
  91.1 3.9 %collective-permute-start.2 = (bf16[8,160,256]{2,1,0:T(8,128)(2,1)S(1)}, bf16[8,160,256]{2,1,0:T(8,128)(2,1)S(1)}, u32[]{:S(2)}, u32[]{:S(2)}) collective-permute-start(bf16[8,160,256]{2,1,0:T(8,128)(2,1)S(1)} %all_to_all.21.mine_ref), channel_id=1, source_target_pairs={{0,1},{1,0},{2,3},{3,2},{4,5},{5,4},{6,7},{7,6},{8,9},{9,8},{10,11... | collective-permute-start | bytes 1966088 | tf_op jit(solution)/shard_map/ppermute | solution.py:209
  95.0 1.0 shard_map.125.picked_ref
  96.7 1.6 %shard_map.126 = (bf16[2,1536,256]{2,1,0:T(8,128)(2,1)S(1)}, bf16[16,256]{1,0:T(8,128)(2,1)S(1)}, f32[1,256]{1,0:T(1,128)}) custom-call(bf16[2,1536,256]{2,1,0:T(8,128)(2,1)S(1)} %shard_map.125.picked_ref, bf16[8,160,256]{2,1,0:T(8,128)(2,1)S(1)} %all_to_all.21.mine_ref, bf16[8,160,256]{2,1,0:T(8,128)(2,1)S(1)} %collective-permute-done.2.other_ref, ...), custom_call_target="tpu_custom_call" | custom-call | flops 805306368 | bytes 2097152 | tf_op jit(solution)/shard_map/pallas_call | solution.py:189
  98.2 0.8 shard_map.130
  99.1 0.8 shard_map.129
  99.9 0.8 shard_map.128
  100.8 2.3 %collective-permute-start.4 = (bf16[528,256]{1,0:T(8,128)(2,1)S(1)}, bf16[528,256]{1,0:T(8,128)(2,1)S(1)}, u32[]{:S(2)}, u32[]{:S(2)}) collective-permute-start(bf16[528,256]{1,0:T(8,128)(2,1)S(1)} %shard_map.129), channel_id=1, source_target_pairs={{0,128},{64,192},{128,0},{192,64},{1,129},{65,193},{129,1},{193,65... | collective-permute-start | bytes 811016 | tf_op jit(solution)/shard_map/ppermute | solution.py:209
  103.1 0.9 collective-permute-start.5
  104.0 0.8 shard_map.127.own_ref
  104.8 5.3 %collective-permute-done.3.first = bf16[528,256]{1,0:T(8,128)(2,1)S(1)} collective-permute-done((bf16[528,256]{1,0:T(8,128)(2,1)S(1)}, bf16[528,256]{1,0:T(8,128)(2,1)S(1)}, u32[]{:S(2)}, u32[]{:S(2)}) %collective-permute-start.3) | collective-permute-done | bytes 270368 | tf_op jit(solution)/shard_map/ppermute | solution.py:209
  110.1 5.0 %collective-permute-done.4.second = bf16[528,256]{1,0:T(8,128)(2,1)S(1)} collective-permute-done((bf16[528,256]{1,0:T(8,128)(2,1)S(1)}, bf16[528,256]{1,0:T(8,128)(2,1)S(1)}, u32[]{:S(2)}, u32[]{:S(2)}) %collective-permute-start.4) | collective-permute-done | bytes 270368 | tf_op jit(solution)/shard_map/ppermute | solution.py:209
  115.8 0.8 shard_map.131
  117.0 1.6 %collective-permute-start.7 = (bf16[192,256]{1,0:T(8,128)(2,1)S(1)}, bf16[192,256]{1,0:T(8,128)(2,1)S(1)}, u32[]{:S(2)}, u32[]{:S(2)}) collective-permute-start(bf16[192,256]{1,0:T(8,128)(2,1)S(1)} %get-tuple-element.27), channel_id=1, source_target_pairs={{0,32},{16,48},{32,0},{48,16},{1,33},{17,49},{33,1},{49,17},{2,34}... | collective-permute-start | bytes 294920 | tf_op jit(solution)/shard_map/ppermute | solution.py:209
  118.6 1.5 %collective-permute-start.8 = (bf16[192,256]{1,0:T(8,128)(2,1)S(1)}, bf16[192,256]{1,0:T(8,128)(2,1)S(1)}, u32[]{:S(2)}, u32[]{:S(2)}) collective-permute-start(bf16[192,256]{1,0:T(8,128)(2,1)S(1)} %get-tuple-element.28), channel_id=1, source_target_pairs={{0,48},{16,0},{32,16},{48,32},{1,49},{17,1},{33,17},{49,33},{2,50}... | collective-permute-start | bytes 294920 | tf_op jit(solution)/shard_map/ppermute | solution.py:209
  120.1 2.2 %collective-permute-done.6.first = bf16[192,256]{1,0:T(8,128)(2,1)S(1)} collective-permute-done((bf16[192,256]{1,0:T(8,128)(2,1)S(1)}, bf16[192,256]{1,0:T(8,128)(2,1)S(1)}, u32[]{:S(2)}, u32[]{:S(2)}) %collective-permute-start.6) | collective-permute-done | bytes 98336 | tf_op jit(solution)/shard_map/ppermute | solution.py:209
  122.5 0.8 collective-permute-done.8.third
  123.2 1.4 %shard_map.132 = (bf16[128,256]{1,0:T(8,128)(2,1)}, f32[256,256]{1,0:T(8,128)}) custom-call(s32[2]{0:T(128)S(1)} %pad_add_fusion.1.at_ref, f32[192,256]{1,0:T(8,128)S(1)} %get-tuple-element.25.keep_ref, bf16[192,256]{1,0:T(8,128)(2,1)S(1)} %collective-permute-done.6.first, bf16[192,256]{1,0:T(8,128)(2,1)S(1)} %collective-permute-done.7.second, ...), custom_call_target="tpu_custom_call" | custom-call | flops 8388608 | bytes 2097152 | tf_op jit(solution)/shard_map/pallas_call | solution.py:189
  (47 shorter events, 4.6 us)
Async XLA Ops:
  2.2 8.9 %copy-start.8 = (s32[1,1,32,4]{2,3,1,0:T(4,128)S(1)}, s32[1,1,32,4]{2,3,1,0:T(4,128)}, u32[]{:S(2)}) copy-start(s32[1,1,32,4]{2,3,1,0:T(4,128)} %param.17) | copy-start | bytes 1540
  2.2 9.3 %copy-start.4 = (s32[1,1,32,96]{3,2,1,0:T(8,128)S(1)}, s32[1,1,32,96]{3,2,1,0:T(8,128)}, u32[]{:S(2)}) copy-start(s32[1,1,32,96]{3,2,1,0:T(8,128)} %param.14) | copy-start | bytes 36868
  2.2 9.5 %copy-start.5 = (s32[1,1,32,96]{3,2,1,0:T(8,128)S(1)}, s32[1,1,32,96]{3,2,1,0:T(8,128)}, u32[]{:S(2)}) copy-start(s32[1,1,32,96]{3,2,1,0:T(8,128)} %param.15) | copy-start | bytes 36868
  2.2 9.6 %copy-start.6 = (s32[1,1,32,96]{3,2,1,0:T(8,128)S(1)}, s32[1,1,32,96]{3,2,1,0:T(8,128)}, u32[]{:S(2)}) copy-start(s32[1,1,32,96]{3,2,1,0:T(8,128)} %param.16) | copy-start | bytes 36868
  3.6 23.1 %all-to-all-start = ((bf16[16,128,256]{2,1,0:T(8,128)(2,1)}), bf16[16,128,256]{2,1,0:T(8,128)(2,1)S(1)}, u32[]{:S(2)}, u32[]{:S(2)}) async-start(bf16[16,128,256]{2,1,0:T(8,128)(2,1)} %multiply_convert_fusion), calls=%async_computation | async-start | bytes 2097152 | tf_op jit(solution)/shard_map/all_to_all | solution.py:205
  11.9 8.1 %collective-permute-start = (s32[2,16,96]{2,1,0:T(8,128)S(1)}, s32[2,16,96]{2,1,0:T(8,128)S(1)}, u32[]{:S(2)}, u32[]{:S(2)}) collective-permute-start(s32[2,16,96]{2,1,0:T(8,128)S(1)} %bitcast.43), channel_id=1, source_target_pairs={{0,8},{8,0},{1,9},{9,1},{2,10},{10,2},{3,11},{11,3},{4,12},{12,4},... | collective-permute-start | bytes 36872 | tf_op jit(solution)/shard_map/ppermute | solution.py:209
  28.1 4.8 %collective-permute-start.1 = (bf16[2,512,256]{2,1,0:T(8,128)(2,1)S(1)}, bf16[2,512,256]{2,1,0:T(8,128)(2,1)S(1)}, u32[]{:S(2)}, u32[]{:S(2)}) collective-permute-start(bf16[2,512,256]{2,1,0:T(8,128)(2,1)S(1)} %get-tuple-element.19), channel_id=1, source_target_pairs={{0,1},{1,0},{2,3},{3,2},{4,5},{5,4},{6,7},{7,6},{8,9},{9,8},{10,11... | collective-permute-start | bytes 1572872 | tf_op jit(solution)/shard_map/ppermute | solution.py:209
  32.3 9.6 %copy-start.7 = (f32[128]{0:T(128)S(1)}, f32[128]{0:T(128)}, u32[]{:S(2)}) copy-start(f32[128]{0:T(128)} %param.12) | copy-start | bytes 1540
  32.3 27.6 %copy-start = (bf16[256,256]{1,0:T(8,128)(2,1)S(1)}, bf16[256,256]{1,0:T(8,128)(2,1)}, u32[]{:S(2)}) copy-start(bf16[256,256]{1,0:T(8,128)(2,1)} %weight_ref.1) | copy-start | bytes 393220
  32.4 27.6 %copy-start.1 = (bf16[128,256]{1,0:T(8,128)(2,1)S(1)}, bf16[128,256]{1,0:T(8,128)(2,1)}, u32[]{:S(2)}) copy-start(bf16[128,256]{1,0:T(8,128)(2,1)} %x_ref.1) | copy-start | bytes 196612
  32.4 27.6 %copy-start.2 = (bf16[128,256]{1,0:T(8,128)(2,1)S(1)}, bf16[128,256]{1,0:T(8,128)(2,1)}, u32[]{:S(2)}) copy-start(bf16[128,256]{1,0:T(8,128)(2,1)} %ct_ref.1) | copy-start | bytes 196612
  32.4 27.6 %copy-start.3 = (f32[256]{0:T(256)S(1)}, f32[256]{0:T(256)}, u32[]{:S(2)}) copy-start(f32[256]{0:T(256)} %param.11) | copy-start | bytes 3076
  33.8 26.1 %all-to-all-start.1 = ((bf16[8,128,256]{2,1,0:T(8,128)(2,1)}), bf16[8,128,256]{2,1,0:T(8,128)(2,1)S(1)}, u32[]{:S(2)}, u32[]{:S(2)}) async-start(bf16[8,128,256]{2,1,0:T(8,128)(2,1)} %bitcast.10), calls=%async_computation.1 | async-start | bytes 1048576 | tf_op jit(solution)/shard_map/all_to_all | solution.py:205
  91.1 5.6 %collective-permute-start.2 = (bf16[8,160,256]{2,1,0:T(8,128)(2,1)S(1)}, bf16[8,160,256]{2,1,0:T(8,128)(2,1)S(1)}, u32[]{:S(2)}, u32[]{:S(2)}) collective-permute-start(bf16[8,160,256]{2,1,0:T(8,128)(2,1)S(1)} %all_to_all.21.mine_ref), channel_id=1, source_target_pairs={{0,1},{1,0},{2,3},{3,2},{4,5},{5,4},{6,7},{7,6},{8,9},{9,8},{10,11... | collective-permute-start | bytes 1966088 | tf_op jit(solution)/shard_map/ppermute | solution.py:209
  100.7 9.4 %collective-permute-start.3 = (bf16[528,256]{1,0:T(8,128)(2,1)S(1)}, bf16[528,256]{1,0:T(8,128)(2,1)S(1)}, u32[]{:S(2)}, u32[]{:S(2)}) collective-permute-start(bf16[528,256]{1,0:T(8,128)(2,1)S(1)} %shard_map.128), channel_id=1, source_target_pairs={{0,64},{64,128},{128,192},{192,0},{1,65},{65,129},{129,193},{193,1... | collective-permute-start | bytes 811016 | tf_op jit(solution)/shard_map/ppermute | solution.py:209
  100.8 14.3 %collective-permute-start.4 = (bf16[528,256]{1,0:T(8,128)(2,1)S(1)}, bf16[528,256]{1,0:T(8,128)(2,1)S(1)}, u32[]{:S(2)}, u32[]{:S(2)}) collective-permute-start(bf16[528,256]{1,0:T(8,128)(2,1)S(1)} %shard_map.129), channel_id=1, source_target_pairs={{0,128},{64,192},{128,0},{192,64},{1,129},{65,193},{129,1},{193,65... | collective-permute-start | bytes 811016 | tf_op jit(solution)/shard_map/ppermute | solution.py:209
  103.1 12.7 %collective-permute-start.5 = (bf16[528,256]{1,0:T(8,128)(2,1)S(1)}, bf16[528,256]{1,0:T(8,128)(2,1)S(1)}, u32[]{:S(2)}, u32[]{:S(2)}) collective-permute-start(bf16[528,256]{1,0:T(8,128)(2,1)S(1)} %shard_map.130), channel_id=1, source_target_pairs={{0,192},{64,0},{128,64},{192,128},{1,193},{65,1},{129,65},{193,129... | collective-permute-start | bytes 811016 | tf_op jit(solution)/shard_map/ppermute | solution.py:209
  116.6 5.7 %collective-permute-start.6 = (bf16[192,256]{1,0:T(8,128)(2,1)S(1)}, bf16[192,256]{1,0:T(8,128)(2,1)S(1)}, u32[]{:S(2)}, u32[]{:S(2)}) collective-permute-start(bf16[192,256]{1,0:T(8,128)(2,1)S(1)} %get-tuple-element.26), channel_id=1, source_target_pairs={{0,16},{16,32},{32,48},{48,0},{1,17},{17,33},{33,49},{49,1},{2,18}... | collective-permute-start | bytes 294920 | tf_op jit(solution)/shard_map/ppermute | solution.py:209
  117.0 5.5 %collective-permute-start.7 = (bf16[192,256]{1,0:T(8,128)(2,1)S(1)}, bf16[192,256]{1,0:T(8,128)(2,1)S(1)}, u32[]{:S(2)}, u32[]{:S(2)}) collective-permute-start(bf16[192,256]{1,0:T(8,128)(2,1)S(1)} %get-tuple-element.27), channel_id=1, source_target_pairs={{0,32},{16,48},{32,0},{48,16},{1,33},{17,49},{33,1},{49,17},{2,34}... | collective-permute-start | bytes 294920 | tf_op jit(solution)/shard_map/ppermute | solution.py:209
  118.6 4.6 %collective-permute-start.8 = (bf16[192,256]{1,0:T(8,128)(2,1)S(1)}, bf16[192,256]{1,0:T(8,128)(2,1)S(1)}, u32[]{:S(2)}, u32[]{:S(2)}) collective-permute-start(bf16[192,256]{1,0:T(8,128)(2,1)S(1)} %get-tuple-element.28), channel_id=1, source_target_pairs={{0,48},{16,0},{32,16},{48,32},{1,49},{17,1},{33,17},{49,33},{2,50}... | collective-permute-start | bytes 294920 | tf_op jit(solution)/shard_map/ppermute | solution.py:209

commit v5 on v3

--- a/solution.py
+++ b/solution.py
@@ -13,7 +13,7 @@
 HALF = L * TILE
 ROWS = C * HALF
 E_ALL = XY * EDGES
-STEP = 256
+STEP = 4 * EDGES
 WR, BB = F // XY, 16
 ZCHUNK = TILE + WR + BB
 XCHUNK = TILE + WR
@@ -37,13 +37,42 @@
     return jnp.where(at == 0, high, jnp.where(at == 1, row - high, 0.0)).astype(BF16)
 
 
-def spread_kernel(x_ref, s_ref, out_ref):
-    scale = jnp.transpose(jnp.broadcast_to(s_ref[...], (TILE, TILE)))
+def spread_kernel(x_ref, s_ref, out_ref, x, s, scaled, sems):
+    loads = [
+        pltpu.make_async_copy(x_ref, x, sems.at[0]),
+        pltpu.make_async_copy(s_ref, s, sems.at[1]),
+    ]
+    for load in loads:
+        load.start()
+    for load in loads:
+        load.wait()
+    scale = jnp.transpose(jnp.broadcast_to(s[...], (TILE, TILE)))
     for k in range(F // TILE):
         part = pl.ds(k * TILE, TILE)
-        scaled = (scale * x_ref[:, part].astype(F32)).astype(BF16)
-        for j in range(XY):
-            out_ref[j, :, part] = scaled
+        scaled[:, part] = (scale * x[:, part].astype(F32)).astype(BF16)
+    stores = [
+        pltpu.make_async_copy(scaled, out_ref.at[j], sems.at[2 + j]) for j in range(XY)
+    ]
+    for store in stores:
+        store.start()
+    for store in stores:
+        store.wait()
+
+
+def spread(features, node_scale):
+    return pl.pallas_call(
+        spread_kernel,
+        out_shape=jax.ShapeDtypeStruct((XY, TILE, F), BF16),
+        in_specs=[pl.BlockSpec(memory_space=pltpu.HBM)] * 2,
+        out_specs=pl.BlockSpec(memory_space=pltpu.HBM),
+        scratch_shapes=[
+            pltpu.VMEM((TILE, F), BF16),
+            pltpu.VMEM((1, TILE), F32),
+            pltpu.VMEM((TILE, F), BF16),
+            pltpu.SemaphoreType.DMA((2 + XY,)),
+        ],
+        compiler_params=pltpu.CompilerParams(vmem_limit_bytes=63_480_000),
+    )(features, node_scale[None, :])
 
 
 def forward_send_kernel(x_ref, lane_ref, sub_ref, gathered_ref, send_ref):
@@ -53,16 +82,14 @@
             pick = one_hot(sub_ref[rows, H + b : H + b + 1], (EDGES, TILE), 1)
             gathered_ref[b, rows, :] = dot(pick, x_ref[j]).astype(BF16)
     for b in range(H):
-        for m in range(HALF // STEP):
-            place = one_hot(lane_ref[b : b + 1, :], (STEP, E_ALL), 0, HALF + m * STEP)
-            send_ref[b, pl.ds(m * STEP, STEP), :] = dot(place, gathered_ref[b]).astype(BF16)
+        place = one_hot(lane_ref[b : b + 1, :], (HALF, E_ALL), 0, HALF)
+        send_ref[b] = dot(place, gathered_ref[b]).astype(BF16)
 
 
 def forward_keep_kernel(gathered_ref, lane_ref, mine_ref):
     for b in range(H):
-        for m in range(HALF // STEP):
-            place = one_hot(lane_ref[b : b + 1, :], (STEP, E_ALL), 0, m * STEP)
-            mine_ref[b, pl.ds(m * STEP, STEP), :] = dot(place, gathered_ref[b])
+        place = one_hot(lane_ref[b : b + 1, :], (HALF, E_ALL), 0)
+        mine_ref[b] = dot(place, gathered_ref[b])
 
 
 def add_kernel(mine_ref, other_ref, out_ref):
@@ -112,9 +139,12 @@
         for k in range(L):
             grads[pl.ds(k * TILE, TILE), :] = mine_ref[b * L + k, pl.ds(0, TILE), :]
         for m in range(E_ALL // STEP):
-            rows = pl.ds(m * STEP, STEP)
-            pick = one_hot(sub_ref[rows, b : b + 1], (STEP, HALF), 1)
-            picked_ref[b, rows, :] = dot(pick, grads[...]).astype(BF16)
+            pick = one_hot(sub_ref[pl.ds(m * STEP, STEP), b : b + 1], (STEP, HALF), 1)
+            value = dot(pick, grads[...]).astype(BF16)
+            for q in range(STEP // EDGES):
+                picked_ref[m * (STEP // EDGES) + q, pl.ds(b * EDGES, EDGES), :] = value[
+                    q * EDGES : (q + 1) * EDGES
+                ]
 
 
 def backward_kernel(
@@ -134,16 +164,15 @@
         for k in range(L):
             grads[pl.ds(k * TILE, TILE), :] = other_ref[b * L + k, pl.ds(0, TILE), :]
         for m in range(E_ALL // STEP):
-            rows = pl.ds(m * STEP, STEP)
-            pick = one_hot(sub_ref[rows, b : b + 1], (STEP, HALF), 1, HALF)
-            value = dot(pick, grads[...]) + picked_ref[b, rows, :].astype(F32)
-            picked[b, rows, :] = value.astype(BF16)
+            pick = one_hot(sub_ref[pl.ds(m * STEP, STEP), b : b + 1], (STEP, HALF), 1, HALF)
+            value = dot(pick, grads[...])
+            for q in range(STEP // EDGES):
+                j, rows = m * (STEP // EDGES) + q, pl.ds(b * EDGES, EDGES)
+                both = value[q * EDGES : (q + 1) * EDGES] + picked_ref[j, rows, :].astype(F32)
+                picked[j, rows, :] = both.astype(BF16)
     for j in range(XY):
-        total = jnp.zeros((TILE, F), F32)
-        for b in range(H):
-            at = b * XY + j
-            place = one_hot(col_ref[at : at + 1, :], (TILE, EDGES), 0)
-            total += dot(place, picked[b, pl.ds(j * EDGES, EDGES), :])
+        place = one_hot(col_ref[j : j + 1, :], (TILE, H * EDGES), 0)
+        total = dot(place, picked[j])
         pay_ref[j, pl.ds(0, TILE), :] = total.astype(BF16)
         pay_ref[j, pl.ds(TILE, WR), :] = own
 
@@ -196,13 +225,12 @@
     kept = lax.dynamic_index_in_dim(edges, h, 2, keepdims=False)
     came = swap(lax.dynamic_index_in_dim(edges, 1 - h, 2, keepdims=False), "h")
 
-    (spread,) = call(spread_kernel, [((XY, TILE, F), BF16)])(features, node_scale[None, :])
-    sources = exchange(spread, ("x", "y"))
+    sources = exchange(spread(features, node_scale), ("x", "y"))
 
     pairs = jnp.stack([jnp.where(h == 0, kept, came), jnp.where(h == 0, came, kept)], axis=1)
     lane = pairs.reshape(2 * H, E_ALL)
     sub = lane.T
-    columns = pairs[1].reshape(H * XY, EDGES)
+    columns = jnp.concatenate([pairs[1, 0], pairs[1, 1]], axis=1)
 
     gathered, send = call(
         forward_send_kernel,
@@ -226,14 +254,14 @@
     other = swap(around, "c")
     (picked,) = call(
         backward_mine_kernel,
-        [((H, E_ALL, F), BF16)],
+        [((XY, H * EDGES, F), BF16)],
         [((HALF, F), BF16)],
         flops=4 * E_ALL * F * HALF,
     )(around, sub)
     terms, bias_grad = call(
         backward_kernel,
         [((XY, XCHUNK, F), BF16), ((1, F), F32)],
-        [((HALF, F), BF16), ((H, E_ALL, F), BF16)],
+        [((HALF, F), BF16), ((XY, H * EDGES, F), BF16)],
         flops=4 * E_ALL * F * (HALF + TILE),
     )(picked, around, other, sub, columns)
     terms = exchange(terms, ("x", "y"))

time: 121 us -> 120 us (level)
  local copies, waits for them, and re-layouts: 2.5 us -> 1.01 us
    unnamed x22 -> x18, local copies, waits for them, and re-layouts: 1.55 us -> 0.06 us
where the time goes in v5:
time: 120 us
  blocking collectives  51.1 us (43%)
  starting transfers between devices  29.9 us (25%)
  waiting for transfers between devices  26.3 us (22%)
  Pallas kernels  10.4 us (9%)
    all_to_all x3, blocking collectives, exchange(): return lax.all_to_all(array, axes, 0, 0, tiled=True)  51.1 us
    all_to_all x2, waiting for transfers between devices, exchange(): return lax.all_to_all(array, axes, 0, 0, tiled=True)  24 us
    all_to_all x2, starting transfers between devices, exchange(): return lax.all_to_all(array, axes, 0, 0, tiled=True)  15.8 us
    ppermute x3, starting transfers between devices, swap(): return lax.ppermute(array, axis, [(0, 1), (1, 0)])  14.1 us
  transfers between devices with their start and end apart: 5, of which 5 were waited for; matrix products, arithmetic and copies ran while one was open for 1% of the time, Pallas kernels for 2%

profile of v5, /device:TPU:1, one launch (start us, length us, event | category | flops | bytes accessed | tf_op | source)
XLA Modules:
  0.0 119.8 jit_solution(14479066077796311936)
XLA Ops:
  0.7 2.1 %shard_map.120 = bf16[16,128,256]{2,1,0:T(8,128)(2,1)} custom-call(bf16[128,256]{1,0:T(8,128)(2,1)} %x_ref.3, f32[1,128]{1,0:T(1,128)} %bitcast.39), custom_call_target="tpu_custom_call" | custom-call | tf_op jit(solution)/shard_map/pallas_call | solution.py:63
  2.8 7.6 %all-to-all-start = ((bf16[16,128,256]{2,1,0:T(8,128)(2,1)}), bf16[16,128,256]{2,1,0:T(8,128)(2,1)S(1)}, u32[]{:S(2)}, u32[]{:S(2)}) async-start(bf16[16,128,256]{2,1,0:T(8,128)(2,1)} %shard_map.120), calls=%async_computation | async-start | bytes 2097152 | tf_op jit(solution)/shard_map/all_to_all | solution.py:205
  10.4 0.1 broadcast_in_dim.50
  10.5 0.1 broadcast_in_dim.56
  10.6 0.1 broadcast_in_dim.54
  10.7 0.1 broadcast_in_dim.52
  10.9 0.1 add_select_fusion
  11.1 0.1 fusion.1
  11.1 7.0 %collective-permute-start = (s32[2,16,96]{2,1,0:T(8,128)S(1)}, s32[2,16,96]{2,1,0:T(8,128)S(1)}, u32[]{:S(2)}, u32[]{:S(2)}) collective-permute-start(s32[2,16,96]{2,1,0:T(8,128)S(1)} %bitcast.38), channel_id=1, source_target_pairs={{0,8},{8,0},{1,9},{9,1},{2,10},{10,2},{3,11},{11,3},{4,12},{12,4},... | collective-permute-start | bytes 36872 | tf_op jit(solution)/shard_map/ppermute | solution.py:209
  18.1 1.1 collective-permute-done
  19.3 0.1 reshape.176.lane_ref
  19.4 0.3 copy.29
  19.7 6.2 %all-to-all-done.x_ref = bf16[16,128,256]{2,1,0:T(8,128)(2,1)S(1)} async-done(((bf16[16,128,256]{2,1,0:T(8,128)(2,1)}), bf16[16,128,256]{2,1,0:T(8,128)(2,1)S(1)}, u32[]{:S(2)}, u32[]{:S(2)}) %all-to-all-start) | async-done | bytes 1048608 | tf_op jit(solution)/shard_map/all_to_all | solution.py:205
  25.9 1.5 %shard_map.121 = (bf16[2,1536,256]{2,1,0:T(8,128)(2,1)S(1)}, bf16[2,512,256]{2,1,0:T(8,128)(2,1)S(1)}) custom-call(bf16[16,128,256]{2,1,0:T(8,128)(2,1)S(1)} %all-to-all-done.x_ref, s32[4,1536]{1,0:T(4,128)S(1)} %reshape.176.lane_ref, s32[1536,4]{1,0:T(8,128)S(1)} %bitcast.29), custom_call_target="tpu_custom_call" | custom-call | flops 1006632960 | bytes 2097152 | tf_op jit(solution)/shard_map/pallas_call | solution.py:235
  27.3 3.2 %collective-permute-start.1 = (bf16[2,512,256]{2,1,0:T(8,128)(2,1)S(1)}, bf16[2,512,256]{2,1,0:T(8,128)(2,1)S(1)}, u32[]{:S(2)}, u32[]{:S(2)}) collective-permute-start(bf16[2,512,256]{2,1,0:T(8,128)(2,1)S(1)} %get-tuple-element.14), channel_id=1, source_target_pairs={{0,1},{1,0},{2,3},{3,2},{4,5},{5,4},{6,7},{7,6},{8,9},{9,8},{10,11... | collective-permute-start | bytes 1572872 | tf_op jit(solution)/shard_map/ppermute | solution.py:209
  30.6 1.0 shard_map.122.mine_ref
  31.6 0.5 collective-permute-done.1.other_ref
  32.1 0.9 shard_map.123
  33.0 8.2 %all-to-all-start.1 = ((bf16[8,128,256]{2,1,0:T(8,128)(2,1)}), bf16[8,128,256]{2,1,0:T(8,128)(2,1)S(1)}, u32[]{:S(2)}, u32[]{:S(2)}) async-start(bf16[8,128,256]{2,1,0:T(8,128)(2,1)} %bitcast.9), calls=%async_computation.1 | async-start | bytes 1048576 | tf_op jit(solution)/shard_map/all_to_all | solution.py:205
  41.2 0.1 copy.30.s_ref
  41.4 17.8 %all-to-all-done.1.part_ref = bf16[8,128,256]{2,1,0:T(8,128)(2,1)S(1)} async-done(((bf16[8,128,256]{2,1,0:T(8,128)(2,1)}), bf16[8,128,256]{2,1,0:T(8,128)(2,1)S(1)}, u32[]{:S(2)}, u32[]{:S(2)}) %all-to-all-start.1) | async-done | bytes 524320 | tf_op jit(solution)/shard_map/all_to_all | solution.py:205
  59.2 1.0 shard_map.124
  60.2 10.2 %all_to_all.25.w_ref = bf16[16,32,256]{2,1,0:T(8,128)(2,1)S(1)} all-to-all(bf16[16,32,256]{2,1,0:T(8,128)(2,1)S(1)} %get-tuple-element.16), channel_id=1, replica_groups=mesh['x'=4,'y'=4,'h'=2,'l'=4,'c'=2] {'x','y'}, dimensions={0} | all-to-all | bytes 524288 | tf_op jit(solution)/shard_map/all_to_all | solution.py:205
  70.5 0.1 shard_map.125
  70.6 19.8 %all_to_all.26.mine_ref = bf16[8,160,256]{2,1,0:T(8,128)(2,1)S(1)} all-to-all(bf16[8,160,256]{2,1,0:T(8,128)(2,1)S(1)} %shard_map.125), channel_id=1, replica_groups=mesh['x'=4,'y'=4,'h'=2,'l'=4,'c'=2] {'h','l'}, dimensions={0} | all-to-all | bytes 1310720 | tf_op jit(solution)/shard_map/all_to_all | solution.py:205
  90.3 3.9 %collective-permute-start.2 = (bf16[8,160,256]{2,1,0:T(8,128)(2,1)S(1)}, bf16[8,160,256]{2,1,0:T(8,128)(2,1)S(1)}, u32[]{:S(2)}, u32[]{:S(2)}) collective-permute-start(bf16[8,160,256]{2,1,0:T(8,128)(2,1)S(1)} %all_to_all.26.mine_ref), channel_id=1, source_target_pairs={{0,1},{1,0},{2,3},{3,2},{4,5},{5,4},{6,7},{7,6},{8,9},{9,8},{10,11... | collective-permute-start | bytes 1966088 | tf_op jit(solution)/shard_map/ppermute | solution.py:209
  94.2 0.1 pad_add_fusion.1.col_ref
  94.3 1.0 shard_map.126.picked_ref
  95.3 0.6 collective-permute-done.2.other_ref
  95.9 1.9 %shard_map.127 = (bf16[16,144,256]{2,1,0:T(8,128)(2,1)S(1)}, f32[1,256]{1,0:T(1,128)}) custom-call(bf16[16,192,256]{2,1,0:T(8,128)(2,1)S(1)} %shard_map.126.picked_ref, bf16[8,160,256]{2,1,0:T(8,128)(2,1)S(1)} %all_to_all.26.mine_ref, bf16[8,160,256]{2,1,0:T(8,128)(2,1)S(1)} %collective-permute-done.2.other_ref, s32[1536,4]{1,0:T(8,128)S(1)} %bitcast.31, ...), custom_call_target="tpu_custom_call" | custom-call | flops 1006632960 | bytes 2097152 | tf_op jit(solution)/shard_map/pallas_call | solution.py:261
  97.9 21.0 %all_to_all.27.part_ref = bf16[16,144,256]{2,1,0:T(8,128)(2,1)S(1)} all-to-all(bf16[16,144,256]{2,1,0:T(8,128)(2,1)S(1)} %get-tuple-element.18), channel_id=1, replica_groups=mesh['x'=4,'y'=4,'h'=2,'l'=4,'c'=2] {'x','y'}, dimensions={0} | all-to-all | bytes 2359296 | tf_op jit(solution)/shard_map/all_to_all | solution.py:205
  118.9 0.9 shard_map.128
  (29 shorter events, 0.2 us)
Async XLA Ops:
  0.6 9.8 %copy-start.8 = (s32[1,1,32,4]{2,3,1,0:T(4,128)S(1)}, s32[1,1,32,4]{2,3,1,0:T(4,128)}, u32[]{:S(2)}) copy-start(s32[1,1,32,4]{2,3,1,0:T(4,128)} %param.17) | copy-start | bytes 1540
  0.6 10.1 %copy-start.4 = (s32[1,1,32,96]{3,2,1,0:T(8,128)S(1)}, s32[1,1,32,96]{3,2,1,0:T(8,128)}, u32[]{:S(2)}) copy-start(s32[1,1,32,96]{3,2,1,0:T(8,128)} %param.14) | copy-start | bytes 36868
  0.7 10.3 %copy-start.5 = (s32[1,1,32,96]{3,2,1,0:T(8,128)S(1)}, s32[1,1,32,96]{3,2,1,0:T(8,128)}, u32[]{:S(2)}) copy-start(s32[1,1,32,96]{3,2,1,0:T(8,128)} %param.15) | copy-start | bytes 36868
  0.7 10.4 %copy-start.6 = (s32[1,1,32,96]{3,2,1,0:T(8,128)S(1)}, s32[1,1,32,96]{3,2,1,0:T(8,128)}, u32[]{:S(2)}) copy-start(s32[1,1,32,96]{3,2,1,0:T(8,128)} %param.16) | copy-start | bytes 36868
  2.8 23.1 %all-to-all-start = ((bf16[16,128,256]{2,1,0:T(8,128)(2,1)}), bf16[16,128,256]{2,1,0:T(8,128)(2,1)S(1)}, u32[]{:S(2)}, u32[]{:S(2)}) async-start(bf16[16,128,256]{2,1,0:T(8,128)(2,1)} %shard_map.120), calls=%async_computation | async-start | bytes 2097152 | tf_op jit(solution)/shard_map/all_to_all | solution.py:205
  11.1 8.1 %collective-permute-start = (s32[2,16,96]{2,1,0:T(8,128)S(1)}, s32[2,16,96]{2,1,0:T(8,128)S(1)}, u32[]{:S(2)}, u32[]{:S(2)}) collective-permute-start(s32[2,16,96]{2,1,0:T(8,128)S(1)} %bitcast.38), channel_id=1, source_target_pairs={{0,8},{8,0},{1,9},{9,1},{2,10},{10,2},{3,11},{11,3},{4,12},{12,4},... | collective-permute-start | bytes 36872 | tf_op jit(solution)/shard_map/ppermute | solution.py:209
  27.3 4.8 %collective-permute-start.1 = (bf16[2,512,256]{2,1,0:T(8,128)(2,1)S(1)}, bf16[2,512,256]{2,1,0:T(8,128)(2,1)S(1)}, u32[]{:S(2)}, u32[]{:S(2)}) collective-permute-start(bf16[2,512,256]{2,1,0:T(8,128)(2,1)S(1)} %get-tuple-element.14), channel_id=1, source_target_pairs={{0,1},{1,0},{2,3},{3,2},{4,5},{5,4},{6,7},{7,6},{8,9},{9,8},{10,11... | collective-permute-start | bytes 1572872 | tf_op jit(solution)/shard_map/ppermute | solution.py:209
  31.6 9.7 %copy-start.7 = (f32[128]{0:T(128)S(1)}, f32[128]{0:T(128)}, u32[]{:S(2)}) copy-start(f32[128]{0:T(128)} %param.12) | copy-start | bytes 1540
  31.6 27.6 %copy-start = (bf16[256,256]{1,0:T(8,128)(2,1)S(1)}, bf16[256,256]{1,0:T(8,128)(2,1)}, u32[]{:S(2)}) copy-start(bf16[256,256]{1,0:T(8,128)(2,1)} %w_ref.3) | copy-start | bytes 393220
  31.6 27.6 %copy-start.1 = (bf16[128,256]{1,0:T(8,128)(2,1)S(1)}, bf16[128,256]{1,0:T(8,128)(2,1)}, u32[]{:S(2)}) copy-start(bf16[128,256]{1,0:T(8,128)(2,1)} %x_ref.3) | copy-start | bytes 196612
  31.6 27.6 %copy-start.2 = (bf16[128,256]{1,0:T(8,128)(2,1)S(1)}, bf16[128,256]{1,0:T(8,128)(2,1)}, u32[]{:S(2)}) copy-start(bf16[128,256]{1,0:T(8,128)(2,1)} %ct_ref.1) | copy-start | bytes 196612
  31.6 27.6 %copy-start.3 = (f32[256]{0:T(256)S(1)}, f32[256]{0:T(256)}, u32[]{:S(2)}) copy-start(f32[256]{0:T(256)} %param.11) | copy-start | bytes 3076
  33.0 26.1 %all-to-all-start.1 = ((bf16[8,128,256]{2,1,0:T(8,128)(2,1)}), bf16[8,128,256]{2,1,0:T(8,128)(2,1)S(1)}, u32[]{:S(2)}, u32[]{:S(2)}) async-start(bf16[8,128,256]{2,1,0:T(8,128)(2,1)} %bitcast.9), calls=%async_computation.1 | async-start | bytes 1048576 | tf_op jit(solution)/shard_map/all_to_all | solution.py:205
  90.3 5.6 %collective-permute-start.2 = (bf16[8,160,256]{2,1,0:T(8,128)(2,1)S(1)}, bf16[8,160,256]{2,1,0:T(8,128)(2,1)S(1)}, u32[]{:S(2)}, u32[]{:S(2)}) collective-permute-start(bf16[8,160,256]{2,1,0:T(8,128)(2,1)S(1)} %all_to_all.26.mine_ref), channel_id=1, source_target_pairs={{0,1},{1,0},{2,3},{3,2},{4,5},{5,4},{6,7},{7,6},{8,9},{9,8},{10,11... | collective-permute-start | bytes 1966088 | tf_op jit(solution)/shard_map/ppermute | solution.py:209

commit v6 on v5

--- a/solution.py
+++ b/solution.py
@@ -37,6 +37,10 @@
     return jnp.where(at == 0, high, jnp.where(at == 1, row - high, 0.0)).astype(BF16)
 
 
+def column(row):
+    return jnp.transpose(jnp.broadcast_to(row, (TILE, TILE)))[:, :1]
+
+
 def spread_kernel(x_ref, s_ref, out_ref, x, s, scaled, sems):
     loads = [
         pltpu.make_async_copy(x_ref, x, sems.at[0]),
@@ -46,10 +50,7 @@
         load.start()
     for load in loads:
         load.wait()
-    scale = jnp.transpose(jnp.broadcast_to(s[...], (TILE, TILE)))
-    for k in range(F // TILE):
-        part = pl.ds(k * TILE, TILE)
-        scaled[:, part] = (scale * x[:, part].astype(F32)).astype(BF16)
+    scaled[...] = (column(s[...]) * x[...].astype(F32)).astype(BF16)
     stores = [
         pltpu.make_async_copy(scaled, out_ref.at[j], sems.at[2 + j]) for j in range(XY)
     ]
@@ -72,7 +73,7 @@
             pltpu.SemaphoreType.DMA((2 + XY,)),
         ],
         compiler_params=pltpu.CompilerParams(vmem_limit_bytes=63_480_000),
-    )(features, node_scale[None, :])
+    )(features, node_scale)
 
 
 def forward_send_kernel(x_ref, lane_ref, sub_ref, gathered_ref, send_ref):
@@ -97,7 +98,7 @@
 
 
 def middle_kernel(part_ref, x_ref, s_ref, w_ref, bias_ref, ct_ref, out_ref, g_ref, wp_ref):
-    s = s_ref[...]
+    s = column(s_ref[...])
     z = s * x_ref[...].astype(F32)
     for k in range(ZN):
         z += part_ref[k].astype(F32)
@@ -182,7 +183,7 @@
     for k in range(XY):
         back += part_ref[k, pl.ds(0, TILE), :].astype(F32)
         wg_ref[pl.ds(k * WR, WR), :] = part_ref[k, pl.ds(TILE, WR), :].astype(F32)
-    grad_xw = (s_ref[...] * back).astype(BF16)
+    grad_xw = (column(s_ref[...]) * back).astype(BF16)
     fg_ref[...] = lax.dot_general(
         grad_xw, w_ref[...], (((1,), (1,)), ((), ())), preferred_element_type=F32
     ).astype(BF16)
@@ -213,7 +214,7 @@
     features, weight, bias, node_scale, cotangent, edge_slot, edge_row, edge_col, tile_row
 ):
     h, c = lax.axis_index("h"), lax.axis_index("c")
-    s = node_scale[:, None]
+    s = node_scale[None, :]
     bias = bias[None, :]
 
     slot = edge_slot.reshape(XY * H, EDGES)
@@ -225,7 +226,7 @@
     kept = lax.dynamic_index_in_dim(edges, h, 2, keepdims=False)
     came = swap(lax.dynamic_index_in_dim(edges, 1 - h, 2, keepdims=False), "h")
 
-    sources = exchange(spread(features, node_scale), ("x", "y"))
+    sources = exchange(spread(features, s), ("x", "y"))
 
     pairs = jnp.stack([jnp.where(h == 0, kept, came), jnp.where(h == 0, came, kept)], axis=1)
     lane = pairs.reshape(2 * H, E_ALL)

time: 120 us -> 118 us (0.983)
  blocking collectives: 51.1 us -> 74.9 us
  waiting for transfers between devices: 26.3 us -> 8.42 us
  starting transfers between devices: 29.9 us -> 22.4 us
    all_to_all x3 -> x4, blocking collectives: 51.1 us -> 74.9 us  [exchange(): return lax.all_to_all(array, axes, 0, 0, tiled=True)]
    all_to_all x2 -> x1, waiting for transfers between devices: 24 us -> 6.2 us  [exchange(): return lax.all_to_all(array, axes, 0, 0, tiled=True)]
    all_to_all x2 -> x1, starting transfers between devices: 15.8 us -> 7.6 us  [exchange(): return lax.all_to_all(array, axes, 0, 0, tiled=True)]
  transfers between devices with their start and end apart: 5 -> 4, of which waited for: 5 -> 4; matrix products, arithmetic and copies ran while one was open for 1% -> 1% of each run, Pallas kernels for 2% -> 2%
where the time goes in v6:
time: 118 us
  blocking collectives  74.9 us (63%)
  starting transfers between devices  22.4 us (19%)
  Pallas kernels  9.85 us (8%)
  waiting for transfers between devices  8.42 us (7%)
    all_to_all x4, blocking collectives, exchange(): return lax.all_to_all(array, axes, 0, 0, tiled=True)  74.9 us
    ppermute x3, starting transfers between devices, swap(): return lax.ppermute(array, axis, [(0, 1), (1, 0)])  14.8 us
    all_to_all x1, starting transfers between devices, exchange(): return lax.all_to_all(array, axes, 0, 0, tiled=True)  7.6 us
    all_to_all x1, waiting for transfers between devices, exchange(): return lax.all_to_all(array, axes, 0, 0, tiled=True)  6.2 us
  transfers between devices with their start and end apart: 4, of which 4 were waited for; matrix products, arithmetic and copies ran while one was open for 1% of the time, Pallas kernels for 2%

profile of v6, /device:TPU:1, one launch (start us, length us, event | category | flops | bytes accessed | tf_op | source)
XLA Modules:
  0.0 117.7 jit_solution(8610221026995927918)
XLA Ops:
  0.7 2.2 %shard_map.120 = bf16[16,128,256]{2,1,0:T(8,128)(2,1)} custom-call(bf16[128,256]{1,0:T(8,128)(2,1)} %x_ref.3, f32[1,128]{1,0:T(1,128)} %bitcast.32), custom_call_target="tpu_custom_call" | custom-call | tf_op jit(solution)/shard_map/pallas_call | solution.py:64
  2.8 7.6 %all-to-all-start = ((bf16[16,128,256]{2,1,0:T(8,128)(2,1)}), bf16[16,128,256]{2,1,0:T(8,128)(2,1)S(1)}, u32[]{:S(2)}, u32[]{:S(2)}) async-start(bf16[16,128,256]{2,1,0:T(8,128)(2,1)} %shard_map.120), calls=%async_computation | async-start | bytes 2097152 | tf_op jit(solution)/shard_map/all_to_all | solution.py:206
  10.5 0.1 broadcast_in_dim.47
  10.6 0.1 broadcast_in_dim.53
  10.6 0.1 broadcast_in_dim.51
  10.7 0.1 broadcast_in_dim.49
  10.8 0.0 copy-done.5
  11.0 0.1 add_select_fusion
  11.1 0.1 fusion.1
  11.2 7.0 %collective-permute-start = (s32[2,16,96]{2,1,0:T(8,128)S(1)}, s32[2,16,96]{2,1,0:T(8,128)S(1)}, u32[]{:S(2)}, u32[]{:S(2)}) collective-permute-start(s32[2,16,96]{2,1,0:T(8,128)S(1)} %bitcast.41), channel_id=1, source_target_pairs={{0,8},{8,0},{1,9},{9,1},{2,10},{10,2},{3,11},{11,3},{4,12},{12,4},... | collective-permute-start | bytes 36872 | tf_op jit(solution)/shard_map/ppermute | solution.py:210
  18.2 1.1 collective-permute-done
  19.4 0.1 reshape.176.lane_ref
  19.5 0.3 copy.27
  19.8 6.2 %all-to-all-done.x_ref = bf16[16,128,256]{2,1,0:T(8,128)(2,1)S(1)} async-done(((bf16[16,128,256]{2,1,0:T(8,128)(2,1)}), bf16[16,128,256]{2,1,0:T(8,128)(2,1)S(1)}, u32[]{:S(2)}, u32[]{:S(2)}) %all-to-all-start) | async-done | bytes 1048608 | tf_op jit(solution)/shard_map/all_to_all | solution.py:206
  26.0 1.5 %shard_map.121 = (bf16[2,1536,256]{2,1,0:T(8,128)(2,1)S(1)}, bf16[2,512,256]{2,1,0:T(8,128)(2,1)S(1)}) custom-call(bf16[16,128,256]{2,1,0:T(8,128)(2,1)S(1)} %all-to-all-done.x_ref, s32[4,1536]{1,0:T(4,128)S(1)} %reshape.176.lane_ref, s32[1536,4]{1,0:T(8,128)S(1)} %bitcast.28), custom_call_target="tpu_custom_call" | custom-call | flops 1006632960 | bytes 2097152 | tf_op jit(solution)/shard_map/pallas_call | solution.py:236
  27.4 3.2 %collective-permute-start.1 = (bf16[2,512,256]{2,1,0:T(8,128)(2,1)S(1)}, bf16[2,512,256]{2,1,0:T(8,128)(2,1)S(1)}, u32[]{:S(2)}, u32[]{:S(2)}) collective-permute-start(bf16[2,512,256]{2,1,0:T(8,128)(2,1)S(1)} %get-tuple-element.14), channel_id=1, source_target_pairs={{0,1},{1,0},{2,3},{3,2},{4,5},{5,4},{6,7},{7,6},{8,9},{9,8},{10,11... | collective-permute-start | bytes 1572872 | tf_op jit(solution)/shard_map/ppermute | solution.py:210
  30.6 1.0 shard_map.122.mine_ref
  31.6 0.0 copy-start
  31.7 0.5 collective-permute-done.1.other_ref
  32.2 0.1 shard_map.123
  32.3 24.7 %all_to_all.25.part_ref = bf16[8,128,256]{2,1,0:T(8,128)(2,1)S(1)} all-to-all(bf16[8,128,256]{2,1,0:T(8,128)(2,1)S(1)} %bitcast.31), channel_id=1, replica_groups=mesh['x'=4,'y'=4,'h'=2,'l'=4,'c'=2] {'h','l'}, dimensions={0} | all-to-all | bytes 1048576 | tf_op jit(solution)/shard_map/all_to_all | solution.py:206
  57.0 1.1 shard_map.124
  58.1 10.2 %all_to_all.26.w_ref = bf16[16,32,256]{2,1,0:T(8,128)(2,1)S(1)} all-to-all(bf16[16,32,256]{2,1,0:T(8,128)(2,1)S(1)} %get-tuple-element.16), channel_id=1, replica_groups=mesh['x'=4,'y'=4,'h'=2,'l'=4,'c'=2] {'x','y'}, dimensions={0} | all-to-all | bytes 524288 | tf_op jit(solution)/shard_map/all_to_all | solution.py:206
  68.2 0.1 shard_map.125
  68.3 19.1 %all_to_all.27.mine_ref = bf16[8,160,256]{2,1,0:T(8,128)(2,1)S(1)} all-to-all(bf16[8,160,256]{2,1,0:T(8,128)(2,1)S(1)} %shard_map.125), channel_id=1, replica_groups=mesh['x'=4,'y'=4,'h'=2,'l'=4,'c'=2] {'h','l'}, dimensions={0} | all-to-all | bytes 1310720 | tf_op jit(solution)/shard_map/all_to_all | solution.py:206
  87.4 4.6 %collective-permute-start.2 = (bf16[8,160,256]{2,1,0:T(8,128)(2,1)S(1)}, bf16[8,160,256]{2,1,0:T(8,128)(2,1)S(1)}, u32[]{:S(2)}, u32[]{:S(2)}) collective-permute-start(bf16[8,160,256]{2,1,0:T(8,128)(2,1)S(1)} %all_to_all.27.mine_ref), channel_id=1, source_target_pairs={{0,1},{1,0},{2,3},{3,2},{4,5},{5,4},{6,7},{7,6},{8,9},{9,8},{10,11... | collective-permute-start | bytes 1966088 | tf_op jit(solution)/shard_map/ppermute | solution.py:210
  92.0 0.1 pad_add_fusion.1.col_ref
  92.0 1.0 shard_map.126.picked_ref
  93.1 0.6 collective-permute-done.2.other_ref
  93.7 2.0 %shard_map.127 = (bf16[16,144,256]{2,1,0:T(8,128)(2,1)S(1)}, f32[1,256]{1,0:T(1,128)}) custom-call(bf16[16,192,256]{2,1,0:T(8,128)(2,1)S(1)} %shard_map.126.picked_ref, bf16[8,160,256]{2,1,0:T(8,128)(2,1)S(1)} %all_to_all.27.mine_ref, bf16[8,160,256]{2,1,0:T(8,128)(2,1)S(1)} %collective-permute-done.2.other_ref, s32[1536,4]{1,0:T(8,128)S(1)} %bitcast.30, ...), custom_call_target="tpu_custom_call" | custom-call | flops 1006632960 | bytes 2097152 | tf_op jit(solution)/shard_map/pallas_call | solution.py:262
  95.7 21.0 %all_to_all.28.part_ref = bf16[16,144,256]{2,1,0:T(8,128)(2,1)S(1)} all-to-all(bf16[16,144,256]{2,1,0:T(8,128)(2,1)S(1)} %get-tuple-element.18), channel_id=1, replica_groups=mesh['x'=4,'y'=4,'h'=2,'l'=4,'c'=2] {'x','y'}, dimensions={0} | all-to-all | bytes 2359296 | tf_op jit(solution)/shard_map/all_to_all | solution.py:206
  116.7 1.0 shard_map.128
  (27 shorter events, 0.2 us)
Async XLA Ops:
  0.6 9.8 %copy-start.8 = (s32[1,1,32,4]{2,3,1,0:T(4,128)S(1)}, s32[1,1,32,4]{2,3,1,0:T(4,128)}, u32[]{:S(2)}) copy-start(s32[1,1,32,4]{2,3,1,0:T(4,128)} %param.17) | copy-start | bytes 1540
  0.6 10.2 %copy-start.5 = (s32[1,1,32,96]{3,2,1,0:T(8,128)S(1)}, s32[1,1,32,96]{3,2,1,0:T(8,128)}, u32[]{:S(2)}) copy-start(s32[1,1,32,96]{3,2,1,0:T(8,128)} %param.14) | copy-start | bytes 36868
  0.7 10.3 %copy-start.6 = (s32[1,1,32,96]{3,2,1,0:T(8,128)S(1)}, s32[1,1,32,96]{3,2,1,0:T(8,128)}, u32[]{:S(2)}) copy-start(s32[1,1,32,96]{3,2,1,0:T(8,128)} %param.15) | copy-start | bytes 36868
  0.7 10.5 %copy-start.7 = (s32[1,1,32,96]{3,2,1,0:T(8,128)S(1)}, s32[1,1,32,96]{3,2,1,0:T(8,128)}, u32[]{:S(2)}) copy-start(s32[1,1,32,96]{3,2,1,0:T(8,128)} %param.16) | copy-start | bytes 36868
  2.8 23.1 %all-to-all-start = ((bf16[16,128,256]{2,1,0:T(8,128)(2,1)}), bf16[16,128,256]{2,1,0:T(8,128)(2,1)S(1)}, u32[]{:S(2)}, u32[]{:S(2)}) async-start(bf16[16,128,256]{2,1,0:T(8,128)(2,1)} %shard_map.120), calls=%async_computation | async-start | bytes 2097152 | tf_op jit(solution)/shard_map/all_to_all | solution.py:206
  11.2 8.1 %collective-permute-start = (s32[2,16,96]{2,1,0:T(8,128)S(1)}, s32[2,16,96]{2,1,0:T(8,128)S(1)}, u32[]{:S(2)}, u32[]{:S(2)}) collective-permute-start(s32[2,16,96]{2,1,0:T(8,128)S(1)} %bitcast.41), channel_id=1, source_target_pairs={{0,8},{8,0},{1,9},{9,1},{2,10},{10,2},{3,11},{11,3},{4,12},{12,4},... | collective-permute-start | bytes 36872 | tf_op jit(solution)/shard_map/ppermute | solution.py:210
  27.4 4.8 %collective-permute-start.1 = (bf16[2,512,256]{2,1,0:T(8,128)(2,1)S(1)}, bf16[2,512,256]{2,1,0:T(8,128)(2,1)S(1)}, u32[]{:S(2)}, u32[]{:S(2)}) collective-permute-start(bf16[2,512,256]{2,1,0:T(8,128)(2,1)S(1)} %get-tuple-element.14), channel_id=1, source_target_pairs={{0,1},{1,0},{2,3},{3,2},{4,5},{5,4},{6,7},{7,6},{8,9},{9,8},{10,11... | collective-permute-start | bytes 1572872 | tf_op jit(solution)/shard_map/ppermute | solution.py:210
  31.6 25.3 %copy-start = (bf16[256,256]{1,0:T(8,128)(2,1)S(1)}, bf16[256,256]{1,0:T(8,128)(2,1)}, u32[]{:S(2)}) copy-start(bf16[256,256]{1,0:T(8,128)(2,1)} %w_ref.3) | copy-start | bytes 393220
  31.6 25.3 %copy-start.1 = (bf16[128,256]{1,0:T(8,128)(2,1)S(1)}, bf16[128,256]{1,0:T(8,128)(2,1)}, u32[]{:S(2)}) copy-start(bf16[128,256]{1,0:T(8,128)(2,1)} %x_ref.3) | copy-start | bytes 196612
  31.7 25.3 %copy-start.2 = (bf16[128,256]{1,0:T(8,128)(2,1)S(1)}, bf16[128,256]{1,0:T(8,128)(2,1)}, u32[]{:S(2)}) copy-start(bf16[128,256]{1,0:T(8,128)(2,1)} %ct_ref.1) | copy-start | bytes 196612
  31.7 25.3 %copy-start.3 = (f32[128]{0:T(128)S(1)}, f32[128]{0:T(128)}, u32[]{:S(2)}) copy-start(f32[128]{0:T(128)} %param.12) | copy-start | bytes 1540
  31.7 25.3 %copy-start.4 = (f32[256]{0:T(256)S(1)}, f32[256]{0:T(256)}, u32[]{:S(2)}) copy-start(f32[256]{0:T(256)} %param.11) | copy-start | bytes 3076
  87.4 6.3 %collective-permute-start.2 = (bf16[8,160,256]{2,1,0:T(8,128)(2,1)S(1)}, bf16[8,160,256]{2,1,0:T(8,128)(2,1)S(1)}, u32[]{:S(2)}, u32[]{:S(2)}) collective-permute-start(bf16[8,160,256]{2,1,0:T(8,128)(2,1)S(1)} %all_to_all.27.mine_ref), channel_id=1, source_target_pairs={{0,1},{1,0},{2,3},{3,2},{4,5},{5,4},{6,7},{7,6},{8,9},{9,8},{10,11... | collective-permute-start | bytes 1966088 | tf_op jit(solution)/shard_map/ppermute | solution.py:210

commit v7 on v6

--- a/solution.py
+++ b/solution.py
@@ -14,7 +14,7 @@
 ROWS = C * HALF
 E_ALL = XY * EDGES
 STEP = 4 * EDGES
-WR, BB = F // XY, 16
+WR, BB = F // XY, 8
 ZCHUNK = TILE + WR + BB
 XCHUNK = TILE + WR
 F32, BF16, I32 = jnp.float32, jnp.bfloat16, jnp.int32
@@ -135,7 +135,8 @@
         pay_ref[k, pl.ds(TILE + WR, BB), :] = bias_rows
 
 
-def backward_mine_kernel(mine_ref, sub_ref, picked_ref, grads):
+def backward_mine_kernel(mine_ref, sub_ref, act_ref, picked_ref, out_ref, grads):
+    out_ref[...] = act_ref[...]
     for b in range(H):
         for k in range(L):
             grads[pl.ds(k * TILE, TILE), :] = mine_ref[b * L + k, pl.ds(0, TILE), :]
@@ -178,7 +179,8 @@
         pay_ref[j, pl.ds(TILE, WR), :] = own
 
 
-def final_kernel(part_ref, g_ref, s_ref, w_ref, fg_ref, wg_ref):
+def final_kernel(part_ref, g_ref, s_ref, w_ref, bias_ref, fg_ref, wg_ref, out_ref):
+    out_ref[...] = bias_ref[...]
     back = g_ref[...].astype(F32)
     for k in range(XY):
         back += part_ref[k, pl.ds(0, TILE), :].astype(F32)
@@ -245,7 +247,7 @@
     (partial,) = call(add_kernel, [((H, HALF, F), BF16)])(mine, other)
     partial = partial.reshape(ZN, TILE, F)
     partial = exchange(partial, ("h", "l"))
-    output, g, w_parts = call(
+    act, g, w_parts = call(
         middle_kernel,
         [((TILE, F), BF16), ((TILE, F), BF16), ((XY, WR + BB, F), BF16)],
     )(partial, features, s, weight, bias, cotangent)
@@ -253,22 +255,22 @@
     (pay,) = call(load_kernel, [((ZN, ZCHUNK, F), BF16)])(w_parts, g)
     around = exchange(pay, ("h", "l"))
     other = swap(around, "c")
-    (picked,) = call(
+    picked, output = call(
         backward_mine_kernel,
-        [((XY, H * EDGES, F), BF16)],
+        [((XY, H * EDGES, F), BF16), ((TILE, F), BF16)],
         [((HALF, F), BF16)],
         flops=4 * E_ALL * F * HALF,
-    )(around, sub)
-    terms, bias_grad = call(
+    )(around, sub, act)
+    terms, bias_sum = call(
         backward_kernel,
         [((XY, XCHUNK, F), BF16), ((1, F), F32)],
         [((HALF, F), BF16), ((XY, H * EDGES, F), BF16)],
         flops=4 * E_ALL * F * (HALF + TILE),
     )(picked, around, other, sub, columns)
     terms = exchange(terms, ("x", "y"))
-    feature_grad, weight_grad = call(
-        final_kernel, [((TILE, F), BF16), ((F, F), F32)]
-    )(terms, g, s, weight)
+    feature_grad, weight_grad, bias_grad = call(
+        final_kernel, [((TILE, F), BF16), ((F, F), F32), ((1, F), F32)]
+    )(terms, g, s, weight, bias_sum)
     return output, feature_grad, weight_grad, bias_grad.reshape(F)
 
 

time: 118 us -> 116 us (0.983)
  transfers between devices with their start and end apart: 4 -> 4, of which waited for: 4 -> 3; matrix products, arithmetic and copies ran while one was open for 1% -> 1% of each run, Pallas kernels for 2% -> 2%
where the time goes in v7:
time: 116 us
  blocking collectives  74.3 us (64%)
  starting transfers between devices  22 us (19%)
  Pallas kernels  9.45 us (8%)
  waiting for transfers between devices  7.83 us (7%)
    all_to_all x4, blocking collectives, exchange(): return lax.all_to_all(array, axes, 0, 0, tiled=True)  74.3 us
    ppermute x3, starting transfers between devices, swap(): return lax.ppermute(array, axis, [(0, 1), (1, 0)])  14.4 us
    all_to_all x1, starting transfers between devices, exchange(): return lax.all_to_all(array, axes, 0, 0, tiled=True)  7.6 us
    all_to_all x1, waiting for transfers between devices, exchange(): return lax.all_to_all(array, axes, 0, 0, tiled=True)  6.2 us
  transfers between devices with their start and end apart: 4, of which 3 were waited for; matrix products, arithmetic and copies ran while one was open for 1% of the time, Pallas kernels for 2%

profile of v7, /device:TPU:1, one launch (start us, length us, event | category | flops | bytes accessed | tf_op | source)
XLA Modules:
  0.0 115.6 jit_solution(1691747302099626650)
XLA Ops:
  0.7 2.2 %shard_map.120 = bf16[16,128,256]{2,1,0:T(8,128)(2,1)} custom-call(bf16[128,256]{1,0:T(8,128)(2,1)} %x_ref.3, f32[1,128]{1,0:T(1,128)} %bitcast.32), custom_call_target="tpu_custom_call" | custom-call | tf_op jit(solution)/shard_map/pallas_call | solution.py:64
  2.8 7.6 %all-to-all-start = ((bf16[16,128,256]{2,1,0:T(8,128)(2,1)}), bf16[16,128,256]{2,1,0:T(8,128)(2,1)S(1)}, u32[]{:S(2)}, u32[]{:S(2)}) async-start(bf16[16,128,256]{2,1,0:T(8,128)(2,1)} %shard_map.120), calls=%async_computation | async-start | bytes 2097152 | tf_op jit(solution)/shard_map/all_to_all | solution.py:208
  10.6 0.1 broadcast_in_dim.53
  10.7 0.1 broadcast_in_dim.51
  10.8 0.1 broadcast_in_dim.49
  10.9 0.1 broadcast_in_dim.47
  11.0 0.0 copy-done.6
  11.0 0.1 add_select_fusion
  11.2 0.1 fusion.1
  11.2 7.0 %collective-permute-start = (s32[2,16,96]{2,1,0:T(8,128)S(1)}, s32[2,16,96]{2,1,0:T(8,128)S(1)}, u32[]{:S(2)}, u32[]{:S(2)}) collective-permute-start(s32[2,16,96]{2,1,0:T(8,128)S(1)} %bitcast.41), channel_id=1, source_target_pairs={{0,8},{8,0},{1,9},{9,1},{2,10},{10,2},{3,11},{11,3},{4,12},{12,4},... | collective-permute-start | bytes 36872 | tf_op jit(solution)/shard_map/ppermute | solution.py:212
  18.2 1.1 collective-permute-done
  19.4 0.1 reshape.176.lane_ref
  19.5 0.3 copy.27
  19.8 6.2 %all-to-all-done.x_ref = bf16[16,128,256]{2,1,0:T(8,128)(2,1)S(1)} async-done(((bf16[16,128,256]{2,1,0:T(8,128)(2,1)}), bf16[16,128,256]{2,1,0:T(8,128)(2,1)S(1)}, u32[]{:S(2)}, u32[]{:S(2)}) %all-to-all-start) | async-done | bytes 1048608 | tf_op jit(solution)/shard_map/all_to_all | solution.py:208
  26.0 1.5 %shard_map.121 = (bf16[2,1536,256]{2,1,0:T(8,128)(2,1)S(1)}, bf16[2,512,256]{2,1,0:T(8,128)(2,1)S(1)}) custom-call(bf16[16,128,256]{2,1,0:T(8,128)(2,1)S(1)} %all-to-all-done.x_ref, s32[4,1536]{1,0:T(4,128)S(1)} %reshape.176.lane_ref, s32[1536,4]{1,0:T(8,128)S(1)} %bitcast.29), custom_call_target="tpu_custom_call" | custom-call | flops 1006632960 | bytes 2097152 | tf_op jit(solution)/shard_map/pallas_call | solution.py:238
  27.4 3.2 %collective-permute-start.1 = (bf16[2,512,256]{2,1,0:T(8,128)(2,1)S(1)}, bf16[2,512,256]{2,1,0:T(8,128)(2,1)S(1)}, u32[]{:S(2)}, u32[]{:S(2)}) collective-permute-start(bf16[2,512,256]{2,1,0:T(8,128)(2,1)S(1)} %get-tuple-element.17), channel_id=1, source_target_pairs={{0,1},{1,0},{2,3},{3,2},{4,5},{5,4},{6,7},{7,6},{8,9},{9,8},{10,11... | collective-permute-start | bytes 1572872 | tf_op jit(solution)/shard_map/ppermute | solution.py:212
  30.6 1.0 shard_map.122.mine_ref
  31.6 0.0 copy-start
  31.6 0.0 copy-start.1
  31.7 0.5 collective-permute-done.1.other_ref
  32.2 0.1 shard_map.123
  32.3 24.7 %all_to_all.25.part_ref = bf16[8,128,256]{2,1,0:T(8,128)(2,1)S(1)} all-to-all(bf16[8,128,256]{2,1,0:T(8,128)(2,1)S(1)} %bitcast.28), channel_id=1, replica_groups=mesh['x'=4,'y'=4,'h'=2,'l'=4,'c'=2] {'h','l'}, dimensions={0} | all-to-all | bytes 1048576 | tf_op jit(solution)/shard_map/all_to_all | solution.py:208
  57.0 0.7 shard_map.124
  57.7 9.8 %all_to_all.26.w_ref = bf16[16,24,256]{2,1,0:T(8,128)(2,1)S(1)} all-to-all(bf16[16,24,256]{2,1,0:T(8,128)(2,1)S(1)} %get-tuple-element.18), channel_id=1, replica_groups=mesh['x'=4,'y'=4,'h'=2,'l'=4,'c'=2] {'x','y'}, dimensions={0} | all-to-all | bytes 393216 | tf_op jit(solution)/shard_map/all_to_all | solution.py:208
  67.6 0.1 shard_map.125
  67.6 18.8 %all_to_all.27.mine_ref = bf16[8,152,256]{2,1,0:T(8,128)(2,1)S(1)} all-to-all(bf16[8,152,256]{2,1,0:T(8,128)(2,1)S(1)} %shard_map.125), channel_id=1, replica_groups=mesh['x'=4,'y'=4,'h'=2,'l'=4,'c'=2] {'h','l'}, dimensions={0} | all-to-all | bytes 1245184 | tf_op jit(solution)/shard_map/all_to_all | solution.py:208
  86.4 4.2 %collective-permute-start.2 = (bf16[8,152,256]{2,1,0:T(8,128)(2,1)S(1)}, bf16[8,152,256]{2,1,0:T(8,128)(2,1)S(1)}, u32[]{:S(2)}, u32[]{:S(2)}) collective-permute-start(bf16[8,152,256]{2,1,0:T(8,128)(2,1)S(1)} %all_to_all.27.mine_ref), channel_id=1, source_target_pairs={{0,1},{1,0},{2,3},{3,2},{4,5},{5,4},{6,7},{7,6},{8,9},{9,8},{10,11... | collective-permute-start | bytes 1867784 | tf_op jit(solution)/shard_map/ppermute | solution.py:212
  90.6 0.1 pad_add_fusion.1.col_ref
  90.7 1.6 %shard_map.126 = (bf16[16,192,256]{2,1,0:T(8,128)(2,1)S(1)}, bf16[128,256]{1,0:T(8,128)(2,1)}) custom-call(bf16[8,152,256]{2,1,0:T(8,128)(2,1)S(1)} %all_to_all.27.mine_ref, s32[1536,4]{1,0:T(8,128)S(1)} %bitcast.30, bf16[128,256]{1,0:T(8,128)(2,1)S(1)} %get-tuple-element.20.act_ref), custom_call_target="tpu_custom_call" | custom-call | flops 805306368 | bytes 2097152 | tf_op jit(solution)/shard_map/pallas_call | solution.py:258
  92.3 1.4 %shard_map.127 = (bf16[16,144,256]{2,1,0:T(8,128)(2,1)S(1)}, f32[1,256]{1,0:T(1,128)S(1)}) custom-call(bf16[16,192,256]{2,1,0:T(8,128)(2,1)S(1)} %get-tuple-element.22.picked_ref, bf16[8,152,256]{2,1,0:T(8,128)(2,1)S(1)} %all_to_all.27.mine_ref, bf16[8,152,256]{2,1,0:T(8,128)(2,1)S(1)} %collective-permute-done.2.other_ref, s32[1536,4]{1,0:T(8,128)S(1)} %bitcast.31, ...), custom_call_target="tpu_custom_call" | custom-call | flops 1006632960 | bytes 2097152 | tf_op jit(solution)/shard_map/pallas_call | solution.py:264
  93.7 21.0 %all_to_all.28.part_ref = bf16[16,144,256]{2,1,0:T(8,128)(2,1)S(1)} all-to-all(bf16[16,144,256]{2,1,0:T(8,128)(2,1)S(1)} %get-tuple-element.23), channel_id=1, replica_groups=mesh['x'=4,'y'=4,'h'=2,'l'=4,'c'=2] {'x','y'}, dimensions={0} | all-to-all | bytes 2359296 | tf_op jit(solution)/shard_map/all_to_all | solution.py:208
  114.7 1.0 shard_map.128
  (27 shorter events, 0.2 us)
Async XLA Ops:
  0.6 9.8 %copy-start.5 = (s32[1,1,32,96]{3,2,1,0:T(8,128)S(1)}, s32[1,1,32,96]{3,2,1,0:T(8,128)}, u32[]{:S(2)}) copy-start(s32[1,1,32,96]{3,2,1,0:T(8,128)} %param.14) | copy-start | bytes 36868
  0.6 10.0 %copy-start.8 = (s32[1,1,32,4]{2,3,1,0:T(4,128)S(1)}, s32[1,1,32,4]{2,3,1,0:T(4,128)}, u32[]{:S(2)}) copy-start(s32[1,1,32,4]{2,3,1,0:T(4,128)} %param.17) | copy-start | bytes 1540
  0.7 10.3 %copy-start.6 = (s32[1,1,32,96]{3,2,1,0:T(8,128)S(1)}, s32[1,1,32,96]{3,2,1,0:T(8,128)}, u32[]{:S(2)}) copy-start(s32[1,1,32,96]{3,2,1,0:T(8,128)} %param.15) | copy-start | bytes 36868
  0.7 10.5 %copy-start.7 = (s32[1,1,32,96]{3,2,1,0:T(8,128)S(1)}, s32[1,1,32,96]{3,2,1,0:T(8,128)}, u32[]{:S(2)}) copy-start(s32[1,1,32,96]{3,2,1,0:T(8,128)} %param.16) | copy-start | bytes 36868
  2.8 23.1 %all-to-all-start = ((bf16[16,128,256]{2,1,0:T(8,128)(2,1)}), bf16[16,128,256]{2,1,0:T(8,128)(2,1)S(1)}, u32[]{:S(2)}, u32[]{:S(2)}) async-start(bf16[16,128,256]{2,1,0:T(8,128)(2,1)} %shard_map.120), calls=%async_computation | async-start | bytes 2097152 | tf_op jit(solution)/shard_map/all_to_all | solution.py:208
  11.2 8.1 %collective-permute-start = (s32[2,16,96]{2,1,0:T(8,128)S(1)}, s32[2,16,96]{2,1,0:T(8,128)S(1)}, u32[]{:S(2)}, u32[]{:S(2)}) collective-permute-start(s32[2,16,96]{2,1,0:T(8,128)S(1)} %bitcast.41), channel_id=1, source_target_pairs={{0,8},{8,0},{1,9},{9,1},{2,10},{10,2},{3,11},{11,3},{4,12},{12,4},... | collective-permute-start | bytes 36872 | tf_op jit(solution)/shard_map/ppermute | solution.py:212
  27.4 4.8 %collective-permute-start.1 = (bf16[2,512,256]{2,1,0:T(8,128)(2,1)S(1)}, bf16[2,512,256]{2,1,0:T(8,128)(2,1)S(1)}, u32[]{:S(2)}, u32[]{:S(2)}) collective-permute-start(bf16[2,512,256]{2,1,0:T(8,128)(2,1)S(1)} %get-tuple-element.17), channel_id=1, source_target_pairs={{0,1},{1,0},{2,3},{3,2},{4,5},{5,4},{6,7},{7,6},{8,9},{9,8},{10,11... | collective-permute-start | bytes 1572872 | tf_op jit(solution)/shard_map/ppermute | solution.py:212
  31.6 25.4 %copy-start = (bf16[256,256]{1,0:T(8,128)(2,1)S(1)}, bf16[256,256]{1,0:T(8,128)(2,1)}, u32[]{:S(2)}) copy-start(bf16[256,256]{1,0:T(8,128)(2,1)} %w_ref.3) | copy-start | bytes 393220
  31.6 25.4 %copy-start.1 = (bf16[128,256]{1,0:T(8,128)(2,1)S(1)}, bf16[128,256]{1,0:T(8,128)(2,1)}, u32[]{:S(2)}) copy-start(bf16[128,256]{1,0:T(8,128)(2,1)} %x_ref.3) | copy-start | bytes 196612
  31.7 25.3 %copy-start.2 = (bf16[128,256]{1,0:T(8,128)(2,1)S(1)}, bf16[128,256]{1,0:T(8,128)(2,1)}, u32[]{:S(2)}) copy-start(bf16[128,256]{1,0:T(8,128)(2,1)} %ct_ref.1) | copy-start | bytes 196612
  31.7 25.3 %copy-start.3 = (f32[128]{0:T(128)S(1)}, f32[128]{0:T(128)}, u32[]{:S(2)}) copy-start(f32[128]{0:T(128)} %param.12) | copy-start | bytes 1540
  31.7 25.3 %copy-start.4 = (f32[256]{0:T(256)S(1)}, f32[256]{0:T(256)}, u32[]{:S(2)}) copy-start(f32[256]{0:T(256)} %param.11) | copy-start | bytes 3076
  86.4 5.8 %collective-permute-start.2 = (bf16[8,152,256]{2,1,0:T(8,128)(2,1)S(1)}, bf16[8,152,256]{2,1,0:T(8,128)(2,1)S(1)}, u32[]{:S(2)}, u32[]{:S(2)}) collective-permute-start(bf16[8,152,256]{2,1,0:T(8,128)(2,1)S(1)} %all_to_all.27.mine_ref), channel_id=1, source_target_pairs={{0,1},{1,0},{2,3},{3,2},{4,5},{5,4},{6,7},{7,6},{8,9},{9,8},{10,11... | collective-permute-start | bytes 1867784 | tf_op jit(solution)/shard_map/ppermute | solution.py:212

commit v8 on v7

--- a/solution.py
+++ b/solution.py
@@ -14,6 +14,7 @@
 ROWS = C * HALF
 E_ALL = XY * EDGES
 STEP = 4 * EDGES
+COPIES = 4
 WR, BB = F // XY, 8
 ZCHUNK = TILE + WR + BB
 XCHUNK = TILE + WR
@@ -50,9 +51,12 @@
         load.start()
     for load in loads:
         load.wait()
-    scaled[...] = (column(s[...]) * x[...].astype(F32)).astype(BF16)
+    value = (column(s[...]) * x[...].astype(F32)).astype(BF16)
+    for j in range(COPIES):
+        scaled[j] = value
     stores = [
-        pltpu.make_async_copy(scaled, out_ref.at[j], sems.at[2 + j]) for j in range(XY)
+        pltpu.make_async_copy(scaled, out_ref.at[pl.ds(j * COPIES, COPIES)], sems.at[2 + j])
+        for j in range(XY // COPIES)
     ]
     for store in stores:
         store.start()
@@ -69,19 +73,22 @@
         scratch_shapes=[
             pltpu.VMEM((TILE, F), BF16),
             pltpu.VMEM((1, TILE), F32),
-            pltpu.VMEM((TILE, F), BF16),
-            pltpu.SemaphoreType.DMA((2 + XY,)),
+            pltpu.VMEM((COPIES, TILE, F), BF16),
+            pltpu.SemaphoreType.DMA((2 + XY // COPIES,)),
         ],
         compiler_params=pltpu.CompilerParams(vmem_limit_bytes=63_480_000),
     )(features, node_scale)
 
 
 def forward_send_kernel(x_ref, lane_ref, sub_ref, gathered_ref, send_ref):
-    for b in range(H):
-        for j in range(XY):
-            rows = pl.ds(j * EDGES, EDGES)
-            pick = one_hot(sub_ref[rows, H + b : H + b + 1], (EDGES, TILE), 1)
-            gathered_ref[b, rows, :] = dot(pick, x_ref[j]).astype(BF16)
+    for j in range(XY):
+        rows = pl.ds(j * EDGES, EDGES)
+        picks = [
+            one_hot(sub_ref[rows, H + b : H + b + 1], (EDGES, TILE), 1) for b in range(H)
+        ]
+        value = dot(jnp.concatenate(picks), x_ref[j]).astype(BF16)
+        for b in range(H):
+            gathered_ref[b, rows, :] = value[b * EDGES : (b + 1) * EDGES]
     for b in range(H):
         place = one_hot(lane_ref[b : b + 1, :], (HALF, E_ALL), 0, HALF)
         send_ref[b] = dot(place, gathered_ref[b]).astype(BF16)

time: 116 us -> 116 us (level)
  no operation moved by 1% of the time
where the time goes in v8:
time: 116 us
  blocking collectives  74.3 us (64%)
  starting transfers between devices  22 us (19%)
  Pallas kernels  9.34 us (8%)
  waiting for transfers between devices  7.83 us (7%)
    all_to_all x4, blocking collectives, exchange(): return lax.all_to_all(array, axes, 0, 0, tiled=True)  74.3 us
    ppermute x3, starting transfers between devices, swap(): return lax.ppermute(array, axis, [(0, 1), (1, 0)])  14.4 us
    all_to_all x1, starting transfers between devices, exchange(): return lax.all_to_all(array, axes, 0, 0, tiled=True)  7.6 us
    all_to_all x1, waiting for transfers between devices, exchange(): return lax.all_to_all(array, axes, 0, 0, tiled=True)  6.2 us
  transfers between devices with their start and end apart: 4, of which 3 were waited for; matrix products, arithmetic and copies ran while one was open for 1% of the time, Pallas kernels for 2%

profile of v8, /device:TPU:1, one launch (start us, length us, event | category | flops | bytes accessed | tf_op | source)
XLA Modules:
  0.0 115.5 jit_solution(3725885193468915174)
XLA Ops:
  0.7 2.1 %shard_map.120 = bf16[16,128,256]{2,1,0:T(8,128)(2,1)} custom-call(bf16[128,256]{1,0:T(8,128)(2,1)} %x_ref.3, f32[1,128]{1,0:T(1,128)} %bitcast.32), custom_call_target="tpu_custom_call" | custom-call | tf_op jit(solution)/shard_map/pallas_call | solution.py:68
  2.7 7.6 %all-to-all-start = ((bf16[16,128,256]{2,1,0:T(8,128)(2,1)}), bf16[16,128,256]{2,1,0:T(8,128)(2,1)S(1)}, u32[]{:S(2)}, u32[]{:S(2)}) async-start(bf16[16,128,256]{2,1,0:T(8,128)(2,1)} %shard_map.120), calls=%async_computation | async-start | bytes 2097152 | tf_op jit(solution)/shard_map/all_to_all | solution.py:215
  10.5 0.1 broadcast_in_dim.53
  10.6 0.1 broadcast_in_dim.51
  10.7 0.1 broadcast_in_dim.49
  10.8 0.1 broadcast_in_dim.47
  10.9 0.0 copy-done.6
  10.9 0.1 add_select_fusion
  11.0 0.1 fusion.1
  11.1 7.0 %collective-permute-start = (s32[2,16,96]{2,1,0:T(8,128)S(1)}, s32[2,16,96]{2,1,0:T(8,128)S(1)}, u32[]{:S(2)}, u32[]{:S(2)}) collective-permute-start(s32[2,16,96]{2,1,0:T(8,128)S(1)} %bitcast.41), channel_id=1, source_target_pairs={{0,8},{8,0},{1,9},{9,1},{2,10},{10,2},{3,11},{11,3},{4,12},{12,4},... | collective-permute-start | bytes 36872 | tf_op jit(solution)/shard_map/ppermute | solution.py:219
  18.1 1.1 collective-permute-done
  19.3 0.1 reshape.176.lane_ref
  19.4 0.3 copy.27
  19.7 6.2 %all-to-all-done.x_ref = bf16[16,128,256]{2,1,0:T(8,128)(2,1)S(1)} async-done(((bf16[16,128,256]{2,1,0:T(8,128)(2,1)}), bf16[16,128,256]{2,1,0:T(8,128)(2,1)S(1)}, u32[]{:S(2)}, u32[]{:S(2)}) %all-to-all-start) | async-done | bytes 1048608 | tf_op jit(solution)/shard_map/all_to_all | solution.py:215
  25.9 1.4 %shard_map.121 = (bf16[2,1536,256]{2,1,0:T(8,128)(2,1)S(1)}, bf16[2,512,256]{2,1,0:T(8,128)(2,1)S(1)}) custom-call(bf16[16,128,256]{2,1,0:T(8,128)(2,1)S(1)} %all-to-all-done.x_ref, s32[4,1536]{1,0:T(4,128)S(1)} %reshape.176.lane_ref, s32[1536,4]{1,0:T(8,128)S(1)} %bitcast.29), custom_call_target="tpu_custom_call" | custom-call | flops 1006632960 | bytes 2097152 | tf_op jit(solution)/shard_map/pallas_call | solution.py:245
  27.3 3.2 %collective-permute-start.1 = (bf16[2,512,256]{2,1,0:T(8,128)(2,1)S(1)}, bf16[2,512,256]{2,1,0:T(8,128)(2,1)S(1)}, u32[]{:S(2)}, u32[]{:S(2)}) collective-permute-start(bf16[2,512,256]{2,1,0:T(8,128)(2,1)S(1)} %get-tuple-element.17), channel_id=1, source_target_pairs={{0,1},{1,0},{2,3},{3,2},{4,5},{5,4},{6,7},{7,6},{8,9},{9,8},{10,11... | collective-permute-start | bytes 1572872 | tf_op jit(solution)/shard_map/ppermute | solution.py:219
  30.5 1.0 shard_map.122.mine_ref
  31.5 0.0 copy-start
  31.5 0.0 copy-start.1
  31.6 0.5 collective-permute-done.1.other_ref
  32.1 0.1 shard_map.123
  32.2 24.7 %all_to_all.25.part_ref = bf16[8,128,256]{2,1,0:T(8,128)(2,1)S(1)} all-to-all(bf16[8,128,256]{2,1,0:T(8,128)(2,1)S(1)} %bitcast.28), channel_id=1, replica_groups=mesh['x'=4,'y'=4,'h'=2,'l'=4,'c'=2] {'h','l'}, dimensions={0} | all-to-all | bytes 1048576 | tf_op jit(solution)/shard_map/all_to_all | solution.py:215
  56.9 0.7 shard_map.124
  57.6 9.8 %all_to_all.26.w_ref = bf16[16,24,256]{2,1,0:T(8,128)(2,1)S(1)} all-to-all(bf16[16,24,256]{2,1,0:T(8,128)(2,1)S(1)} %get-tuple-element.18), channel_id=1, replica_groups=mesh['x'=4,'y'=4,'h'=2,'l'=4,'c'=2] {'x','y'}, dimensions={0} | all-to-all | bytes 393216 | tf_op jit(solution)/shard_map/all_to_all | solution.py:215
  67.5 0.1 shard_map.125
  67.5 18.8 %all_to_all.27.mine_ref = bf16[8,152,256]{2,1,0:T(8,128)(2,1)S(1)} all-to-all(bf16[8,152,256]{2,1,0:T(8,128)(2,1)S(1)} %shard_map.125), channel_id=1, replica_groups=mesh['x'=4,'y'=4,'h'=2,'l'=4,'c'=2] {'h','l'}, dimensions={0} | all-to-all | bytes 1245184 | tf_op jit(solution)/shard_map/all_to_all | solution.py:215
  86.3 4.2 %collective-permute-start.2 = (bf16[8,152,256]{2,1,0:T(8,128)(2,1)S(1)}, bf16[8,152,256]{2,1,0:T(8,128)(2,1)S(1)}, u32[]{:S(2)}, u32[]{:S(2)}) collective-permute-start(bf16[8,152,256]{2,1,0:T(8,128)(2,1)S(1)} %all_to_all.27.mine_ref), channel_id=1, source_target_pairs={{0,1},{1,0},{2,3},{3,2},{4,5},{5,4},{6,7},{7,6},{8,9},{9,8},{10,11... | collective-permute-start | bytes 1867784 | tf_op jit(solution)/shard_map/ppermute | solution.py:219
  90.5 0.1 pad_add_fusion.1.col_ref
  90.6 1.6 %shard_map.126 = (bf16[16,192,256]{2,1,0:T(8,128)(2,1)S(1)}, bf16[128,256]{1,0:T(8,128)(2,1)}) custom-call(bf16[8,152,256]{2,1,0:T(8,128)(2,1)S(1)} %all_to_all.27.mine_ref, s32[1536,4]{1,0:T(8,128)S(1)} %bitcast.30, bf16[128,256]{1,0:T(8,128)(2,1)S(1)} %get-tuple-element.20.act_ref), custom_call_target="tpu_custom_call" | custom-call | flops 805306368 | bytes 2097152 | tf_op jit(solution)/shard_map/pallas_call | solution.py:265
  92.2 1.4 %shard_map.127 = (bf16[16,144,256]{2,1,0:T(8,128)(2,1)S(1)}, f32[1,256]{1,0:T(1,128)S(1)}) custom-call(bf16[16,192,256]{2,1,0:T(8,128)(2,1)S(1)} %get-tuple-element.22.picked_ref, bf16[8,152,256]{2,1,0:T(8,128)(2,1)S(1)} %all_to_all.27.mine_ref, bf16[8,152,256]{2,1,0:T(8,128)(2,1)S(1)} %collective-permute-done.2.other_ref, s32[1536,4]{1,0:T(8,128)S(1)} %bitcast.31, ...), custom_call_target="tpu_custom_call" | custom-call | flops 1006632960 | bytes 2097152 | tf_op jit(solution)/shard_map/pallas_call | solution.py:271
  93.6 21.0 %all_to_all.28.part_ref = bf16[16,144,256]{2,1,0:T(8,128)(2,1)S(1)} all-to-all(bf16[16,144,256]{2,1,0:T(8,128)(2,1)S(1)} %get-tuple-element.23), channel_id=1, replica_groups=mesh['x'=4,'y'=4,'h'=2,'l'=4,'c'=2] {'x','y'}, dimensions={0} | all-to-all | bytes 2359296 | tf_op jit(solution)/shard_map/all_to_all | solution.py:215
  114.5 1.0 shard_map.128
  (27 shorter events, 0.2 us)
Async XLA Ops:
  0.6 9.7 %copy-start.5 = (s32[1,1,32,96]{3,2,1,0:T(8,128)S(1)}, s32[1,1,32,96]{3,2,1,0:T(8,128)}, u32[]{:S(2)}) copy-start(s32[1,1,32,96]{3,2,1,0:T(8,128)} %param.14) | copy-start | bytes 36868
  0.6 9.8 %copy-start.8 = (s32[1,1,32,4]{2,3,1,0:T(4,128)S(1)}, s32[1,1,32,4]{2,3,1,0:T(4,128)}, u32[]{:S(2)}) copy-start(s32[1,1,32,4]{2,3,1,0:T(4,128)} %param.17) | copy-start | bytes 1540
  0.7 10.2 %copy-start.6 = (s32[1,1,32,96]{3,2,1,0:T(8,128)S(1)}, s32[1,1,32,96]{3,2,1,0:T(8,128)}, u32[]{:S(2)}) copy-start(s32[1,1,32,96]{3,2,1,0:T(8,128)} %param.15) | copy-start | bytes 36868
  0.7 10.4 %copy-start.7 = (s32[1,1,32,96]{3,2,1,0:T(8,128)S(1)}, s32[1,1,32,96]{3,2,1,0:T(8,128)}, u32[]{:S(2)}) copy-start(s32[1,1,32,96]{3,2,1,0:T(8,128)} %param.16) | copy-start | bytes 36868
  2.7 23.1 %all-to-all-start = ((bf16[16,128,256]{2,1,0:T(8,128)(2,1)}), bf16[16,128,256]{2,1,0:T(8,128)(2,1)S(1)}, u32[]{:S(2)}, u32[]{:S(2)}) async-start(bf16[16,128,256]{2,1,0:T(8,128)(2,1)} %shard_map.120), calls=%async_computation | async-start | bytes 2097152 | tf_op jit(solution)/shard_map/all_to_all | solution.py:215
  11.1 8.1 %collective-permute-start = (s32[2,16,96]{2,1,0:T(8,128)S(1)}, s32[2,16,96]{2,1,0:T(8,128)S(1)}, u32[]{:S(2)}, u32[]{:S(2)}) collective-permute-start(s32[2,16,96]{2,1,0:T(8,128)S(1)} %bitcast.41), channel_id=1, source_target_pairs={{0,8},{8,0},{1,9},{9,1},{2,10},{10,2},{3,11},{11,3},{4,12},{12,4},... | collective-permute-start | bytes 36872 | tf_op jit(solution)/shard_map/ppermute | solution.py:219
  27.3 4.8 %collective-permute-start.1 = (bf16[2,512,256]{2,1,0:T(8,128)(2,1)S(1)}, bf16[2,512,256]{2,1,0:T(8,128)(2,1)S(1)}, u32[]{:S(2)}, u32[]{:S(2)}) collective-permute-start(bf16[2,512,256]{2,1,0:T(8,128)(2,1)S(1)} %get-tuple-element.17), channel_id=1, source_target_pairs={{0,1},{1,0},{2,3},{3,2},{4,5},{5,4},{6,7},{7,6},{8,9},{9,8},{10,11... | collective-permute-start | bytes 1572872 | tf_op jit(solution)/shard_map/ppermute | solution.py:219
  31.5 25.4 %copy-start = (bf16[256,256]{1,0:T(8,128)(2,1)S(1)}, bf16[256,256]{1,0:T(8,128)(2,1)}, u32[]{:S(2)}) copy-start(bf16[256,256]{1,0:T(8,128)(2,1)} %w_ref.3) | copy-start | bytes 393220
  31.5 25.4 %copy-start.1 = (bf16[128,256]{1,0:T(8,128)(2,1)S(1)}, bf16[128,256]{1,0:T(8,128)(2,1)}, u32[]{:S(2)}) copy-start(bf16[128,256]{1,0:T(8,128)(2,1)} %x_ref.3) | copy-start | bytes 196612
  31.5 25.3 %copy-start.2 = (bf16[128,256]{1,0:T(8,128)(2,1)S(1)}, bf16[128,256]{1,0:T(8,128)(2,1)}, u32[]{:S(2)}) copy-start(bf16[128,256]{1,0:T(8,128)(2,1)} %ct_ref.1) | copy-start | bytes 196612
  31.6 25.3 %copy-start.3 = (f32[128]{0:T(128)S(1)}, f32[128]{0:T(128)}, u32[]{:S(2)}) copy-start(f32[128]{0:T(128)} %param.12) | copy-start | bytes 1540
  31.6 25.3 %copy-start.4 = (f32[256]{0:T(256)S(1)}, f32[256]{0:T(256)}, u32[]{:S(2)}) copy-start(f32[256]{0:T(256)} %param.11) | copy-start | bytes 3076
  86.3 5.8 %collective-permute-start.2 = (bf16[8,152,256]{2,1,0:T(8,128)(2,1)S(1)}, bf16[8,152,256]{2,1,0:T(8,128)(2,1)S(1)}, u32[]{:S(2)}, u32[]{:S(2)}) collective-permute-start(bf16[8,152,256]{2,1,0:T(8,128)(2,1)S(1)} %all_to_all.27.mine_ref), channel_id=1, source_target_pairs={{0,1},{1,0},{2,3},{3,2},{4,5},{5,4},{6,7},{7,6},{8,9},{9,8},{10,11... | collective-permute-start | bytes 1867784 | tf_op jit(solution)/shard_map/ppermute | solution.py:219

commit v9 on v8

--- a/solution.py
+++ b/solution.py
@@ -14,7 +14,6 @@
 ROWS = C * HALF
 E_ALL = XY * EDGES
 STEP = 4 * EDGES
-COPIES = 4
 WR, BB = F // XY, 8
 ZCHUNK = TILE + WR + BB
 XCHUNK = TILE + WR
@@ -40,44 +39,6 @@
 
 def column(row):
     return jnp.transpose(jnp.broadcast_to(row, (TILE, TILE)))[:, :1]
-
-
-def spread_kernel(x_ref, s_ref, out_ref, x, s, scaled, sems):
-    loads = [
-        pltpu.make_async_copy(x_ref, x, sems.at[0]),
-        pltpu.make_async_copy(s_ref, s, sems.at[1]),
-    ]
-    for load in loads:
-        load.start()
-    for load in loads:
-        load.wait()
-    value = (column(s[...]) * x[...].astype(F32)).astype(BF16)
-    for j in range(COPIES):
-        scaled[j] = value
-    stores = [
-        pltpu.make_async_copy(scaled, out_ref.at[pl.ds(j * COPIES, COPIES)], sems.at[2 + j])
-        for j in range(XY // COPIES)
-    ]
-    for store in stores:
-        store.start()
-    for store in stores:
-        store.wait()
-
-
-def spread(features, node_scale):
-    return pl.pallas_call(
-        spread_kernel,
-        out_shape=jax.ShapeDtypeStruct((XY, TILE, F), BF16),
-        in_specs=[pl.BlockSpec(memory_space=pltpu.HBM)] * 2,
-        out_specs=pl.BlockSpec(memory_space=pltpu.HBM),
-        scratch_shapes=[
-            pltpu.VMEM((TILE, F), BF16),
-            pltpu.VMEM((1, TILE), F32),
-            pltpu.VMEM((COPIES, TILE, F), BF16),
-            pltpu.SemaphoreType.DMA((2 + XY // COPIES,)),
-        ],
-        compiler_params=pltpu.CompilerParams(vmem_limit_bytes=63_480_000),
-    )(features, node_scale)
 
 
 def forward_send_kernel(x_ref, lane_ref, sub_ref, gathered_ref, send_ref):
@@ -235,7 +196,9 @@
     kept = lax.dynamic_index_in_dim(edges, h, 2, keepdims=False)
     came = swap(lax.dynamic_index_in_dim(edges, 1 - h, 2, keepdims=False), "h")
 
-    sources = exchange(spread(features, s), ("x", "y"))
+    scaled = (node_scale[:, None] * features.astype(F32)).astype(BF16)
+    copies = jnp.concatenate([scaled] * XY).reshape(XY, TILE, F)
+    sources = exchange(copies, ("x", "y"))
 
     pairs = jnp.stack([jnp.where(h == 0, kept, came), jnp.where(h == 0, came, kept)], axis=1)
     lane = pairs.reshape(2 * H, E_ALL)

time: 116 us -> 136 us (1.17)
  other arithmetic: 0.3 us -> 21.9 us
  Pallas kernels: 9.34 us -> 7.25 us
    unnamed x0 -> x15, other arithmetic: none -> 20.9 us
    pallas_call x1 -> x0, Pallas kernels: 2.06 us -> none  [spread(): pl.pallas_call(spread_kernel, out_shape=jax.ShapeDtypeStruct((XY, TILE, F...]
where the time goes in v9:
time: 136 us; the launch traced here: 135 us
  blocking collectives  74.3 us (55%)
  starting transfers between devices  22 us (16%)
  other arithmetic  21.9 us (16%)
  waiting for transfers between devices  7.86 us (6%)
  Pallas kernels  7.25 us (5%)
    all_to_all x4, blocking collectives, exchange(): return lax.all_to_all(array, axes, 0, 0, tiled=True)  74.3 us
    unnamed x15, other arithmetic  20.9 us
    ppermute x3, starting transfers between devices, swap(): return lax.ppermute(array, axis, [(0, 1), (1, 0)])  14.4 us
    all_to_all x1, starting transfers between devices, exchange(): return lax.all_to_all(array, axes, 0, 0, tiled=True)  7.58 us
    all_to_all x1, waiting for transfers between devices, exchange(): return lax.all_to_all(array, axes, 0, 0, tiled=True)  6.2 us
  transfers between devices with their start and end apart: 4, of which 3 were waited for; matrix products, arithmetic and copies ran while one was open for 1% of the time, Pallas kernels for 2%

profile of v9, /device:TPU:1, one launch (start us, length us, event | category | flops | bytes accessed | tf_op | source)
XLA Modules:
  0.0 135.0 jit_solution(17818446211089809715)
XLA Ops:
  0.7 1.6 %constant_dynamic-update-slice_fusion.15 = bf16[2048,256]{1,0:T(8,128)(2,1)} fusion(bf16[128,256]{1,0:T(8,128)(2,1)} %x_ref.1, f32[128]{0:T(128)} %param.12), kind=kLoop, calls=%fused_computation.16 | loop fusion | flops 98303 | bytes 131584
  2.3 1.5 %constant_dynamic-update-slice_fusion.14 = bf16[2048,256]{1,0:T(8,128)(2,1)} fusion(bf16[2048,256]{1,0:T(8,128)(2,1)} %constant_dynamic-update-slice_fusion.15, bf16[128,256]{1,0:T(8,128)(2,1)} %x_ref.1, f32[128]{0:T(128)} %param.12), kind=kLoop, calls=%fused_computation.15 | loop fusion | flops 98304 | bytes 131584
  3.8 1.5 %constant_dynamic-update-slice_fusion.13 = bf16[2048,256]{1,0:T(8,128)(2,1)} fusion(bf16[2048,256]{1,0:T(8,128)(2,1)} %constant_dynamic-update-slice_fusion.14, bf16[128,256]{1,0:T(8,128)(2,1)} %x_ref.1, f32[128]{0:T(128)} %param.12), kind=kLoop, calls=%fused_computation.14 | loop fusion | flops 98304 | bytes 131584
  5.4 1.5 %constant_dynamic-update-slice_fusion.12 = bf16[2048,256]{1,0:T(8,128)(2,1)} fusion(bf16[2048,256]{1,0:T(8,128)(2,1)} %constant_dynamic-update-slice_fusion.13, bf16[128,256]{1,0:T(8,128)(2,1)} %x_ref.1, f32[128]{0:T(128)} %param.12), kind=kLoop, calls=%fused_computation.13 | loop fusion | flops 98304 | bytes 131584
  6.9 1.5 %constant_dynamic-update-slice_fusion.11 = bf16[2048,256]{1,0:T(8,128)(2,1)} fusion(bf16[2048,256]{1,0:T(8,128)(2,1)} %constant_dynamic-update-slice_fusion.12, bf16[128,256]{1,0:T(8,128)(2,1)} %x_ref.1, f32[128]{0:T(128)} %param.12), kind=kLoop, calls=%fused_computation.12 | loop fusion | flops 98304 | bytes 131584
  8.5 1.6 %constant_dynamic-update-slice_fusion.10 = bf16[2048,256]{1,0:T(8,128)(2,1)} fusion(bf16[2048,256]{1,0:T(8,128)(2,1)} %constant_dynamic-update-slice_fusion.11, bf16[128,256]{1,0:T(8,128)(2,1)} %x_ref.1, f32[128]{0:T(128)} %param.12), kind=kLoop, calls=%fused_computation.11 | loop fusion | flops 98304 | bytes 131584
  10.0 1.6 %constant_dynamic-update-slice_fusion.9 = bf16[2048,256]{1,0:T(8,128)(2,1)} fusion(bf16[2048,256]{1,0:T(8,128)(2,1)} %constant_dynamic-update-slice_fusion.10, bf16[128,256]{1,0:T(8,128)(2,1)} %x_ref.1, f32[128]{0:T(128)} %param.12), kind=kLoop, calls=%fused_computation.10 | loop fusion | flops 98304 | bytes 131584
  11.6 1.5 %constant_dynamic-update-slice_fusion.8 = bf16[2048,256]{1,0:T(8,128)(2,1)} fusion(bf16[2048,256]{1,0:T(8,128)(2,1)} %constant_dynamic-update-slice_fusion.9, bf16[128,256]{1,0:T(8,128)(2,1)} %x_ref.1, f32[128]{0:T(128)} %param.12), kind=kLoop, calls=%fused_computation.9 | loop fusion | flops 98304 | bytes 131584
  13.1 1.6 %constant_dynamic-update-slice_fusion.7 = bf16[2048,256]{1,0:T(8,128)(2,1)} fusion(bf16[2048,256]{1,0:T(8,128)(2,1)} %constant_dynamic-update-slice_fusion.8, bf16[128,256]{1,0:T(8,128)(2,1)} %x_ref.1, f32[128]{0:T(128)} %param.12), kind=kLoop, calls=%fused_computation.8 | loop fusion | flops 98304 | bytes 131584
  14.7 1.6 %constant_dynamic-update-slice_fusion.6 = bf16[2048,256]{1,0:T(8,128)(2,1)} fusion(bf16[2048,256]{1,0:T(8,128)(2,1)} %constant_dynamic-update-slice_fusion.7, bf16[128,256]{1,0:T(8,128)(2,1)} %x_ref.1, f32[128]{0:T(128)} %param.12), kind=kLoop, calls=%fused_computation.7 | loop fusion | flops 98304 | bytes 131584
  16.3 1.6 %constant_dynamic-update-slice_fusion.5 = bf16[2048,256]{1,0:T(8,128)(2,1)} fusion(bf16[2048,256]{1,0:T(8,128)(2,1)} %constant_dynamic-update-slice_fusion.6, bf16[128,256]{1,0:T(8,128)(2,1)} %x_ref.1, f32[128]{0:T(128)} %param.12), kind=kLoop, calls=%fused_computation.6 | loop fusion | flops 98304 | bytes 131584
  17.8 1.6 %constant_dynamic-update-slice_fusion.4 = bf16[2048,256]{1,0:T(8,128)(2,1)} fusion(bf16[2048,256]{1,0:T(8,128)(2,1)} %constant_dynamic-update-slice_fusion.5, bf16[128,256]{1,0:T(8,128)(2,1)} %x_ref.1, f32[128]{0:T(128)} %param.12), kind=kLoop, calls=%fused_computation.5 | loop fusion | flops 98304 | bytes 131584
  19.4 0.7 constant_dynamic-update-slice_fusion.3
  20.1 0.7 constant_dynamic-update-slice_fusion.2
  20.8 0.7 constant_dynamic-update-slice_fusion.1
  21.5 0.7 constant_dynamic-update-slice_fusion
  22.3 7.6 %all-to-all-start = ((bf16[16,128,256]{2,1,0:T(8,128)(2,1)}), bf16[16,128,256]{2,1,0:T(8,128)(2,1)S(1)}, u32[]{:S(2)}, u32[]{:S(2)}) async-start(bf16[16,128,256]{2,1,0:T(8,128)(2,1)} %bitcast), calls=%async_computation | async-start | bytes 2097152 | tf_op jit(solution)/shard_map/all_to_all | solution.py:176
  30.6 7.0 %collective-permute-start = (s32[2,16,96]{2,1,0:T(8,128)S(1)}, s32[2,16,96]{2,1,0:T(8,128)S(1)}, u32[]{:S(2)}, u32[]{:S(2)}) collective-permute-start(s32[2,16,96]{2,1,0:T(8,128)S(1)} %bitcast.41), channel_id=1, source_target_pairs={{0,8},{8,0},{1,9},{9,1},{2,10},{10,2},{3,11},{11,3},{4,12},{12,4},... | collective-permute-start | bytes 36872 | tf_op jit(solution)/shard_map/ppermute | solution.py:180
  37.6 1.1 collective-permute-done
  39.2 6.2 %all-to-all-done.x_ref = bf16[16,128,256]{2,1,0:T(8,128)(2,1)S(1)} async-done(((bf16[16,128,256]{2,1,0:T(8,128)(2,1)}), bf16[16,128,256]{2,1,0:T(8,128)(2,1)S(1)}, u32[]{:S(2)}, u32[]{:S(2)}) %all-to-all-start) | async-done | bytes 1048608 | tf_op jit(solution)/shard_map/all_to_all | solution.py:176
  45.4 1.4 %shard_map.120 = (bf16[2,1536,256]{2,1,0:T(8,128)(2,1)S(1)}, bf16[2,512,256]{2,1,0:T(8,128)(2,1)S(1)}) custom-call(bf16[16,128,256]{2,1,0:T(8,128)(2,1)S(1)} %all-to-all-done.x_ref, s32[4,1536]{1,0:T(4,128)S(1)} %reshape.181.lane_ref, s32[1536,4]{1,0:T(8,128)S(1)} %bitcast.30), custom_call_target="tpu_custom_call" | custom-call | flops 1006632960 | bytes 2097152 | tf_op jit(solution)/shard_map/pallas_call | solution.py:208
  46.8 3.2 %collective-permute-start.1 = (bf16[2,512,256]{2,1,0:T(8,128)(2,1)S(1)}, bf16[2,512,256]{2,1,0:T(8,128)(2,1)S(1)}, u32[]{:S(2)}, u32[]{:S(2)}) collective-permute-start(bf16[2,512,256]{2,1,0:T(8,128)(2,1)S(1)} %get-tuple-element.17), channel_id=1, source_target_pairs={{0,1},{1,0},{2,3},{3,2},{4,5},{5,4},{6,7},{7,6},{8,9},{9,8},{10,11... | collective-permute-start | bytes 1572872 | tf_op jit(solution)/shard_map/ppermute | solution.py:180
  50.0 1.0 shard_map.121.mine_ref
  51.7 24.7 %all_to_all.25.part_ref = bf16[8,128,256]{2,1,0:T(8,128)(2,1)S(1)} all-to-all(bf16[8,128,256]{2,1,0:T(8,128)(2,1)S(1)} %bitcast.29), channel_id=1, replica_groups=mesh['x'=4,'y'=4,'h'=2,'l'=4,'c'=2] {'h','l'}, dimensions={0} | all-to-all | bytes 1048576 | tf_op jit(solution)/shard_map/all_to_all | solution.py:176
  76.4 0.7 shard_map.123
  77.1 9.8 %all_to_all.26.w_ref = bf16[16,24,256]{2,1,0:T(8,128)(2,1)S(1)} all-to-all(bf16[16,24,256]{2,1,0:T(8,128)(2,1)S(1)} %get-tuple-element.18), channel_id=1, replica_groups=mesh['x'=4,'y'=4,'h'=2,'l'=4,'c'=2] {'x','y'}, dimensions={0} | all-to-all | bytes 393216 | tf_op jit(solution)/shard_map/all_to_all | solution.py:176
  87.0 18.8 %all_to_all.27.mine_ref = bf16[8,152,256]{2,1,0:T(8,128)(2,1)S(1)} all-to-all(bf16[8,152,256]{2,1,0:T(8,128)(2,1)S(1)} %shard_map.124), channel_id=1, replica_groups=mesh['x'=4,'y'=4,'h'=2,'l'=4,'c'=2] {'h','l'}, dimensions={0} | all-to-all | bytes 1245184 | tf_op jit(solution)/shard_map/all_to_all | solution.py:176
  105.8 4.2 %collective-permute-start.2 = (bf16[8,152,256]{2,1,0:T(8,128)(2,1)S(1)}, bf16[8,152,256]{2,1,0:T(8,128)(2,1)S(1)}, u32[]{:S(2)}, u32[]{:S(2)}) collective-permute-start(bf16[8,152,256]{2,1,0:T(8,128)(2,1)S(1)} %all_to_all.27.mine_ref), channel_id=1, source_target_pairs={{0,1},{1,0},{2,3},{3,2},{4,5},{5,4},{6,7},{7,6},{8,9},{9,8},{10,11... | collective-permute-start | bytes 1867784 | tf_op jit(solution)/shard_map/ppermute | solution.py:180
  110.0 1.6 %shard_map.125 = (bf16[16,192,256]{2,1,0:T(8,128)(2,1)S(1)}, bf16[128,256]{1,0:T(8,128)(2,1)}) custom-call(bf16[8,152,256]{2,1,0:T(8,128)(2,1)S(1)} %all_to_all.27.mine_ref, s32[1536,4]{1,0:T(8,128)S(1)} %bitcast.31, bf16[128,256]{1,0:T(8,128)(2,1)S(1)} %get-tuple-element.20.act_ref), custom_call_target="tpu_custom_call" | custom-call | flops 805306368 | bytes 2097152 | tf_op jit(solution)/shard_map/pallas_call | solution.py:228
  111.6 1.4 %shard_map.126 = (bf16[16,144,256]{2,1,0:T(8,128)(2,1)S(1)}, f32[1,256]{1,0:T(1,128)S(1)}) custom-call(bf16[16,192,256]{2,1,0:T(8,128)(2,1)S(1)} %get-tuple-element.22.picked_ref, bf16[8,152,256]{2,1,0:T(8,128)(2,1)S(1)} %all_to_all.27.mine_ref, bf16[8,152,256]{2,1,0:T(8,128)(2,1)S(1)} %collective-permute-done.2.other_ref, s32[1536,4]{1,0:T(8,128)S(1)} %bitcast.32, ...), custom_call_target="tpu_custom_call" | custom-call | flops 1006632960 | bytes 2097152 | tf_op jit(solution)/shard_map/pallas_call | solution.py:234
  113.0 21.0 %all_to_all.28.part_ref = bf16[16,144,256]{2,1,0:T(8,128)(2,1)S(1)} all-to-all(bf16[16,144,256]{2,1,0:T(8,128)(2,1)S(1)} %get-tuple-element.23), channel_id=1, replica_groups=mesh['x'=4,'y'=4,'h'=2,'l'=4,'c'=2] {'x','y'}, dimensions={0} | all-to-all | bytes 2359296 | tf_op jit(solution)/shard_map/all_to_all | solution.py:176
  134.0 1.0 shard_map.127
  (42 shorter events, 1.9 us)
Async XLA Ops:
  0.6 18.8 %copy-start = (bf16[128,256]{1,0:T(8,128)(2,1)S(1)}, bf16[128,256]{1,0:T(8,128)(2,1)}, u32[]{:S(2)}) copy-start(bf16[128,256]{1,0:T(8,128)(2,1)} %x_ref.1) | copy-start | bytes 196612
  0.6 18.8 %copy-start.2 = (f32[128]{0:T(128)S(1)}, f32[128]{0:T(128)}, u32[]{:S(2)}) copy-start(f32[128]{0:T(128)} %param.12) | copy-start | bytes 1540
  13.1 16.7 %copy-start.5 = (s32[1,1,32,96]{3,2,1,0:T(8,128)S(1)}, s32[1,1,32,96]{3,2,1,0:T(8,128)}, u32[]{:S(2)}) copy-start(s32[1,1,32,96]{3,2,1,0:T(8,128)} %param.14) | copy-start | bytes 36868
  14.7 15.3 %copy-start.8 = (s32[1,1,32,4]{2,3,1,0:T(4,128)S(1)}, s32[1,1,32,4]{2,3,1,0:T(4,128)}, u32[]{:S(2)}) copy-start(s32[1,1,32,4]{2,3,1,0:T(4,128)} %param.17) | copy-start | bytes 1540
  14.7 15.7 %copy-start.6 = (s32[1,1,32,96]{3,2,1,0:T(8,128)S(1)}, s32[1,1,32,96]{3,2,1,0:T(8,128)}, u32[]{:S(2)}) copy-start(s32[1,1,32,96]{3,2,1,0:T(8,128)} %param.15) | copy-start | bytes 36868
  16.3 14.3 %copy-start.7 = (s32[1,1,32,96]{3,2,1,0:T(8,128)S(1)}, s32[1,1,32,96]{3,2,1,0:T(8,128)}, u32[]{:S(2)}) copy-start(s32[1,1,32,96]{3,2,1,0:T(8,128)} %param.16) | copy-start | bytes 36868
  22.3 23.1 %all-to-all-start = ((bf16[16,128,256]{2,1,0:T(8,128)(2,1)}), bf16[16,128,256]{2,1,0:T(8,128)(2,1)S(1)}, u32[]{:S(2)}, u32[]{:S(2)}) async-start(bf16[16,128,256]{2,1,0:T(8,128)(2,1)} %bitcast), calls=%async_computation | async-start | bytes 2097152 | tf_op jit(solution)/shard_map/all_to_all | solution.py:176
  30.6 8.1 %collective-permute-start = (s32[2,16,96]{2,1,0:T(8,128)S(1)}, s32[2,16,96]{2,1,0:T(8,128)S(1)}, u32[]{:S(2)}, u32[]{:S(2)}) collective-permute-start(s32[2,16,96]{2,1,0:T(8,128)S(1)} %bitcast.41), channel_id=1, source_target_pairs={{0,8},{8,0},{1,9},{9,1},{2,10},{10,2},{3,11},{11,3},{4,12},{12,4},... | collective-permute-start | bytes 36872 | tf_op jit(solution)/shard_map/ppermute | solution.py:180
  46.8 4.8 %collective-permute-start.1 = (bf16[2,512,256]{2,1,0:T(8,128)(2,1)S(1)}, bf16[2,512,256]{2,1,0:T(8,128)(2,1)S(1)}, u32[]{:S(2)}, u32[]{:S(2)}) collective-permute-start(bf16[2,512,256]{2,1,0:T(8,128)(2,1)S(1)} %get-tuple-element.17), channel_id=1, source_target_pairs={{0,1},{1,0},{2,3},{3,2},{4,5},{5,4},{6,7},{7,6},{8,9},{9,8},{10,11... | collective-permute-start | bytes 1572872 | tf_op jit(solution)/shard_map/ppermute | solution.py:180
  51.0 25.3 %copy-start.1 = (bf16[256,256]{1,0:T(8,128)(2,1)S(1)}, bf16[256,256]{1,0:T(8,128)(2,1)}, u32[]{:S(2)}) copy-start(bf16[256,256]{1,0:T(8,128)(2,1)} %w_ref.3) | copy-start | bytes 393220
  51.0 25.3 %copy-start.3 = (bf16[128,256]{1,0:T(8,128)(2,1)S(1)}, bf16[128,256]{1,0:T(8,128)(2,1)}, u32[]{:S(2)}) copy-start(bf16[128,256]{1,0:T(8,128)(2,1)} %ct_ref.1) | copy-start | bytes 196612
  51.0 25.3 %copy-start.4 = (f32[256]{0:T(256)S(1)}, f32[256]{0:T(256)}, u32[]{:S(2)}) copy-start(f32[256]{0:T(256)} %param.11) | copy-start | bytes 3076
  105.8 5.8 %collective-permute-start.2 = (bf16[8,152,256]{2,1,0:T(8,128)(2,1)S(1)}, bf16[8,152,256]{2,1,0:T(8,128)(2,1)S(1)}, u32[]{:S(2)}, u32[]{:S(2)}) collective-permute-start(bf16[8,152,256]{2,1,0:T(8,128)(2,1)S(1)} %all_to_all.27.mine_ref), channel_id=1, source_target_pairs={{0,1},{1,0},{2,3},{3,2},{4,5},{5,4},{6,7},{7,6},{8,9},{9,8},{10,11... | collective-permute-start | bytes 1867784 | tf_op jit(solution)/shard_map/ppermute | solution.py:180

commit v10 on v8

--- a/solution.py
+++ b/solution.py
@@ -142,8 +142,11 @@
         pay_ref[k, pl.ds(TILE + WR, BB), :] = bias_rows
 
 
-def backward_mine_kernel(mine_ref, sub_ref, act_ref, picked_ref, out_ref, grads):
-    out_ref[...] = act_ref[...]
+def backward_mine_kernel(mine_ref, sub_ref, col_ref, picked_ref, place_ref, tail_ref, grads):
+    tail = jnp.zeros((WR + BB, F), F32)
+    for k in range(ZN):
+        tail += mine_ref[k, pl.ds(TILE, WR + BB), :].astype(F32)
+    tail_ref[...] = tail
     for b in range(H):
         for k in range(L):
             grads[pl.ds(k * TILE, TILE), :] = mine_ref[b * L + k, pl.ds(0, TILE), :]
@@ -154,19 +157,18 @@
                 picked_ref[m * (STEP // EDGES) + q, pl.ds(b * EDGES, EDGES), :] = value[
                     q * EDGES : (q + 1) * EDGES
                 ]
+    for j in range(XY):
+        place_ref[j] = one_hot(col_ref[j : j + 1, :], (TILE, H * EDGES), 0)
 
 
 def backward_kernel(
-    picked_ref, mine_ref, other_ref, sub_ref, col_ref, pay_ref, bias_ref, grads, picked
+    picked_ref, tail_ref, other_ref, sub_ref, place_ref, pay_ref, bias_ref, grads, picked
 ):
     factor = 1.0 / math.sqrt(XY * ZN * C * TILE)
-    tail_mine = jnp.zeros((WR + BB, F), F32)
     tail_other = jnp.zeros((WR + BB, F), F32)
     for k in range(ZN):
-        rows = pl.ds(TILE, WR + BB)
-        tail_mine += mine_ref[k, rows, :].astype(F32)
-        tail_other += other_ref[k, rows, :].astype(F32)
-    tail = (tail_mine + tail_other) * factor
+        tail_other += other_ref[k, pl.ds(TILE, WR + BB), :].astype(F32)
+    tail = (tail_ref[...] + tail_other) * factor
     own = tail[:WR].astype(BF16)
     bias_ref[...] = jnp.sum(tail[WR:], axis=0, keepdims=True)
     for b in range(H):
@@ -180,14 +182,16 @@
                 both = value[q * EDGES : (q + 1) * EDGES] + picked_ref[j, rows, :].astype(F32)
                 picked[j, rows, :] = both.astype(BF16)
     for j in range(XY):
-        place = one_hot(col_ref[j : j + 1, :], (TILE, H * EDGES), 0)
-        total = dot(place, picked[j])
+        total = dot(place_ref[j], picked[j])
         pay_ref[j, pl.ds(0, TILE), :] = total.astype(BF16)
         pay_ref[j, pl.ds(TILE, WR), :] = own
 
 
-def final_kernel(part_ref, g_ref, s_ref, w_ref, bias_ref, fg_ref, wg_ref, out_ref):
-    out_ref[...] = bias_ref[...]
+def final_kernel(
+    part_ref, g_ref, s_ref, w_ref, bias_in, act_ref, fg_ref, wg_ref, bias_ref, out_ref
+):
+    bias_ref[...] = bias_in[...]
+    out_ref[...] = act_ref[...]
     back = g_ref[...].astype(F32)
     for k in range(XY):
         back += part_ref[k, pl.ds(0, TILE), :].astype(F32)
@@ -262,22 +266,22 @@
     (pay,) = call(load_kernel, [((ZN, ZCHUNK, F), BF16)])(w_parts, g)
     around = exchange(pay, ("h", "l"))
     other = swap(around, "c")
-    picked, output = call(
+    picked, places, tail = call(
         backward_mine_kernel,
-        [((XY, H * EDGES, F), BF16), ((TILE, F), BF16)],
+        [((XY, H * EDGES, F), BF16), ((XY, TILE, H * EDGES), BF16), ((WR + BB, F), F32)],
         [((HALF, F), BF16)],
         flops=4 * E_ALL * F * HALF,
-    )(around, sub, act)
+    )(around, sub, columns)
     terms, bias_sum = call(
         backward_kernel,
         [((XY, XCHUNK, F), BF16), ((1, F), F32)],
         [((HALF, F), BF16), ((XY, H * EDGES, F), BF16)],
         flops=4 * E_ALL * F * (HALF + TILE),
-    )(picked, around, other, sub, columns)
+    )(picked, tail, other, sub, places)
     terms = exchange(terms, ("x", "y"))
-    feature_grad, weight_grad, bias_grad = call(
-        final_kernel, [((TILE, F), BF16), ((F, F), F32), ((1, F), F32)]
-    )(terms, g, s, weight, bias_sum)
+    feature_grad, weight_grad, bias_grad, output = call(
+        final_kernel, [((TILE, F), BF16), ((F, F), F32), ((1, F), F32), ((TILE, F), BF16)]
+    )(terms, g, s, weight, bias_sum, act)
     return output, feature_grad, weight_grad, bias_grad.reshape(F)
 
 

time: 116 us -> 116 us (level)
  transfers between devices with their start and end apart: 4 -> 4, of which waited for: 3 -> 4; matrix products, arithmetic and copies ran while one was open for 1% -> 1% of each run, Pallas kernels for 2% -> 2%
where the time goes in v10:
time: 116 us
  blocking collectives  74.3 us (64%)
  starting transfers between devices  22 us (19%)
  Pallas kernels  9 us (8%)
  waiting for transfers between devices  8.14 us (7%)
    all_to_all x4, blocking collectives, exchange(): return lax.all_to_all(array, axes, 0, 0, tiled=True)  74.3 us
    ppermute x3, starting transfers between devices, swap(): return lax.ppermute(array, axis, [(0, 1), (1, 0)])  14.4 us
    all_to_all x1, starting transfers between devices, exchange(): return lax.all_to_all(array, axes, 0, 0, tiled=True)  7.6 us
    all_to_all x1, waiting for transfers between devices, exchange(): return lax.all_to_all(array, axes, 0, 0, tiled=True)  6.2 us
  transfers between devices with their start and end apart: 4, of which 4 were waited for; matrix products, arithmetic and copies ran while one was open for 1% of the time, Pallas kernels for 2%

profile of v10, /device:TPU:1, one launch (start us, length us, event | category | flops | bytes accessed | tf_op | source)
XLA Modules:
  0.0 115.5 jit_solution(2490890315838570063)
XLA Ops:
  0.7 2.1 %shard_map.120 = bf16[16,128,256]{2,1,0:T(8,128)(2,1)} custom-call(bf16[128,256]{1,0:T(8,128)(2,1)} %x_ref.3, f32[1,128]{1,0:T(1,128)} %bitcast.32), custom_call_target="tpu_custom_call" | custom-call | tf_op jit(solution)/shard_map/pallas_call | solution.py:68
  2.7 7.6 %all-to-all-start = ((bf16[16,128,256]{2,1,0:T(8,128)(2,1)}), bf16[16,128,256]{2,1,0:T(8,128)(2,1)S(1)}, u32[]{:S(2)}, u32[]{:S(2)}) async-start(bf16[16,128,256]{2,1,0:T(8,128)(2,1)} %shard_map.120), calls=%async_computation | async-start | bytes 2097152 | tf_op jit(solution)/shard_map/all_to_all | solution.py:219
  10.4 0.1 broadcast_in_dim.47
  10.5 0.1 broadcast_in_dim.53
  10.5 0.1 broadcast_in_dim.51
  10.6 0.1 broadcast_in_dim.49
  10.7 0.0 copy-done.5
  10.9 0.1 add_select_fusion
  11.0 0.1 fusion.1
  11.1 7.0 %collective-permute-start = (s32[2,16,96]{2,1,0:T(8,128)S(1)}, s32[2,16,96]{2,1,0:T(8,128)S(1)}, u32[]{:S(2)}, u32[]{:S(2)}) collective-permute-start(s32[2,16,96]{2,1,0:T(8,128)S(1)} %bitcast.41), channel_id=1, source_target_pairs={{0,8},{8,0},{1,9},{9,1},{2,10},{10,2},{3,11},{11,3},{4,12},{12,4},... | collective-permute-start | bytes 36872 | tf_op jit(solution)/shard_map/ppermute | solution.py:223
  18.1 1.1 collective-permute-done
  19.3 0.1 reshape.176.lane_ref
  19.4 0.3 copy.28
  19.7 6.2 %all-to-all-done.x_ref = bf16[16,128,256]{2,1,0:T(8,128)(2,1)S(1)} async-done(((bf16[16,128,256]{2,1,0:T(8,128)(2,1)}), bf16[16,128,256]{2,1,0:T(8,128)(2,1)S(1)}, u32[]{:S(2)}, u32[]{:S(2)}) %all-to-all-start) | async-done | bytes 1048608 | tf_op jit(solution)/shard_map/all_to_all | solution.py:219
  25.9 1.4 %shard_map.121 = (bf16[2,1536,256]{2,1,0:T(8,128)(2,1)S(1)}, bf16[2,512,256]{2,1,0:T(8,128)(2,1)S(1)}) custom-call(bf16[16,128,256]{2,1,0:T(8,128)(2,1)S(1)} %all-to-all-done.x_ref, s32[4,1536]{1,0:T(4,128)S(1)} %reshape.176.lane_ref, s32[1536,4]{1,0:T(8,128)S(1)} %bitcast.28), custom_call_target="tpu_custom_call" | custom-call | flops 1006632960 | bytes 2097152 | tf_op jit(solution)/shard_map/pallas_call | solution.py:249
  27.3 3.2 %collective-permute-start.1 = (bf16[2,512,256]{2,1,0:T(8,128)(2,1)S(1)}, bf16[2,512,256]{2,1,0:T(8,128)(2,1)S(1)}, u32[]{:S(2)}, u32[]{:S(2)}) collective-permute-start(bf16[2,512,256]{2,1,0:T(8,128)(2,1)S(1)} %get-tuple-element.19), channel_id=1, source_target_pairs={{0,1},{1,0},{2,3},{3,2},{4,5},{5,4},{6,7},{7,6},{8,9},{9,8},{10,11... | collective-permute-start | bytes 1572872 | tf_op jit(solution)/shard_map/ppermute | solution.py:223
  30.5 1.0 shard_map.122.mine_ref
  31.5 0.0 copy-start
  31.6 0.5 collective-permute-done.1.other_ref
  32.1 0.1 shard_map.123
  32.2 24.7 %all_to_all.25.part_ref = bf16[8,128,256]{2,1,0:T(8,128)(2,1)S(1)} all-to-all(bf16[8,128,256]{2,1,0:T(8,128)(2,1)S(1)} %bitcast.31), channel_id=1, replica_groups=mesh['x'=4,'y'=4,'h'=2,'l'=4,'c'=2] {'h','l'}, dimensions={0} | all-to-all | bytes 1048576 | tf_op jit(solution)/shard_map/all_to_all | solution.py:219
  56.9 0.7 shard_map.124
  57.6 9.8 %all_to_all.26.w_ref = bf16[16,24,256]{2,1,0:T(8,128)(2,1)S(1)} all-to-all(bf16[16,24,256]{2,1,0:T(8,128)(2,1)S(1)} %get-tuple-element.20), channel_id=1, replica_groups=mesh['x'=4,'y'=4,'h'=2,'l'=4,'c'=2] {'x','y'}, dimensions={0} | all-to-all | bytes 393216 | tf_op jit(solution)/shard_map/all_to_all | solution.py:219
  67.5 0.1 shard_map.125
  67.5 18.8 %all_to_all.27.mine_ref = bf16[8,152,256]{2,1,0:T(8,128)(2,1)S(1)} all-to-all(bf16[8,152,256]{2,1,0:T(8,128)(2,1)S(1)} %shard_map.125), channel_id=1, replica_groups=mesh['x'=4,'y'=4,'h'=2,'l'=4,'c'=2] {'h','l'}, dimensions={0} | all-to-all | bytes 1245184 | tf_op jit(solution)/shard_map/all_to_all | solution.py:219
  86.3 4.2 %collective-permute-start.2 = (bf16[8,152,256]{2,1,0:T(8,128)(2,1)S(1)}, bf16[8,152,256]{2,1,0:T(8,128)(2,1)S(1)}, u32[]{:S(2)}, u32[]{:S(2)}) collective-permute-start(bf16[8,152,256]{2,1,0:T(8,128)(2,1)S(1)} %all_to_all.27.mine_ref), channel_id=1, source_target_pairs={{0,1},{1,0},{2,3},{3,2},{4,5},{5,4},{6,7},{7,6},{8,9},{9,8},{10,11... | collective-permute-start | bytes 1867784 | tf_op jit(solution)/shard_map/ppermute | solution.py:223
  90.5 0.1 pad_add_fusion.1.col_ref
  90.6 1.3 %shard_map.126 = (bf16[16,192,256]{2,1,0:T(8,128)(2,1)S(1)}, bf16[16,128,192]{2,1,0:T(8,128)(2,1)S(1)}, f32[24,256]{1,0:T(8,128)S(1)}) custom-call(bf16[8,152,256]{2,1,0:T(8,128)(2,1)S(1)} %all_to_all.27.mine_ref, s32[1536,4]{1,0:T(8,128)S(1)} %bitcast.29, s32[16,192]{1,0:T(8,128)S(1)} %pad_add_fusion.1.col_ref), custom_call_target="tpu_custom_call" | custom-call | flops 805306368 | bytes 2097152 | tf_op jit(solution)/shard_map/pallas_call | solution.py:269
  91.8 0.3 collective-permute-done.2.other_ref
  92.2 1.4 %shard_map.127 = (bf16[16,144,256]{2,1,0:T(8,128)(2,1)S(1)}, f32[1,256]{1,0:T(1,128)S(1)}) custom-call(bf16[16,192,256]{2,1,0:T(8,128)(2,1)S(1)} %get-tuple-element.22.picked_ref, f32[24,256]{1,0:T(8,128)S(1)} %get-tuple-element.23.tail_ref, bf16[8,152,256]{2,1,0:T(8,128)(2,1)S(1)} %collective-permute-done.2.other_ref, s32[1536,4]{1,0:T(8,128)S(1)} %bitcast.30, ...), custom_call_target="tpu_custom_call" | custom-call | flops 1006632960 | bytes 2097152 | tf_op jit(solution)/shard_map/pallas_call | solution.py:275
  93.5 21.0 %all_to_all.28.part_ref = bf16[16,144,256]{2,1,0:T(8,128)(2,1)S(1)} all-to-all(bf16[16,144,256]{2,1,0:T(8,128)(2,1)S(1)} %get-tuple-element.25), channel_id=1, replica_groups=mesh['x'=4,'y'=4,'h'=2,'l'=4,'c'=2] {'x','y'}, dimensions={0} | all-to-all | bytes 2359296 | tf_op jit(solution)/shard_map/all_to_all | solution.py:219
  114.5 1.0 shard_map.128
  (27 shorter events, 0.2 us)
Async XLA Ops:
  0.6 9.7 %copy-start.8 = (s32[1,1,32,4]{2,3,1,0:T(4,128)S(1)}, s32[1,1,32,4]{2,3,1,0:T(4,128)}, u32[]{:S(2)}) copy-start(s32[1,1,32,4]{2,3,1,0:T(4,128)} %param.17) | copy-start | bytes 1540
  0.6 10.1 %copy-start.5 = (s32[1,1,32,96]{3,2,1,0:T(8,128)S(1)}, s32[1,1,32,96]{3,2,1,0:T(8,128)}, u32[]{:S(2)}) copy-start(s32[1,1,32,96]{3,2,1,0:T(8,128)} %param.14) | copy-start | bytes 36868
  0.7 10.2 %copy-start.6 = (s32[1,1,32,96]{3,2,1,0:T(8,128)S(1)}, s32[1,1,32,96]{3,2,1,0:T(8,128)}, u32[]{:S(2)}) copy-start(s32[1,1,32,96]{3,2,1,0:T(8,128)} %param.15) | copy-start | bytes 36868
  0.7 10.4 %copy-start.7 = (s32[1,1,32,96]{3,2,1,0:T(8,128)S(1)}, s32[1,1,32,96]{3,2,1,0:T(8,128)}, u32[]{:S(2)}) copy-start(s32[1,1,32,96]{3,2,1,0:T(8,128)} %param.16) | copy-start | bytes 36868
  2.7 23.1 %all-to-all-start = ((bf16[16,128,256]{2,1,0:T(8,128)(2,1)}), bf16[16,128,256]{2,1,0:T(8,128)(2,1)S(1)}, u32[]{:S(2)}, u32[]{:S(2)}) async-start(bf16[16,128,256]{2,1,0:T(8,128)(2,1)} %shard_map.120), calls=%async_computation | async-start | bytes 2097152 | tf_op jit(solution)/shard_map/all_to_all | solution.py:219
  11.1 8.1 %collective-permute-start = (s32[2,16,96]{2,1,0:T(8,128)S(1)}, s32[2,16,96]{2,1,0:T(8,128)S(1)}, u32[]{:S(2)}, u32[]{:S(2)}) collective-permute-start(s32[2,16,96]{2,1,0:T(8,128)S(1)} %bitcast.41), channel_id=1, source_target_pairs={{0,8},{8,0},{1,9},{9,1},{2,10},{10,2},{3,11},{11,3},{4,12},{12,4},... | collective-permute-start | bytes 36872 | tf_op jit(solution)/shard_map/ppermute | solution.py:223
  27.3 4.8 %collective-permute-start.1 = (bf16[2,512,256]{2,1,0:T(8,128)(2,1)S(1)}, bf16[2,512,256]{2,1,0:T(8,128)(2,1)S(1)}, u32[]{:S(2)}, u32[]{:S(2)}) collective-permute-start(bf16[2,512,256]{2,1,0:T(8,128)(2,1)S(1)} %get-tuple-element.19), channel_id=1, source_target_pairs={{0,1},{1,0},{2,3},{3,2},{4,5},{5,4},{6,7},{7,6},{8,9},{9,8},{10,11... | collective-permute-start | bytes 1572872 | tf_op jit(solution)/shard_map/ppermute | solution.py:223
  31.5 25.4 %copy-start = (bf16[256,256]{1,0:T(8,128)(2,1)S(1)}, bf16[256,256]{1,0:T(8,128)(2,1)}, u32[]{:S(2)}) copy-start(bf16[256,256]{1,0:T(8,128)(2,1)} %w_ref.3) | copy-start | bytes 393220
  31.5 25.4 %copy-start.1 = (bf16[128,256]{1,0:T(8,128)(2,1)S(1)}, bf16[128,256]{1,0:T(8,128)(2,1)}, u32[]{:S(2)}) copy-start(bf16[128,256]{1,0:T(8,128)(2,1)} %x_ref.3) | copy-start | bytes 196612
  31.5 25.3 %copy-start.2 = (bf16[128,256]{1,0:T(8,128)(2,1)S(1)}, bf16[128,256]{1,0:T(8,128)(2,1)}, u32[]{:S(2)}) copy-start(bf16[128,256]{1,0:T(8,128)(2,1)} %ct_ref.1) | copy-start | bytes 196612
  31.6 25.3 %copy-start.3 = (f32[128]{0:T(128)S(1)}, f32[128]{0:T(128)}, u32[]{:S(2)}) copy-start(f32[128]{0:T(128)} %param.12) | copy-start | bytes 1540
  31.6 25.3 %copy-start.4 = (f32[256]{0:T(256)S(1)}, f32[256]{0:T(256)}, u32[]{:S(2)}) copy-start(f32[256]{0:T(256)} %param.11) | copy-start | bytes 3076
  86.3 5.8 %collective-permute-start.2 = (bf16[8,152,256]{2,1,0:T(8,128)(2,1)S(1)}, bf16[8,152,256]{2,1,0:T(8,128)(2,1)S(1)}, u32[]{:S(2)}, u32[]{:S(2)}) collective-permute-start(bf16[8,152,256]{2,1,0:T(8,128)(2,1)S(1)} %all_to_all.27.mine_ref), channel_id=1, source_target_pairs={{0,1},{1,0},{2,3},{3,2},{4,5},{5,4},{6,7},{7,6},{8,9},{9,8},{10,11... | collective-permute-start | bytes 1867784 | tf_op jit(solution)/shard_map/ppermute | solution.py:223

commit v11 on v8

--- a/solution.py
+++ b/solution.py
@@ -101,7 +101,11 @@
 
 
 def add_kernel(mine_ref, other_ref, out_ref):
-    out_ref[...] = (mine_ref[...] + other_ref[...].astype(F32)).astype(BF16)
+    for b in range(H):
+        for k in range(L):
+            rows = pl.ds(k * TILE, TILE)
+            total = mine_ref[b, rows, :] + other_ref[b, rows, :].astype(F32)
+            out_ref[k * H + b] = total.astype(BF16)
 
 
 def middle_kernel(part_ref, x_ref, s_ref, w_ref, bias_ref, ct_ref, out_ref, g_ref, wp_ref):
@@ -146,7 +150,7 @@
     out_ref[...] = act_ref[...]
     for b in range(H):
         for k in range(L):
-            grads[pl.ds(k * TILE, TILE), :] = mine_ref[b * L + k, pl.ds(0, TILE), :]
+            grads[pl.ds(k * TILE, TILE), :] = mine_ref[k * H + b, pl.ds(0, TILE), :]
         for m in range(E_ALL // STEP):
             pick = one_hot(sub_ref[pl.ds(m * STEP, STEP), b : b + 1], (STEP, HALF), 1)
             value = dot(pick, grads[...]).astype(BF16)
@@ -171,7 +175,7 @@
     bias_ref[...] = jnp.sum(tail[WR:], axis=0, keepdims=True)
     for b in range(H):
         for k in range(L):
-            grads[pl.ds(k * TILE, TILE), :] = other_ref[b * L + k, pl.ds(0, TILE), :]
+            grads[pl.ds(k * TILE, TILE), :] = other_ref[k * H + b, pl.ds(0, TILE), :]
         for m in range(E_ALL // STEP):
             pick = one_hot(sub_ref[pl.ds(m * STEP, STEP), b : b + 1], (STEP, HALF), 1, HALF)
             value = dot(pick, grads[...])
@@ -251,16 +255,15 @@
     (mine,) = call(
         forward_keep_kernel, [((H, HALF, F), F32)], flops=4 * E_ALL * F * HALF
     )(gathered, lane)
-    (partial,) = call(add_kernel, [((H, HALF, F), BF16)])(mine, other)
-    partial = partial.reshape(ZN, TILE, F)
-    partial = exchange(partial, ("h", "l"))
+    (partial,) = call(add_kernel, [((ZN, TILE, F), BF16)])(mine, other)
+    partial = exchange(partial, ("l", "h"))
     act, g, w_parts = call(
         middle_kernel,
         [((TILE, F), BF16), ((TILE, F), BF16), ((XY, WR + BB, F), BF16)],
     )(partial, features, s, weight, bias, cotangent)
     w_parts = exchange(w_parts, ("x", "y"))
     (pay,) = call(load_kernel, [((ZN, ZCHUNK, F), BF16)])(w_parts, g)
-    around = exchange(pay, ("h", "l"))
+    around = exchange(pay, ("l", "h"))
     other = swap(around, "c")
     picked, output = call(
         backward_mine_kernel,

time: 116 us -> 115 us (level)
  blocking collectives: 74.3 us -> 72.3 us
    all_to_all x4, blocking collectives: 74.3 us -> 72.3 us  [exchange(): return lax.all_to_all(array, axes, 0, 0, tiled=True)]
where the time goes in v11:
time: 115 us; the launch traced here: 114 us
  blocking collectives  72.3 us (63%)
  starting transfers between devices  22.3 us (19%)
  Pallas kernels  9.38 us (8%)
  waiting for transfers between devices  7.83 us (7%)
    all_to_all x4, blocking collectives, exchange(): return lax.all_to_all(array, axes, 0, 0, tiled=True)  72.3 us
    ppermute x3, starting transfers between devices, swap(): return lax.ppermute(array, axis, [(0, 1), (1, 0)])  14.8 us
    all_to_all x1, starting transfers between devices, exchange(): return lax.all_to_all(array, axes, 0, 0, tiled=True)  7.6 us
    all_to_all x1, waiting for transfers between devices, exchange(): return lax.all_to_all(array, axes, 0, 0, tiled=True)  6.2 us
  transfers between devices with their start and end apart: 4, of which 3 were waited for; matrix products, arithmetic and copies ran while one was open for 1% of the time, Pallas kernels for 2%

profile of v11, /device:TPU:1, one launch (start us, length us, event | category | flops | bytes accessed | tf_op | source)
XLA Modules:
  0.0 114.0 jit_solution(11574499652395552804)
XLA Ops:
  0.7 2.1 %shard_map.120 = bf16[16,128,256]{2,1,0:T(8,128)(2,1)} custom-call(bf16[128,256]{1,0:T(8,128)(2,1)} %x_ref.3, f32[1,128]{1,0:T(1,128)} %bitcast.30), custom_call_target="tpu_custom_call" | custom-call | tf_op jit(solution)/shard_map/pallas_call | solution.py:68
  2.7 7.6 %all-to-all-start = ((bf16[16,128,256]{2,1,0:T(8,128)(2,1)}), bf16[16,128,256]{2,1,0:T(8,128)(2,1)S(1)}, u32[]{:S(2)}, u32[]{:S(2)}) async-start(bf16[16,128,256]{2,1,0:T(8,128)(2,1)} %shard_map.120), calls=%async_computation | async-start | bytes 2097152 | tf_op jit(solution)/shard_map/all_to_all | solution.py:219
  10.5 0.1 broadcast_in_dim.53
  10.6 0.1 broadcast_in_dim.51
  10.7 0.1 broadcast_in_dim.49
  10.8 0.1 broadcast_in_dim.47
  10.9 0.0 copy-done.6
  10.9 0.1 add_select_fusion
  11.0 0.1 fusion.1
  11.1 7.0 %collective-permute-start = (s32[2,16,96]{2,1,0:T(8,128)S(1)}, s32[2,16,96]{2,1,0:T(8,128)S(1)}, u32[]{:S(2)}, u32[]{:S(2)}) collective-permute-start(s32[2,16,96]{2,1,0:T(8,128)S(1)} %bitcast.39), channel_id=1, source_target_pairs={{0,8},{8,0},{1,9},{9,1},{2,10},{10,2},{3,11},{11,3},{4,12},{12,4},... | collective-permute-start | bytes 36872 | tf_op jit(solution)/shard_map/ppermute | solution.py:223
  18.1 1.1 collective-permute-done
  19.3 0.1 reshape.173.lane_ref
  19.4 0.3 copy.27
  19.7 6.2 %all-to-all-done.x_ref = bf16[16,128,256]{2,1,0:T(8,128)(2,1)S(1)} async-done(((bf16[16,128,256]{2,1,0:T(8,128)(2,1)}), bf16[16,128,256]{2,1,0:T(8,128)(2,1)S(1)}, u32[]{:S(2)}, u32[]{:S(2)}) %all-to-all-start) | async-done | bytes 1048608 | tf_op jit(solution)/shard_map/all_to_all | solution.py:219
  25.9 1.4 %shard_map.121 = (bf16[2,1536,256]{2,1,0:T(8,128)(2,1)S(1)}, bf16[2,512,256]{2,1,0:T(8,128)(2,1)S(1)}) custom-call(bf16[16,128,256]{2,1,0:T(8,128)(2,1)S(1)} %all-to-all-done.x_ref, s32[4,1536]{1,0:T(4,128)S(1)} %reshape.173.lane_ref, s32[1536,4]{1,0:T(8,128)S(1)} %bitcast.27), custom_call_target="tpu_custom_call" | custom-call | flops 1006632960 | bytes 2097152 | tf_op jit(solution)/shard_map/pallas_call | solution.py:249
  27.3 3.2 %collective-permute-start.1 = (bf16[2,512,256]{2,1,0:T(8,128)(2,1)S(1)}, bf16[2,512,256]{2,1,0:T(8,128)(2,1)S(1)}, u32[]{:S(2)}, u32[]{:S(2)}) collective-permute-start(bf16[2,512,256]{2,1,0:T(8,128)(2,1)S(1)} %get-tuple-element.17), channel_id=1, source_target_pairs={{0,1},{1,0},{2,3},{3,2},{4,5},{5,4},{6,7},{7,6},{8,9},{9,8},{10,11... | collective-permute-start | bytes 1572872 | tf_op jit(solution)/shard_map/ppermute | solution.py:223
  30.5 1.0 shard_map.122.mine_ref
  31.5 0.0 copy-start.2
  31.6 0.0 copy-start.3
  31.6 0.5 collective-permute-done.1.other_ref
  32.1 0.1 shard_map.123
  32.2 19.8 %all_to_all.25.part_ref = bf16[8,128,256]{2,1,0:T(8,128)(2,1)S(1)} all-to-all(bf16[8,128,256]{2,1,0:T(8,128)(2,1)S(1)} %shard_map.123), channel_id=1, replica_groups=mesh['x'=4,'y'=4,'h'=2,'l'=4,'c'=2] {'l','h'}, dimensions={0} | all-to-all | bytes 1048576 | tf_op jit(solution)/shard_map/all_to_all | solution.py:219
  52.0 0.7 shard_map.124
  52.7 9.7 %all_to_all.26.w_ref = bf16[16,24,256]{2,1,0:T(8,128)(2,1)S(1)} all-to-all(bf16[16,24,256]{2,1,0:T(8,128)(2,1)S(1)} %get-tuple-element.18), channel_id=1, replica_groups=mesh['x'=4,'y'=4,'h'=2,'l'=4,'c'=2] {'x','y'}, dimensions={0} | all-to-all | bytes 393216 | tf_op jit(solution)/shard_map/all_to_all | solution.py:219
  62.5 0.1 shard_map.125
  62.5 22.0 %all_to_all.27.mine_ref = bf16[8,152,256]{2,1,0:T(8,128)(2,1)S(1)} all-to-all(bf16[8,152,256]{2,1,0:T(8,128)(2,1)S(1)} %shard_map.125), channel_id=1, replica_groups=mesh['x'=4,'y'=4,'h'=2,'l'=4,'c'=2] {'l','h'}, dimensions={0} | all-to-all | bytes 1245184 | tf_op jit(solution)/shard_map/all_to_all | solution.py:219
  84.5 4.5 %collective-permute-start.2 = (bf16[8,152,256]{2,1,0:T(8,128)(2,1)S(1)}, bf16[8,152,256]{2,1,0:T(8,128)(2,1)S(1)}, u32[]{:S(2)}, u32[]{:S(2)}) collective-permute-start(bf16[8,152,256]{2,1,0:T(8,128)(2,1)S(1)} %all_to_all.27.mine_ref), channel_id=1, source_target_pairs={{0,1},{1,0},{2,3},{3,2},{4,5},{5,4},{6,7},{7,6},{8,9},{9,8},{10,11... | collective-permute-start | bytes 1867784 | tf_op jit(solution)/shard_map/ppermute | solution.py:223
  89.0 0.1 pad_add_fusion.1.col_ref
  89.1 1.6 %shard_map.126 = (bf16[16,192,256]{2,1,0:T(8,128)(2,1)S(1)}, bf16[128,256]{1,0:T(8,128)(2,1)}) custom-call(bf16[8,152,256]{2,1,0:T(8,128)(2,1)S(1)} %all_to_all.27.mine_ref, s32[1536,4]{1,0:T(8,128)S(1)} %bitcast.28, bf16[128,256]{1,0:T(8,128)(2,1)S(1)} %get-tuple-element.20.act_ref), custom_call_target="tpu_custom_call" | custom-call | flops 805306368 | bytes 2097152 | tf_op jit(solution)/shard_map/pallas_call | solution.py:268
  90.7 1.4 %shard_map.127 = (bf16[16,144,256]{2,1,0:T(8,128)(2,1)S(1)}, f32[1,256]{1,0:T(1,128)S(1)}) custom-call(bf16[16,192,256]{2,1,0:T(8,128)(2,1)S(1)} %get-tuple-element.22.picked_ref, bf16[8,152,256]{2,1,0:T(8,128)(2,1)S(1)} %all_to_all.27.mine_ref, bf16[8,152,256]{2,1,0:T(8,128)(2,1)S(1)} %collective-permute-done.2.other_ref, s32[1536,4]{1,0:T(8,128)S(1)} %bitcast.29, ...), custom_call_target="tpu_custom_call" | custom-call | flops 1006632960 | bytes 2097152 | tf_op jit(solution)/shard_map/pallas_call | solution.py:274
  92.1 20.9 %all_to_all.28.part_ref = bf16[16,144,256]{2,1,0:T(8,128)(2,1)S(1)} all-to-all(bf16[16,144,256]{2,1,0:T(8,128)(2,1)S(1)} %get-tuple-element.23), channel_id=1, replica_groups=mesh['x'=4,'y'=4,'h'=2,'l'=4,'c'=2] {'x','y'}, dimensions={0} | all-to-all | bytes 2359296 | tf_op jit(solution)/shard_map/all_to_all | solution.py:219
  113.0 1.0 shard_map.128
  (27 shorter events, 0.2 us)
Async XLA Ops:
  0.6 9.7 %copy-start.5 = (s32[1,1,32,96]{3,2,1,0:T(8,128)S(1)}, s32[1,1,32,96]{3,2,1,0:T(8,128)}, u32[]{:S(2)}) copy-start(s32[1,1,32,96]{3,2,1,0:T(8,128)} %param.14) | copy-start | bytes 36868
  0.6 9.8 %copy-start.8 = (s32[1,1,32,4]{2,3,1,0:T(4,128)S(1)}, s32[1,1,32,4]{2,3,1,0:T(4,128)}, u32[]{:S(2)}) copy-start(s32[1,1,32,4]{2,3,1,0:T(4,128)} %param.17) | copy-start | bytes 1540
  0.7 10.2 %copy-start.6 = (s32[1,1,32,96]{3,2,1,0:T(8,128)S(1)}, s32[1,1,32,96]{3,2,1,0:T(8,128)}, u32[]{:S(2)}) copy-start(s32[1,1,32,96]{3,2,1,0:T(8,128)} %param.15) | copy-start | bytes 36868
  0.7 10.4 %copy-start.7 = (s32[1,1,32,96]{3,2,1,0:T(8,128)S(1)}, s32[1,1,32,96]{3,2,1,0:T(8,128)}, u32[]{:S(2)}) copy-start(s32[1,1,32,96]{3,2,1,0:T(8,128)} %param.16) | copy-start | bytes 36868
  2.7 23.1 %all-to-all-start = ((bf16[16,128,256]{2,1,0:T(8,128)(2,1)}), bf16[16,128,256]{2,1,0:T(8,128)(2,1)S(1)}, u32[]{:S(2)}, u32[]{:S(2)}) async-start(bf16[16,128,256]{2,1,0:T(8,128)(2,1)} %shard_map.120), calls=%async_computation | async-start | bytes 2097152 | tf_op jit(solution)/shard_map/all_to_all | solution.py:219
  11.1 8.1 %collective-permute-start = (s32[2,16,96]{2,1,0:T(8,128)S(1)}, s32[2,16,96]{2,1,0:T(8,128)S(1)}, u32[]{:S(2)}, u32[]{:S(2)}) collective-permute-start(s32[2,16,96]{2,1,0:T(8,128)S(1)} %bitcast.39), channel_id=1, source_target_pairs={{0,8},{8,0},{1,9},{9,1},{2,10},{10,2},{3,11},{11,3},{4,12},{12,4},... | collective-permute-start | bytes 36872 | tf_op jit(solution)/shard_map/ppermute | solution.py:223
  27.3 4.8 %collective-permute-start.1 = (bf16[2,512,256]{2,1,0:T(8,128)(2,1)S(1)}, bf16[2,512,256]{2,1,0:T(8,128)(2,1)S(1)}, u32[]{:S(2)}, u32[]{:S(2)}) collective-permute-start(bf16[2,512,256]{2,1,0:T(8,128)(2,1)S(1)} %get-tuple-element.17), channel_id=1, source_target_pairs={{0,1},{1,0},{2,3},{3,2},{4,5},{5,4},{6,7},{7,6},{8,9},{9,8},{10,11... | collective-permute-start | bytes 1572872 | tf_op jit(solution)/shard_map/ppermute | solution.py:223
  31.5 20.5 %copy-start = (bf16[256,256]{1,0:T(8,128)(2,1)S(1)}, bf16[256,256]{1,0:T(8,128)(2,1)}, u32[]{:S(2)}) copy-start(bf16[256,256]{1,0:T(8,128)(2,1)} %w_ref.3) | copy-start | bytes 393220
  31.5 20.5 %copy-start.1 = (bf16[128,256]{1,0:T(8,128)(2,1)S(1)}, bf16[128,256]{1,0:T(8,128)(2,1)}, u32[]{:S(2)}) copy-start(bf16[128,256]{1,0:T(8,128)(2,1)} %x_ref.3) | copy-start | bytes 196612
  31.5 20.5 %copy-start.2 = (bf16[128,256]{1,0:T(8,128)(2,1)S(1)}, bf16[128,256]{1,0:T(8,128)(2,1)}, u32[]{:S(2)}) copy-start(bf16[128,256]{1,0:T(8,128)(2,1)} %ct_ref.1) | copy-start | bytes 196612
  31.6 20.5 %copy-start.3 = (f32[128]{0:T(128)S(1)}, f32[128]{0:T(128)}, u32[]{:S(2)}) copy-start(f32[128]{0:T(128)} %param.12) | copy-start | bytes 1540
  31.6 20.5 %copy-start.4 = (f32[256]{0:T(256)S(1)}, f32[256]{0:T(256)}, u32[]{:S(2)}) copy-start(f32[256]{0:T(256)} %param.11) | copy-start | bytes 3076
  84.5 6.2 %collective-permute-start.2 = (bf16[8,152,256]{2,1,0:T(8,128)(2,1)S(1)}, bf16[8,152,256]{2,1,0:T(8,128)(2,1)S(1)}, u32[]{:S(2)}, u32[]{:S(2)}) collective-permute-start(bf16[8,152,256]{2,1,0:T(8,128)(2,1)S(1)} %all_to_all.27.mine_ref), channel_id=1, source_target_pairs={{0,1},{1,0},{2,3},{3,2},{4,5},{5,4},{6,7},{7,6},{8,9},{9,8},{10,11... | collective-permute-start | bytes 1867784 | tf_op jit(solution)/shard_map/ppermute | solution.py:223

commit v12 on v11

--- a/solution.py
+++ b/solution.py
@@ -20,7 +20,8 @@
 XCHUNK = TILE + WR
 F32, BF16, I32 = jnp.float32, jnp.bfloat16, jnp.int32
 K0, K1 = math.sqrt(2.0 / math.pi), 0.044715
-ALL = ("x", "y", "h", "l", "c")
+ALL = ("xa", "xb", "ya", "yb", "h", "l", "c")
+PLANE = ("xa", "ya", "xb", "yb")
 PARAMS = pltpu.CompilerParams(vmem_limit_bytes=40 * 1024 * 1024)
 
 
@@ -235,11 +236,12 @@
     tile = sum(jnp.where(slot == k, tiles[:, k : k + 1], 0) for k in range(SLOTS))
     target = ((tile & 1) ^ c) * HALF + (tile >> 1) * TILE + edge_row.reshape(slot.shape)
     target = jnp.where(slot < SLOTS, target, -1)
-    edges = jnp.stack([target, edge_col.reshape(slot.shape)]).reshape(2, XY, H, EDGES)
+    edges = jnp.stack([target, edge_col.reshape(slot.shape)]).reshape(2, 2, 2, 2, 2, H, EDGES)
+    edges = edges.transpose(0, 1, 3, 2, 4, 5, 6).reshape(2, XY, H, EDGES)
     kept = lax.dynamic_index_in_dim(edges, h, 2, keepdims=False)
     came = swap(lax.dynamic_index_in_dim(edges, 1 - h, 2, keepdims=False), "h")
 
-    sources = exchange(spread(features, s), ("x", "y"))
+    sources = exchange(spread(features, s), PLANE)
 
     pairs = jnp.stack([jnp.where(h == 0, kept, came), jnp.where(h == 0, came, kept)], axis=1)
     lane = pairs.reshape(2 * H, E_ALL)
@@ -261,7 +263,7 @@
         middle_kernel,
         [((TILE, F), BF16), ((TILE, F), BF16), ((XY, WR + BB, F), BF16)],
     )(partial, features, s, weight, bias, cotangent)
-    w_parts = exchange(w_parts, ("x", "y"))
+    w_parts = exchange(w_parts, PLANE)
     (pay,) = call(load_kernel, [((ZN, ZCHUNK, F), BF16)])(w_parts, g)
     around = exchange(pay, ("l", "h"))
     other = swap(around, "c")
@@ -277,7 +279,7 @@
         [((HALF, F), BF16), ((XY, H * EDGES, F), BF16)],
         flops=4 * E_ALL * F * (HALF + TILE),
     )(picked, around, other, sub, columns)
-    terms = exchange(terms, ("x", "y"))
+    terms = exchange(terms, PLANE)
     feature_grad, weight_grad, bias_grad = call(
         final_kernel, [((TILE, F), BF16), ((F, F), F32), ((1, F), F32)]
     )(terms, g, s, weight, bias_sum)
@@ -285,8 +287,8 @@
 
 
 def solution(mesh):
-    fine = Mesh(mesh.devices.reshape(X, Y, H, L, C), ALL)
-    rows, edges = P(ALL, None), P(("x", "y", "h"), ("l", "c"), None, None)
+    fine = Mesh(mesh.devices.reshape(2, 2, 2, 2, H, L, C), ALL)
+    rows, edges = P(ALL, None), P(ALL[:5], ALL[5:], None, None)
     return jax.shard_map(
         per_device,
         mesh=fine,

time: 115 us -> 115 us (level)
  waiting for transfers between devices: 7.83 us -> 9.88 us
  starting transfers between devices: 22.3 us -> 20.6 us
    ppermute x3, starting transfers between devices: 14.8 us -> 13 us  [swap(): return lax.ppermute(array, axis, [(0, 1), (1, 0)])]
    all_to_all x1, waiting for transfers between devices: 6.2 us -> 7.96 us  [exchange(): return lax.all_to_all(array, axes, 0, 0, tiled=True)]
where the time goes in v12:
time: 115 us
  blocking collectives  73.1 us (64%)
  starting transfers between devices  20.6 us (18%)
  waiting for transfers between devices  9.88 us (9%)
  Pallas kernels  9.37 us (8%)
    all_to_all x4, blocking collectives, exchange(): return lax.all_to_all(array, axes, 0, 0, tiled=True)  73.1 us
    ppermute x3, starting transfers between devices, swap(): return lax.ppermute(array, axis, [(0, 1), (1, 0)])  13 us
    all_to_all x1, waiting for transfers between devices, exchange(): return lax.all_to_all(array, axes, 0, 0, tiled=True)  7.96 us
    all_to_all x1, starting transfers between devices, exchange(): return lax.all_to_all(array, axes, 0, 0, tiled=True)  7.6 us
  transfers between devices with their start and end apart: 4, of which 3 were waited for; matrix products, arithmetic and copies ran while one was open for 1% of the time, Pallas kernels for 2%

profile of v12, /device:TPU:1, one launch (start us, length us, event | category | flops | bytes accessed | tf_op | source)
XLA Modules:
  0.0 115.0 jit_solution(1782022880453530555)
XLA Ops:
  0.7 2.1 %shard_map.120 = bf16[16,128,256]{2,1,0:T(8,128)(2,1)} custom-call(bf16[128,256]{1,0:T(8,128)(2,1)} %x_ref.3, f32[1,128]{1,0:T(1,128)} %bitcast.36), custom_call_target="tpu_custom_call" | custom-call | tf_op jit(solution)/shard_map/pallas_call | solution.py:69
  2.7 7.6 %all-to-all-start = ((bf16[16,128,256]{2,1,0:T(8,128)(2,1)}), bf16[16,128,256]{2,1,0:T(8,128)(2,1)S(1)}, u32[]{:S(2)}, u32[]{:S(2)}) async-start(bf16[16,128,256]{2,1,0:T(8,128)(2,1)} %shard_map.120), calls=%async_computation | async-start | bytes 2097152 | tf_op jit(solution)/shard_map/all_to_all | solution.py:220
  10.5 0.1 broadcast_in_dim.53
  10.6 0.1 broadcast_in_dim.51
  10.7 0.1 broadcast_in_dim.49
  10.8 0.1 broadcast_in_dim.47
  10.9 0.1 add_select_fusion
  11.2 7.0 %collective-permute-start = (s32[2,16,96]{2,1,0:T(8,128)S(1)}, s32[2,16,96]{2,1,0:T(8,128)S(1)}, u32[]{:S(2)}, u32[]{:S(2)}) collective-permute-start(s32[2,16,96]{2,1,0:T(8,128)S(1)} %dynamic-slice_bitcast_fusion), channel_id=1, source_target_pairs={{0,8},{8,0},{1,9},{9,1},{2,10},{10,2},{3,11},{11,3},{4,12},{12,4},... | collective-permute-start | bytes 36872 | tf_op jit(solution)/shard_map/ppermute | solution.py:224
  18.2 1.4 %collective-permute-done = s32[2,16,96]{2,1,0:T(8,128)S(1)} collective-permute-done((s32[2,16,96]{2,1,0:T(8,128)S(1)}, s32[2,16,96]{2,1,0:T(8,128)S(1)}, u32[]{:S(2)}, u32[]{:S(2)}) %collective-permute-start) | collective-permute-done | bytes 12320 | tf_op jit(solution)/shard_map/ppermute | solution.py:224
  19.6 0.1 reshape.177.lane_ref
  19.7 0.3 copy.18
  20.0 8.0 %all-to-all-done.x_ref = bf16[16,128,256]{2,1,0:T(8,128)(2,1)S(1)} async-done(((bf16[16,128,256]{2,1,0:T(8,128)(2,1)}), bf16[16,128,256]{2,1,0:T(8,128)(2,1)S(1)}, u32[]{:S(2)}, u32[]{:S(2)}) %all-to-all-start) | async-done | bytes 1048608 | tf_op jit(solution)/shard_map/all_to_all | solution.py:220
  28.0 1.4 %shard_map.121 = (bf16[2,1536,256]{2,1,0:T(8,128)(2,1)S(1)}, bf16[2,512,256]{2,1,0:T(8,128)(2,1)S(1)}) custom-call(bf16[16,128,256]{2,1,0:T(8,128)(2,1)S(1)} %all-to-all-done.x_ref, s32[4,1536]{1,0:T(4,128)S(1)} %reshape.177.lane_ref, s32[1536,4]{1,0:T(8,128)S(1)} %bitcast.33), custom_call_target="tpu_custom_call" | custom-call | flops 1006632960 | bytes 2097152 | tf_op jit(solution)/shard_map/pallas_call | solution.py:251
  29.4 1.2 %collective-permute-start.1 = (bf16[2,512,256]{2,1,0:T(8,128)(2,1)S(1)}, bf16[2,512,256]{2,1,0:T(8,128)(2,1)S(1)}, u32[]{:S(2)}, u32[]{:S(2)}) collective-permute-start(bf16[2,512,256]{2,1,0:T(8,128)(2,1)S(1)} %get-tuple-element.17), channel_id=1, source_target_pairs={{0,1},{1,0},{2,3},{3,2},{4,5},{5,4},{6,7},{7,6},{8,9},{9,8},{10,11... | collective-permute-start | bytes 1572872 | tf_op jit(solution)/shard_map/ppermute | solution.py:224
  30.6 1.0 shard_map.122.mine_ref
  31.6 0.0 copy-start
  31.6 0.0 copy-start.1
  31.7 0.0 copy-start.3
  31.7 0.0 copy-start.4
  31.7 0.5 collective-permute-done.1.other_ref
  32.2 0.1 shard_map.123
  32.3 19.8 %all_to_all.25.part_ref = bf16[8,128,256]{2,1,0:T(8,128)(2,1)S(1)} all-to-all(bf16[8,128,256]{2,1,0:T(8,128)(2,1)S(1)} %shard_map.123), channel_id=1, replica_groups=mesh['xa'=2,'xb'=2,'ya'=2,'yb'=2,'h'=2,'l'=4,'c'=2] {'l','h'}, dimensions={0} | all-to-all | bytes 1048576 | tf_op jit(solution)/shard_map/all_to_all | solution.py:220
  52.1 0.7 shard_map.124
  52.9 10.0 %all_to_all.26.w_ref = bf16[16,24,256]{2,1,0:T(8,128)(2,1)S(1)} all-to-all(bf16[16,24,256]{2,1,0:T(8,128)(2,1)S(1)} %get-tuple-element.18), channel_id=1, replica_groups=mesh['xa'=2,'xb'=2,'ya'=2,'yb'=2,'h'=2,'l'=4,'c'=2] {'xa','ya','xb','yb'}, dimensions={0} | all-to-all | bytes 393216 | tf_op jit(solution)/shard_map/all_to_all | solution.py:220
  62.8 0.1 shard_map.125
  62.9 21.8 %all_to_all.27.mine_ref = bf16[8,152,256]{2,1,0:T(8,128)(2,1)S(1)} all-to-all(bf16[8,152,256]{2,1,0:T(8,128)(2,1)S(1)} %shard_map.125), channel_id=1, replica_groups=mesh['xa'=2,'xb'=2,'ya'=2,'yb'=2,'h'=2,'l'=4,'c'=2] {'l','h'}, dimensions={0} | all-to-all | bytes 1245184 | tf_op jit(solution)/shard_map/all_to_all | solution.py:220
  84.7 4.7 %collective-permute-start.2 = (bf16[8,152,256]{2,1,0:T(8,128)(2,1)S(1)}, bf16[8,152,256]{2,1,0:T(8,128)(2,1)S(1)}, u32[]{:S(2)}, u32[]{:S(2)}) collective-permute-start(bf16[8,152,256]{2,1,0:T(8,128)(2,1)S(1)} %all_to_all.27.mine_ref), channel_id=1, source_target_pairs={{0,1},{1,0},{2,3},{3,2},{4,5},{5,4},{6,7},{7,6},{8,9},{9,8},{10,11... | collective-permute-start | bytes 1867784 | tf_op jit(solution)/shard_map/ppermute | solution.py:224
  89.4 0.1 pad_add_fusion.1.col_ref
  89.5 1.6 %shard_map.126 = (bf16[16,192,256]{2,1,0:T(8,128)(2,1)S(1)}, bf16[128,256]{1,0:T(8,128)(2,1)}) custom-call(bf16[8,152,256]{2,1,0:T(8,128)(2,1)S(1)} %all_to_all.27.mine_ref, s32[1536,4]{1,0:T(8,128)S(1)} %bitcast.34, bf16[128,256]{1,0:T(8,128)(2,1)S(1)} %get-tuple-element.20.act_ref), custom_call_target="tpu_custom_call" | custom-call | flops 805306368 | bytes 2097152 | tf_op jit(solution)/shard_map/pallas_call | solution.py:270
  91.1 1.4 %shard_map.127 = (bf16[16,144,256]{2,1,0:T(8,128)(2,1)S(1)}, f32[1,256]{1,0:T(1,128)S(1)}) custom-call(bf16[16,192,256]{2,1,0:T(8,128)(2,1)S(1)} %get-tuple-element.22.picked_ref, bf16[8,152,256]{2,1,0:T(8,128)(2,1)S(1)} %all_to_all.27.mine_ref, bf16[8,152,256]{2,1,0:T(8,128)(2,1)S(1)} %collective-permute-done.2.other_ref, s32[1536,4]{1,0:T(8,128)S(1)} %bitcast.35, ...), custom_call_target="tpu_custom_call" | custom-call | flops 1006632960 | bytes 2097152 | tf_op jit(solution)/shard_map/pallas_call | solution.py:276
  92.5 21.6 %all_to_all.28.part_ref = bf16[16,144,256]{2,1,0:T(8,128)(2,1)S(1)} all-to-all(bf16[16,144,256]{2,1,0:T(8,128)(2,1)S(1)} %get-tuple-element.23), channel_id=1, replica_groups=mesh['xa'=2,'xb'=2,'ya'=2,'yb'=2,'h'=2,'l'=4,'c'=2] {'xa','ya','xb','yb'}, dimensions={0} | all-to-all | bytes 2359296 | tf_op jit(solution)/shard_map/all_to_all | solution.py:220
  114.1 1.0 shard_map.128
  (29 shorter events, 0.2 us)
Async XLA Ops:
  0.6 9.7 %copy-start.5 = (s32[1,1,32,96]{3,2,1,0:T(8,128)S(1)}, s32[1,1,32,96]{3,2,1,0:T(8,128)}, u32[]{:S(2)}) copy-start(s32[1,1,32,96]{3,2,1,0:T(8,128)} %param.14) | copy-start | bytes 36868
  0.6 9.8 %copy-start.8 = (s32[1,1,32,4]{2,3,1,0:T(4,128)S(1)}, s32[1,1,32,4]{2,3,1,0:T(4,128)}, u32[]{:S(2)}) copy-start(s32[1,1,32,4]{2,3,1,0:T(4,128)} %param.17) | copy-start | bytes 1540
  0.7 10.3 %copy-start.6 = (s32[1,1,32,96]{3,2,1,0:T(8,128)S(1)}, s32[1,1,32,96]{3,2,1,0:T(8,128)}, u32[]{:S(2)}) copy-start(s32[1,1,32,96]{3,2,1,0:T(8,128)} %param.15) | copy-start | bytes 36868
  0.7 10.4 %copy-start.7 = (s32[1,1,32,96]{3,2,1,0:T(8,128)S(1)}, s32[1,1,32,96]{3,2,1,0:T(8,128)}, u32[]{:S(2)}) copy-start(s32[1,1,32,96]{3,2,1,0:T(8,128)} %param.16) | copy-start | bytes 36868
  2.7 25.2 %all-to-all-start = ((bf16[16,128,256]{2,1,0:T(8,128)(2,1)}), bf16[16,128,256]{2,1,0:T(8,128)(2,1)S(1)}, u32[]{:S(2)}, u32[]{:S(2)}) async-start(bf16[16,128,256]{2,1,0:T(8,128)(2,1)} %shard_map.120), calls=%async_computation | async-start | bytes 2097152 | tf_op jit(solution)/shard_map/all_to_all | solution.py:220
  11.2 8.4 %collective-permute-start = (s32[2,16,96]{2,1,0:T(8,128)S(1)}, s32[2,16,96]{2,1,0:T(8,128)S(1)}, u32[]{:S(2)}, u32[]{:S(2)}) collective-permute-start(s32[2,16,96]{2,1,0:T(8,128)S(1)} %dynamic-slice_bitcast_fusion), channel_id=1, source_target_pairs={{0,8},{8,0},{1,9},{9,1},{2,10},{10,2},{3,11},{11,3},{4,12},{12,4},... | collective-permute-start | bytes 36872 | tf_op jit(solution)/shard_map/ppermute | solution.py:224
  29.4 2.8 %collective-permute-start.1 = (bf16[2,512,256]{2,1,0:T(8,128)(2,1)S(1)}, bf16[2,512,256]{2,1,0:T(8,128)(2,1)S(1)}, u32[]{:S(2)}, u32[]{:S(2)}) collective-permute-start(bf16[2,512,256]{2,1,0:T(8,128)(2,1)S(1)} %get-tuple-element.17), channel_id=1, source_target_pairs={{0,1},{1,0},{2,3},{3,2},{4,5},{5,4},{6,7},{7,6},{8,9},{9,8},{10,11... | collective-permute-start | bytes 1572872 | tf_op jit(solution)/shard_map/ppermute | solution.py:224
  31.6 20.5 %copy-start = (bf16[256,256]{1,0:T(8,128)(2,1)S(1)}, bf16[256,256]{1,0:T(8,128)(2,1)}, u32[]{:S(2)}) copy-start(bf16[256,256]{1,0:T(8,128)(2,1)} %w_ref.3) | copy-start | bytes 393220
  31.6 20.5 %copy-start.1 = (bf16[128,256]{1,0:T(8,128)(2,1)S(1)}, bf16[128,256]{1,0:T(8,128)(2,1)}, u32[]{:S(2)}) copy-start(bf16[128,256]{1,0:T(8,128)(2,1)} %x_ref.3) | copy-start | bytes 196612
  31.7 20.5 %copy-start.2 = (bf16[128,256]{1,0:T(8,128)(2,1)S(1)}, bf16[128,256]{1,0:T(8,128)(2,1)}, u32[]{:S(2)}) copy-start(bf16[128,256]{1,0:T(8,128)(2,1)} %ct_ref.1) | copy-start | bytes 196612
  31.7 20.5 %copy-start.3 = (f32[128]{0:T(128)S(1)}, f32[128]{0:T(128)}, u32[]{:S(2)}) copy-start(f32[128]{0:T(128)} %param.12) | copy-start | bytes 1540
  31.7 20.5 %copy-start.4 = (f32[256]{0:T(256)S(1)}, f32[256]{0:T(256)}, u32[]{:S(2)}) copy-start(f32[256]{0:T(256)} %param.11) | copy-start | bytes 3076
  84.7 6.4 %collective-permute-start.2 = (bf16[8,152,256]{2,1,0:T(8,128)(2,1)S(1)}, bf16[8,152,256]{2,1,0:T(8,128)(2,1)S(1)}, u32[]{:S(2)}, u32[]{:S(2)}) collective-permute-start(bf16[8,152,256]{2,1,0:T(8,128)(2,1)S(1)} %all_to_all.27.mine_ref), channel_id=1, source_target_pairs={{0,1},{1,0},{2,3},{3,2},{4,5},{5,4},{6,7},{7,6},{8,9},{9,8},{10,11... | collective-permute-start | bytes 1867784 | tf_op jit(solution)/shard_map/ppermute | solution.py:224

commit v13 on v11

--- a/solution.py
+++ b/solution.py
@@ -20,8 +20,13 @@
 XCHUNK = TILE + WR
 F32, BF16, I32 = jnp.float32, jnp.bfloat16, jnp.int32
 K0, K1 = math.sqrt(2.0 / math.pi), 0.044715
-ALL = ("x", "y", "h", "l", "c")
+ALL = ("x", "y", "h", "la", "lb", "c")
+LINE = ("lb", "la", "h")
 PARAMS = pltpu.CompilerParams(vmem_limit_bytes=40 * 1024 * 1024)
+
+
+def place_of(l, h):
+    return (l % 2) * 4 + (l // 2) * 2 + h
 
 
 def dot(a, b):
@@ -105,7 +110,7 @@
         for k in range(L):
             rows = pl.ds(k * TILE, TILE)
             total = mine_ref[b, rows, :] + other_ref[b, rows, :].astype(F32)
-            out_ref[k * H + b] = total.astype(BF16)
+            out_ref[place_of(k, b)] = total.astype(BF16)
 
 
 def middle_kernel(part_ref, x_ref, s_ref, w_ref, bias_ref, ct_ref, out_ref, g_ref, wp_ref):
@@ -150,7 +155,7 @@
     out_ref[...] = act_ref[...]
     for b in range(H):
         for k in range(L):
-            grads[pl.ds(k * TILE, TILE), :] = mine_ref[k * H + b, pl.ds(0, TILE), :]
+            grads[pl.ds(k * TILE, TILE), :] = mine_ref[place_of(k, b), pl.ds(0, TILE), :]
         for m in range(E_ALL // STEP):
             pick = one_hot(sub_ref[pl.ds(m * STEP, STEP), b : b + 1], (STEP, HALF), 1)
             value = dot(pick, grads[...]).astype(BF16)
@@ -175,7 +180,7 @@
     bias_ref[...] = jnp.sum(tail[WR:], axis=0, keepdims=True)
     for b in range(H):
         for k in range(L):
-            grads[pl.ds(k * TILE, TILE), :] = other_ref[k * H + b, pl.ds(0, TILE), :]
+            grads[pl.ds(k * TILE, TILE), :] = other_ref[place_of(k, b), pl.ds(0, TILE), :]
         for m in range(E_ALL // STEP):
             pick = one_hot(sub_ref[pl.ds(m * STEP, STEP), b : b + 1], (STEP, HALF), 1, HALF)
             value = dot(pick, grads[...])
@@ -256,14 +261,14 @@
         forward_keep_kernel, [((H, HALF, F), F32)], flops=4 * E_ALL * F * HALF
     )(gathered, lane)
     (partial,) = call(add_kernel, [((ZN, TILE, F), BF16)])(mine, other)
-    partial = exchange(partial, ("l", "h"))
+    partial = exchange(partial, LINE)
     act, g, w_parts = call(
         middle_kernel,
         [((TILE, F), BF16), ((TILE, F), BF16), ((XY, WR + BB, F), BF16)],
     )(partial, features, s, weight, bias, cotangent)
     w_parts = exchange(w_parts, ("x", "y"))
     (pay,) = call(load_kernel, [((ZN, ZCHUNK, F), BF16)])(w_parts, g)
-    around = exchange(pay, ("l", "h"))
+    around = exchange(pay, LINE)
     other = swap(around, "c")
     picked, output = call(
         backward_mine_kernel,
@@ -285,8 +290,8 @@
 
 
 def solution(mesh):
-    fine = Mesh(mesh.devices.reshape(X, Y, H, L, C), ALL)
-    rows, edges = P(ALL, None), P(("x", "y", "h"), ("l", "c"), None, None)
+    fine = Mesh(mesh.devices.reshape(X, Y, H, 2, 2, C), ALL)
+    rows, edges = P(ALL, None), P(ALL[:3], ALL[3:], None, None)
     return jax.shard_map(
         per_device,
         mesh=fine,

time: 115 us -> 115 us (level)
  blocking collectives: 72.3 us -> 73.6 us
    all_to_all x4, blocking collectives: 72.3 us -> 73.6 us  [exchange(): return lax.all_to_all(array, axes, 0, 0, tiled=True)]
where the time goes in v13:
time: 115 us
  blocking collectives  73.6 us (64%)
  starting transfers between devices  21.9 us (19%)
  Pallas kernels  9.37 us (8%)
  waiting for transfers between devices  7.83 us (7%)
    all_to_all x4, blocking collectives, exchange(): return lax.all_to_all(array, axes, 0, 0, tiled=True)  73.6 us
    ppermute x3, starting transfers between devices, swap(): return lax.ppermute(array, axis, [(0, 1), (1, 0)])  14.3 us
    all_to_all x1, starting transfers between devices, exchange(): return lax.all_to_all(array, axes, 0, 0, tiled=True)  7.6 us
    all_to_all x1, waiting for transfers between devices, exchange(): return lax.all_to_all(array, axes, 0, 0, tiled=True)  6.2 us
  transfers between devices with their start and end apart: 4, of which 3 were waited for; matrix products, arithmetic and copies ran while one was open for 1% of the time, Pallas kernels for 2%

profile of v13, /device:TPU:1, one launch (start us, length us, event | category | flops | bytes accessed | tf_op | source)
XLA Modules:
  0.0 114.8 jit_solution(84596994001697332)
XLA Ops:
  0.7 2.1 %shard_map.120 = bf16[16,128,256]{2,1,0:T(8,128)(2,1)} custom-call(bf16[128,256]{1,0:T(8,128)(2,1)} %x_ref.3, f32[1,128]{1,0:T(1,128)} %bitcast.30), custom_call_target="tpu_custom_call" | custom-call | tf_op jit(solution)/shard_map/pallas_call | solution.py:73
  2.7 7.6 %all-to-all-start = ((bf16[16,128,256]{2,1,0:T(8,128)(2,1)}), bf16[16,128,256]{2,1,0:T(8,128)(2,1)S(1)}, u32[]{:S(2)}, u32[]{:S(2)}) async-start(bf16[16,128,256]{2,1,0:T(8,128)(2,1)} %shard_map.120), calls=%async_computation | async-start | bytes 2097152 | tf_op jit(solution)/shard_map/all_to_all | solution.py:224
  10.5 0.1 broadcast_in_dim.53
  10.6 0.1 broadcast_in_dim.51
  10.7 0.1 broadcast_in_dim.49
  10.8 0.1 broadcast_in_dim.47
  10.9 0.0 copy-done.6
  10.9 0.1 add_select_fusion
  11.0 0.1 fusion.1
  11.1 7.0 %collective-permute-start = (s32[2,16,96]{2,1,0:T(8,128)S(1)}, s32[2,16,96]{2,1,0:T(8,128)S(1)}, u32[]{:S(2)}, u32[]{:S(2)}) collective-permute-start(s32[2,16,96]{2,1,0:T(8,128)S(1)} %bitcast.39), channel_id=1, source_target_pairs={{0,8},{8,0},{1,9},{9,1},{2,10},{10,2},{3,11},{11,3},{4,12},{12,4},... | collective-permute-start | bytes 36872 | tf_op jit(solution)/shard_map/ppermute | solution.py:228
  18.1 1.1 collective-permute-done
  19.3 0.1 reshape.173.lane_ref
  19.4 0.3 copy.27
  19.7 6.2 %all-to-all-done.x_ref = bf16[16,128,256]{2,1,0:T(8,128)(2,1)S(1)} async-done(((bf16[16,128,256]{2,1,0:T(8,128)(2,1)}), bf16[16,128,256]{2,1,0:T(8,128)(2,1)S(1)}, u32[]{:S(2)}, u32[]{:S(2)}) %all-to-all-start) | async-done | bytes 1048608 | tf_op jit(solution)/shard_map/all_to_all | solution.py:224
  25.9 1.4 %shard_map.121 = (bf16[2,1536,256]{2,1,0:T(8,128)(2,1)S(1)}, bf16[2,512,256]{2,1,0:T(8,128)(2,1)S(1)}) custom-call(bf16[16,128,256]{2,1,0:T(8,128)(2,1)S(1)} %all-to-all-done.x_ref, s32[4,1536]{1,0:T(4,128)S(1)} %reshape.173.lane_ref, s32[1536,4]{1,0:T(8,128)S(1)} %bitcast.27), custom_call_target="tpu_custom_call" | custom-call | flops 1006632960 | bytes 2097152 | tf_op jit(solution)/shard_map/pallas_call | solution.py:254
  27.3 3.2 %collective-permute-start.1 = (bf16[2,512,256]{2,1,0:T(8,128)(2,1)S(1)}, bf16[2,512,256]{2,1,0:T(8,128)(2,1)S(1)}, u32[]{:S(2)}, u32[]{:S(2)}) collective-permute-start(bf16[2,512,256]{2,1,0:T(8,128)(2,1)S(1)} %get-tuple-element.17), channel_id=1, source_target_pairs={{0,1},{1,0},{2,3},{3,2},{4,5},{5,4},{6,7},{7,6},{8,9},{9,8},{10,11... | collective-permute-start | bytes 1572872 | tf_op jit(solution)/shard_map/ppermute | solution.py:228
  30.5 1.0 shard_map.122.mine_ref
  31.5 0.0 copy-start
  31.5 0.0 copy-start.1
  31.6 0.5 collective-permute-done.1.other_ref
  32.1 0.1 shard_map.123
  32.2 20.6 %all_to_all.25.part_ref = bf16[8,128,256]{2,1,0:T(8,128)(2,1)S(1)} all-to-all(bf16[8,128,256]{2,1,0:T(8,128)(2,1)S(1)} %shard_map.123), channel_id=1, replica_groups=mesh['x'=4,'y'=4,'h'=2,'la'=2,'lb'=2,'c'=2] {'lb','la','h'}, dimensions={0} | all-to-all | bytes 1048576 | tf_op jit(solution)/shard_map/all_to_all | solution.py:224
  52.9 0.7 shard_map.124
  53.6 9.7 %all_to_all.26.w_ref = bf16[16,24,256]{2,1,0:T(8,128)(2,1)S(1)} all-to-all(bf16[16,24,256]{2,1,0:T(8,128)(2,1)S(1)} %get-tuple-element.18), channel_id=1, replica_groups=mesh['x'=4,'y'=4,'h'=2,'la'=2,'lb'=2,'c'=2] {'x','y'}, dimensions={0} | all-to-all | bytes 393216 | tf_op jit(solution)/shard_map/all_to_all | solution.py:224
  63.3 0.1 shard_map.125
  63.4 22.4 %all_to_all.27.mine_ref = bf16[8,152,256]{2,1,0:T(8,128)(2,1)S(1)} all-to-all(bf16[8,152,256]{2,1,0:T(8,128)(2,1)S(1)} %shard_map.125), channel_id=1, replica_groups=mesh['x'=4,'y'=4,'h'=2,'la'=2,'lb'=2,'c'=2] {'lb','la','h'}, dimensions={0} | all-to-all | bytes 1245184 | tf_op jit(solution)/shard_map/all_to_all | solution.py:224
  85.8 4.1 %collective-permute-start.2 = (bf16[8,152,256]{2,1,0:T(8,128)(2,1)S(1)}, bf16[8,152,256]{2,1,0:T(8,128)(2,1)S(1)}, u32[]{:S(2)}, u32[]{:S(2)}) collective-permute-start(bf16[8,152,256]{2,1,0:T(8,128)(2,1)S(1)} %all_to_all.27.mine_ref), channel_id=1, source_target_pairs={{0,1},{1,0},{2,3},{3,2},{4,5},{5,4},{6,7},{7,6},{8,9},{9,8},{10,11... | collective-permute-start | bytes 1867784 | tf_op jit(solution)/shard_map/ppermute | solution.py:228
  89.8 0.1 pad_add_fusion.1.col_ref
  89.9 1.6 %shard_map.126 = (bf16[16,192,256]{2,1,0:T(8,128)(2,1)S(1)}, bf16[128,256]{1,0:T(8,128)(2,1)}) custom-call(bf16[8,152,256]{2,1,0:T(8,128)(2,1)S(1)} %all_to_all.27.mine_ref, s32[1536,4]{1,0:T(8,128)S(1)} %bitcast.28, bf16[128,256]{1,0:T(8,128)(2,1)S(1)} %get-tuple-element.20.act_ref), custom_call_target="tpu_custom_call" | custom-call | flops 805306368 | bytes 2097152 | tf_op jit(solution)/shard_map/pallas_call | solution.py:273
  91.5 1.4 %shard_map.127 = (bf16[16,144,256]{2,1,0:T(8,128)(2,1)S(1)}, f32[1,256]{1,0:T(1,128)S(1)}) custom-call(bf16[16,192,256]{2,1,0:T(8,128)(2,1)S(1)} %get-tuple-element.22.picked_ref, bf16[8,152,256]{2,1,0:T(8,128)(2,1)S(1)} %all_to_all.27.mine_ref, bf16[8,152,256]{2,1,0:T(8,128)(2,1)S(1)} %collective-permute-done.2.other_ref, s32[1536,4]{1,0:T(8,128)S(1)} %bitcast.29, ...), custom_call_target="tpu_custom_call" | custom-call | flops 1006632960 | bytes 2097152 | tf_op jit(solution)/shard_map/pallas_call | solution.py:279
  92.9 20.9 %all_to_all.28.part_ref = bf16[16,144,256]{2,1,0:T(8,128)(2,1)S(1)} all-to-all(bf16[16,144,256]{2,1,0:T(8,128)(2,1)S(1)} %get-tuple-element.23), channel_id=1, replica_groups=mesh['x'=4,'y'=4,'h'=2,'la'=2,'lb'=2,'c'=2] {'x','y'}, dimensions={0} | all-to-all | bytes 2359296 | tf_op jit(solution)/shard_map/all_to_all | solution.py:224
  113.8 1.0 shard_map.128
  (27 shorter events, 0.2 us)
Async XLA Ops:
  0.6 9.7 %copy-start.5 = (s32[1,1,32,96]{3,2,1,0:T(8,128)S(1)}, s32[1,1,32,96]{3,2,1,0:T(8,128)}, u32[]{:S(2)}) copy-start(s32[1,1,32,96]{3,2,1,0:T(8,128)} %param.14) | copy-start | bytes 36868
  0.6 9.8 %copy-start.8 = (s32[1,1,32,4]{2,3,1,0:T(4,128)S(1)}, s32[1,1,32,4]{2,3,1,0:T(4,128)}, u32[]{:S(2)}) copy-start(s32[1,1,32,4]{2,3,1,0:T(4,128)} %param.17) | copy-start | bytes 1540
  0.7 10.2 %copy-start.6 = (s32[1,1,32,96]{3,2,1,0:T(8,128)S(1)}, s32[1,1,32,96]{3,2,1,0:T(8,128)}, u32[]{:S(2)}) copy-start(s32[1,1,32,96]{3,2,1,0:T(8,128)} %param.15) | copy-start | bytes 36868
  0.7 10.4 %copy-start.7 = (s32[1,1,32,96]{3,2,1,0:T(8,128)S(1)}, s32[1,1,32,96]{3,2,1,0:T(8,128)}, u32[]{:S(2)}) copy-start(s32[1,1,32,96]{3,2,1,0:T(8,128)} %param.16) | copy-start | bytes 36868
  2.7 23.1 %all-to-all-start = ((bf16[16,128,256]{2,1,0:T(8,128)(2,1)}), bf16[16,128,256]{2,1,0:T(8,128)(2,1)S(1)}, u32[]{:S(2)}, u32[]{:S(2)}) async-start(bf16[16,128,256]{2,1,0:T(8,128)(2,1)} %shard_map.120), calls=%async_computation | async-start | bytes 2097152 | tf_op jit(solution)/shard_map/all_to_all | solution.py:224
  11.1 8.1 %collective-permute-start = (s32[2,16,96]{2,1,0:T(8,128)S(1)}, s32[2,16,96]{2,1,0:T(8,128)S(1)}, u32[]{:S(2)}, u32[]{:S(2)}) collective-permute-start(s32[2,16,96]{2,1,0:T(8,128)S(1)} %bitcast.39), channel_id=1, source_target_pairs={{0,8},{8,0},{1,9},{9,1},{2,10},{10,2},{3,11},{11,3},{4,12},{12,4},... | collective-permute-start | bytes 36872 | tf_op jit(solution)/shard_map/ppermute | solution.py:228
  27.3 4.8 %collective-permute-start.1 = (bf16[2,512,256]{2,1,0:T(8,128)(2,1)S(1)}, bf16[2,512,256]{2,1,0:T(8,128)(2,1)S(1)}, u32[]{:S(2)}, u32[]{:S(2)}) collective-permute-start(bf16[2,512,256]{2,1,0:T(8,128)(2,1)S(1)} %get-tuple-element.17), channel_id=1, source_target_pairs={{0,1},{1,0},{2,3},{3,2},{4,5},{5,4},{6,7},{7,6},{8,9},{9,8},{10,11... | collective-permute-start | bytes 1572872 | tf_op jit(solution)/shard_map/ppermute | solution.py:228
  31.5 21.3 %copy-start = (bf16[256,256]{1,0:T(8,128)(2,1)S(1)}, bf16[256,256]{1,0:T(8,128)(2,1)}, u32[]{:S(2)}) copy-start(bf16[256,256]{1,0:T(8,128)(2,1)} %w_ref.3) | copy-start | bytes 393220
  31.5 21.3 %copy-start.1 = (bf16[128,256]{1,0:T(8,128)(2,1)S(1)}, bf16[128,256]{1,0:T(8,128)(2,1)}, u32[]{:S(2)}) copy-start(bf16[128,256]{1,0:T(8,128)(2,1)} %x_ref.3) | copy-start | bytes 196612
  31.5 21.3 %copy-start.2 = (bf16[128,256]{1,0:T(8,128)(2,1)S(1)}, bf16[128,256]{1,0:T(8,128)(2,1)}, u32[]{:S(2)}) copy-start(bf16[128,256]{1,0:T(8,128)(2,1)} %ct_ref.1) | copy-start | bytes 196612
  31.6 21.3 %copy-start.3 = (f32[128]{0:T(128)S(1)}, f32[128]{0:T(128)}, u32[]{:S(2)}) copy-start(f32[128]{0:T(128)} %param.12) | copy-start | bytes 1540
  31.6 21.3 %copy-start.4 = (f32[256]{0:T(256)S(1)}, f32[256]{0:T(256)}, u32[]{:S(2)}) copy-start(f32[256]{0:T(256)} %param.11) | copy-start | bytes 3076
  85.8 5.7 %collective-permute-start.2 = (bf16[8,152,256]{2,1,0:T(8,128)(2,1)S(1)}, bf16[8,152,256]{2,1,0:T(8,128)(2,1)S(1)}, u32[]{:S(2)}, u32[]{:S(2)}) collective-permute-start(bf16[8,152,256]{2,1,0:T(8,128)(2,1)S(1)} %all_to_all.27.mine_ref), channel_id=1, source_target_pairs={{0,1},{1,0},{2,3},{3,2},{4,5},{5,4},{6,7},{7,6},{8,9},{9,8},{10,11... | collective-permute-start | bytes 1867784 | tf_op jit(solution)/shard_map/ppermute | solution.py:228

commit v14 on v13

--- a/solution.py
+++ b/solution.py
@@ -21,12 +21,12 @@
 F32, BF16, I32 = jnp.float32, jnp.bfloat16, jnp.int32
 K0, K1 = math.sqrt(2.0 / math.pi), 0.044715
 ALL = ("x", "y", "h", "la", "lb", "c")
-LINE = ("lb", "la", "h")
+LINE = ("lb", "h", "la")
 PARAMS = pltpu.CompilerParams(vmem_limit_bytes=40 * 1024 * 1024)
 
 
 def place_of(l, h):
-    return (l % 2) * 4 + (l // 2) * 2 + h
+    return (l % 2) * 4 + h * 2 + l // 2
 
 
 def dot(a, b):

time: 115 us -> 115 us (level)
  blocking collectives: 73.6 us -> 72.1 us
  starting transfers between devices: 21.9 us -> 23.2 us
    all_to_all x4, blocking collectives: 73.6 us -> 72.1 us  [exchange(): return lax.all_to_all(array, axes, 0, 0, tiled=True)]
    ppermute x3, starting transfers between devices: 14.3 us -> 15.7 us  [swap(): return lax.ppermute(array, axis, [(0, 1), (1, 0)])]
where the time goes in v14:
time: 115 us
  blocking collectives  72.1 us (63%)
  starting transfers between devices  23.2 us (20%)
  Pallas kernels  9.37 us (8%)
  waiting for transfers between devices  7.83 us (7%)
    all_to_all x4, blocking collectives, exchange(): return lax.all_to_all(array, axes, 0, 0, tiled=True)  72.1 us
    ppermute x3, starting transfers between devices, swap(): return lax.ppermute(array, axis, [(0, 1), (1, 0)])  15.7 us
    all_to_all x1, starting transfers between devices, exchange(): return lax.all_to_all(array, axes, 0, 0, tiled=True)  7.6 us
    all_to_all x1, waiting for transfers between devices, exchange(): return lax.all_to_all(array, axes, 0, 0, tiled=True)  6.2 us
  transfers between devices with their start and end apart: 4, of which 3 were waited for; matrix products, arithmetic and copies ran while one was open for 1% of the time, Pallas kernels for 2%

profile of v14, /device:TPU:1, one launch (start us, length us, event | category | flops | bytes accessed | tf_op | source)
XLA Modules:
  0.0 114.6 jit_solution(14199730199262978284)
XLA Ops:
  0.7 2.1 %shard_map.120 = bf16[16,128,256]{2,1,0:T(8,128)(2,1)} custom-call(bf16[128,256]{1,0:T(8,128)(2,1)} %x_ref.3, f32[1,128]{1,0:T(1,128)} %bitcast.30), custom_call_target="tpu_custom_call" | custom-call | tf_op jit(solution)/shard_map/pallas_call | solution.py:73
  2.7 7.6 %all-to-all-start = ((bf16[16,128,256]{2,1,0:T(8,128)(2,1)}), bf16[16,128,256]{2,1,0:T(8,128)(2,1)S(1)}, u32[]{:S(2)}, u32[]{:S(2)}) async-start(bf16[16,128,256]{2,1,0:T(8,128)(2,1)} %shard_map.120), calls=%async_computation | async-start | bytes 2097152 | tf_op jit(solution)/shard_map/all_to_all | solution.py:224
  10.5 0.1 broadcast_in_dim.53
  10.6 0.1 broadcast_in_dim.51
  10.7 0.1 broadcast_in_dim.49
  10.8 0.1 broadcast_in_dim.47
  10.9 0.0 copy-done.6
  10.9 0.1 add_select_fusion
  11.0 0.1 fusion.1
  11.1 7.0 %collective-permute-start = (s32[2,16,96]{2,1,0:T(8,128)S(1)}, s32[2,16,96]{2,1,0:T(8,128)S(1)}, u32[]{:S(2)}, u32[]{:S(2)}) collective-permute-start(s32[2,16,96]{2,1,0:T(8,128)S(1)} %bitcast.39), channel_id=1, source_target_pairs={{0,8},{8,0},{1,9},{9,1},{2,10},{10,2},{3,11},{11,3},{4,12},{12,4},... | collective-permute-start | bytes 36872 | tf_op jit(solution)/shard_map/ppermute | solution.py:228
  18.1 1.1 collective-permute-done
  19.3 0.1 reshape.173.lane_ref
  19.4 0.3 copy.27
  19.7 6.2 %all-to-all-done.x_ref = bf16[16,128,256]{2,1,0:T(8,128)(2,1)S(1)} async-done(((bf16[16,128,256]{2,1,0:T(8,128)(2,1)}), bf16[16,128,256]{2,1,0:T(8,128)(2,1)S(1)}, u32[]{:S(2)}, u32[]{:S(2)}) %all-to-all-start) | async-done | bytes 1048608 | tf_op jit(solution)/shard_map/all_to_all | solution.py:224
  25.9 1.4 %shard_map.121 = (bf16[2,1536,256]{2,1,0:T(8,128)(2,1)S(1)}, bf16[2,512,256]{2,1,0:T(8,128)(2,1)S(1)}) custom-call(bf16[16,128,256]{2,1,0:T(8,128)(2,1)S(1)} %all-to-all-done.x_ref, s32[4,1536]{1,0:T(4,128)S(1)} %reshape.173.lane_ref, s32[1536,4]{1,0:T(8,128)S(1)} %bitcast.27), custom_call_target="tpu_custom_call" | custom-call | flops 1006632960 | bytes 2097152 | tf_op jit(solution)/shard_map/pallas_call | solution.py:254
  27.3 3.2 %collective-permute-start.1 = (bf16[2,512,256]{2,1,0:T(8,128)(2,1)S(1)}, bf16[2,512,256]{2,1,0:T(8,128)(2,1)S(1)}, u32[]{:S(2)}, u32[]{:S(2)}) collective-permute-start(bf16[2,512,256]{2,1,0:T(8,128)(2,1)S(1)} %get-tuple-element.17), channel_id=1, source_target_pairs={{0,1},{1,0},{2,3},{3,2},{4,5},{5,4},{6,7},{7,6},{8,9},{9,8},{10,11... | collective-permute-start | bytes 1572872 | tf_op jit(solution)/shard_map/ppermute | solution.py:228
  30.5 1.0 shard_map.122.mine_ref
  31.5 0.0 copy-start
  31.6 0.5 collective-permute-done.1.other_ref
  32.1 0.1 shard_map.123
  32.2 20.9 %all_to_all.25.part_ref = bf16[8,128,256]{2,1,0:T(8,128)(2,1)S(1)} all-to-all(bf16[8,128,256]{2,1,0:T(8,128)(2,1)S(1)} %shard_map.123), channel_id=1, replica_groups=mesh['x'=4,'y'=4,'h'=2,'la'=2,'lb'=2,'c'=2] {'lb','h','la'}, dimensions={0} | all-to-all | bytes 1048576 | tf_op jit(solution)/shard_map/all_to_all | solution.py:224
  53.2 0.7 shard_map.124
  53.9 9.7 %all_to_all.26.w_ref = bf16[16,24,256]{2,1,0:T(8,128)(2,1)S(1)} all-to-all(bf16[16,24,256]{2,1,0:T(8,128)(2,1)S(1)} %get-tuple-element.18), channel_id=1, replica_groups=mesh['x'=4,'y'=4,'h'=2,'la'=2,'lb'=2,'c'=2] {'x','y'}, dimensions={0} | all-to-all | bytes 393216 | tf_op jit(solution)/shard_map/all_to_all | solution.py:224
  63.6 0.1 shard_map.125
  63.7 20.3 %all_to_all.27.mine_ref = bf16[8,152,256]{2,1,0:T(8,128)(2,1)S(1)} all-to-all(bf16[8,152,256]{2,1,0:T(8,128)(2,1)S(1)} %shard_map.125), channel_id=1, replica_groups=mesh['x'=4,'y'=4,'h'=2,'la'=2,'lb'=2,'c'=2] {'lb','h','la'}, dimensions={0} | all-to-all | bytes 1245184 | tf_op jit(solution)/shard_map/all_to_all | solution.py:224
  84.0 5.4 %collective-permute-start.2 = (bf16[8,152,256]{2,1,0:T(8,128)(2,1)S(1)}, bf16[8,152,256]{2,1,0:T(8,128)(2,1)S(1)}, u32[]{:S(2)}, u32[]{:S(2)}) collective-permute-start(bf16[8,152,256]{2,1,0:T(8,128)(2,1)S(1)} %all_to_all.27.mine_ref), channel_id=1, source_target_pairs={{0,1},{1,0},{2,3},{3,2},{4,5},{5,4},{6,7},{7,6},{8,9},{9,8},{10,11... | collective-permute-start | bytes 1867784 | tf_op jit(solution)/shard_map/ppermute | solution.py:228
  89.4 0.1 pad_add_fusion.1.col_ref
  89.5 1.6 %shard_map.126 = (bf16[16,192,256]{2,1,0:T(8,128)(2,1)S(1)}, bf16[128,256]{1,0:T(8,128)(2,1)}) custom-call(bf16[8,152,256]{2,1,0:T(8,128)(2,1)S(1)} %all_to_all.27.mine_ref, s32[1536,4]{1,0:T(8,128)S(1)} %bitcast.28, bf16[128,256]{1,0:T(8,128)(2,1)S(1)} %get-tuple-element.20.act_ref), custom_call_target="tpu_custom_call" | custom-call | flops 805306368 | bytes 2097152 | tf_op jit(solution)/shard_map/pallas_call | solution.py:273
  91.1 0.0 collective-permute-done.2.other_ref
  91.1 1.4 %shard_map.127 = (bf16[16,144,256]{2,1,0:T(8,128)(2,1)S(1)}, f32[1,256]{1,0:T(1,128)S(1)}) custom-call(bf16[16,192,256]{2,1,0:T(8,128)(2,1)S(1)} %get-tuple-element.22.picked_ref, bf16[8,152,256]{2,1,0:T(8,128)(2,1)S(1)} %all_to_all.27.mine_ref, bf16[8,152,256]{2,1,0:T(8,128)(2,1)S(1)} %collective-permute-done.2.other_ref, s32[1536,4]{1,0:T(8,128)S(1)} %bitcast.29, ...), custom_call_target="tpu_custom_call" | custom-call | flops 1006632960 | bytes 2097152 | tf_op jit(solution)/shard_map/pallas_call | solution.py:279
  92.5 21.1 %all_to_all.28.part_ref = bf16[16,144,256]{2,1,0:T(8,128)(2,1)S(1)} all-to-all(bf16[16,144,256]{2,1,0:T(8,128)(2,1)S(1)} %get-tuple-element.23), channel_id=1, replica_groups=mesh['x'=4,'y'=4,'h'=2,'la'=2,'lb'=2,'c'=2] {'x','y'}, dimensions={0} | all-to-all | bytes 2359296 | tf_op jit(solution)/shard_map/all_to_all | solution.py:224
  113.6 1.0 shard_map.128
  (27 shorter events, 0.2 us)
Async XLA Ops:
  0.6 9.7 %copy-start.5 = (s32[1,1,32,96]{3,2,1,0:T(8,128)S(1)}, s32[1,1,32,96]{3,2,1,0:T(8,128)}, u32[]{:S(2)}) copy-start(s32[1,1,32,96]{3,2,1,0:T(8,128)} %param.14) | copy-start | bytes 36868
  0.6 9.8 %copy-start.8 = (s32[1,1,32,4]{2,3,1,0:T(4,128)S(1)}, s32[1,1,32,4]{2,3,1,0:T(4,128)}, u32[]{:S(2)}) copy-start(s32[1,1,32,4]{2,3,1,0:T(4,128)} %param.17) | copy-start | bytes 1540
  0.7 10.2 %copy-start.6 = (s32[1,1,32,96]{3,2,1,0:T(8,128)S(1)}, s32[1,1,32,96]{3,2,1,0:T(8,128)}, u32[]{:S(2)}) copy-start(s32[1,1,32,96]{3,2,1,0:T(8,128)} %param.15) | copy-start | bytes 36868
  0.7 10.4 %copy-start.7 = (s32[1,1,32,96]{3,2,1,0:T(8,128)S(1)}, s32[1,1,32,96]{3,2,1,0:T(8,128)}, u32[]{:S(2)}) copy-start(s32[1,1,32,96]{3,2,1,0:T(8,128)} %param.16) | copy-start | bytes 36868
  2.7 23.1 %all-to-all-start = ((bf16[16,128,256]{2,1,0:T(8,128)(2,1)}), bf16[16,128,256]{2,1,0:T(8,128)(2,1)S(1)}, u32[]{:S(2)}, u32[]{:S(2)}) async-start(bf16[16,128,256]{2,1,0:T(8,128)(2,1)} %shard_map.120), calls=%async_computation | async-start | bytes 2097152 | tf_op jit(solution)/shard_map/all_to_all | solution.py:224
  11.1 8.1 %collective-permute-start = (s32[2,16,96]{2,1,0:T(8,128)S(1)}, s32[2,16,96]{2,1,0:T(8,128)S(1)}, u32[]{:S(2)}, u32[]{:S(2)}) collective-permute-start(s32[2,16,96]{2,1,0:T(8,128)S(1)} %bitcast.39), channel_id=1, source_target_pairs={{0,8},{8,0},{1,9},{9,1},{2,10},{10,2},{3,11},{11,3},{4,12},{12,4},... | collective-permute-start | bytes 36872 | tf_op jit(solution)/shard_map/ppermute | solution.py:228
  27.3 4.8 %collective-permute-start.1 = (bf16[2,512,256]{2,1,0:T(8,128)(2,1)S(1)}, bf16[2,512,256]{2,1,0:T(8,128)(2,1)S(1)}, u32[]{:S(2)}, u32[]{:S(2)}) collective-permute-start(bf16[2,512,256]{2,1,0:T(8,128)(2,1)S(1)} %get-tuple-element.17), channel_id=1, source_target_pairs={{0,1},{1,0},{2,3},{3,2},{4,5},{5,4},{6,7},{7,6},{8,9},{9,8},{10,11... | collective-permute-start | bytes 1572872 | tf_op jit(solution)/shard_map/ppermute | solution.py:228
  31.5 21.6 %copy-start = (bf16[256,256]{1,0:T(8,128)(2,1)S(1)}, bf16[256,256]{1,0:T(8,128)(2,1)}, u32[]{:S(2)}) copy-start(bf16[256,256]{1,0:T(8,128)(2,1)} %w_ref.3) | copy-start | bytes 393220
  31.5 21.6 %copy-start.1 = (bf16[128,256]{1,0:T(8,128)(2,1)S(1)}, bf16[128,256]{1,0:T(8,128)(2,1)}, u32[]{:S(2)}) copy-start(bf16[128,256]{1,0:T(8,128)(2,1)} %x_ref.3) | copy-start | bytes 196612
  31.5 21.6 %copy-start.2 = (bf16[128,256]{1,0:T(8,128)(2,1)S(1)}, bf16[128,256]{1,0:T(8,128)(2,1)}, u32[]{:S(2)}) copy-start(bf16[128,256]{1,0:T(8,128)(2,1)} %ct_ref.1) | copy-start | bytes 196612
  31.6 21.6 %copy-start.3 = (f32[128]{0:T(128)S(1)}, f32[128]{0:T(128)}, u32[]{:S(2)}) copy-start(f32[128]{0:T(128)} %param.12) | copy-start | bytes 1540
  31.6 21.6 %copy-start.4 = (f32[256]{0:T(256)S(1)}, f32[256]{0:T(256)}, u32[]{:S(2)}) copy-start(f32[256]{0:T(256)} %param.11) | copy-start | bytes 3076
  84.0 7.1 %collective-permute-start.2 = (bf16[8,152,256]{2,1,0:T(8,128)(2,1)S(1)}, bf16[8,152,256]{2,1,0:T(8,128)(2,1)S(1)}, u32[]{:S(2)}, u32[]{:S(2)}) collective-permute-start(bf16[8,152,256]{2,1,0:T(8,128)(2,1)S(1)} %all_to_all.27.mine_ref), channel_id=1, source_target_pairs={{0,1},{1,0},{2,3},{3,2},{4,5},{5,4},{6,7},{7,6},{8,9},{9,8},{10,11... | collective-permute-start | bytes 1867784 | tf_op jit(solution)/shard_map/ppermute | solution.py:228

commit v15 on v11

--- a/solution.py
+++ b/solution.py
@@ -235,11 +235,12 @@
     tile = sum(jnp.where(slot == k, tiles[:, k : k + 1], 0) for k in range(SLOTS))
     target = ((tile & 1) ^ c) * HALF + (tile >> 1) * TILE + edge_row.reshape(slot.shape)
     target = jnp.where(slot < SLOTS, target, -1)
-    edges = jnp.stack([target, edge_col.reshape(slot.shape)]).reshape(2, XY, H, EDGES)
+    edges = jnp.stack([target, edge_col.reshape(slot.shape)]).reshape(2, X, Y, H, EDGES)
+    edges = edges.transpose(0, 2, 1, 3, 4).reshape(2, XY, H, EDGES)
     kept = lax.dynamic_index_in_dim(edges, h, 2, keepdims=False)
     came = swap(lax.dynamic_index_in_dim(edges, 1 - h, 2, keepdims=False), "h")
 
-    sources = exchange(spread(features, s), ("x", "y"))
+    sources = exchange(spread(features, s), ("y", "x"))
 
     pairs = jnp.stack([jnp.where(h == 0, kept, came), jnp.where(h == 0, came, kept)], axis=1)
     lane = pairs.reshape(2 * H, E_ALL)
@@ -261,7 +262,7 @@
         middle_kernel,
         [((TILE, F), BF16), ((TILE, F), BF16), ((XY, WR + BB, F), BF16)],
     )(partial, features, s, weight, bias, cotangent)
-    w_parts = exchange(w_parts, ("x", "y"))
+    w_parts = exchange(w_parts, ("y", "x"))
     (pay,) = call(load_kernel, [((ZN, ZCHUNK, F), BF16)])(w_parts, g)
     around = exchange(pay, ("l", "h"))
     other = swap(around, "c")
@@ -277,7 +278,7 @@
         [((HALF, F), BF16), ((XY, H * EDGES, F), BF16)],
         flops=4 * E_ALL * F * (HALF + TILE),
     )(picked, around, other, sub, columns)
-    terms = exchange(terms, ("x", "y"))
+    terms = exchange(terms, ("y", "x"))
     feature_grad, weight_grad, bias_grad = call(
         final_kernel, [((TILE, F), BF16), ((F, F), F32), ((1, F), F32)]
     )(terms, g, s, weight, bias_sum)

time: 115 us -> 114 us (level)
  starting transfers between devices: 22.3 us -> 20.6 us
    ppermute x3, starting transfers between devices: 14.8 us -> 13 us  [swap(): return lax.ppermute(array, axis, [(0, 1), (1, 0)])]
where the time goes in v15:
time: 114 us
  blocking collectives  73.4 us (64%)
  starting transfers between devices  20.6 us (18%)
  Pallas kernels  9.38 us (8%)
  waiting for transfers between devices  8.26 us (7%)
    all_to_all x4, blocking collectives, exchange(): return lax.all_to_all(array, axes, 0, 0, tiled=True)  73.4 us
    ppermute x3, starting transfers between devices, swap(): return lax.ppermute(array, axis, [(0, 1), (1, 0)])  13 us
    all_to_all x1, starting transfers between devices, exchange(): return lax.all_to_all(array, axes, 0, 0, tiled=True)  7.6 us
    all_to_all x1, waiting for transfers between devices, exchange(): return lax.all_to_all(array, axes, 0, 0, tiled=True)  6.33 us
  transfers between devices with their start and end apart: 4, of which 3 were waited for; matrix products, arithmetic and copies ran while one was open for 1% of the time, Pallas kernels for 2%

profile of v15, /device:TPU:1, one launch (start us, length us, event | category | flops | bytes accessed | tf_op | source)
XLA Modules:
  0.0 113.8 jit_solution(14529952658280119320)
XLA Ops:
  0.7 2.1 %shard_map.120 = bf16[16,128,256]{2,1,0:T(8,128)(2,1)} custom-call(bf16[128,256]{1,0:T(8,128)(2,1)} %x_ref.3, f32[1,128]{1,0:T(1,128)} %bitcast.36), custom_call_target="tpu_custom_call" | custom-call | tf_op jit(solution)/shard_map/pallas_call | solution.py:68
  2.7 7.6 %all-to-all-start = ((bf16[16,128,256]{2,1,0:T(8,128)(2,1)}), bf16[16,128,256]{2,1,0:T(8,128)(2,1)S(1)}, u32[]{:S(2)}, u32[]{:S(2)}) async-start(bf16[16,128,256]{2,1,0:T(8,128)(2,1)} %shard_map.120), calls=%async_computation | async-start | bytes 2097152 | tf_op jit(solution)/shard_map/all_to_all | solution.py:219
  10.5 0.1 broadcast_in_dim.53
  10.6 0.1 broadcast_in_dim.51
  10.7 0.1 broadcast_in_dim.49
  10.8 0.1 broadcast_in_dim.47
  10.9 0.1 add_select_fusion
  11.1 7.0 %collective-permute-start = (s32[2,16,96]{2,1,0:T(8,128)S(1)}, s32[2,16,96]{2,1,0:T(8,128)S(1)}, u32[]{:S(2)}, u32[]{:S(2)}) collective-permute-start(s32[2,16,96]{2,1,0:T(8,128)S(1)} %dynamic-slice_bitcast_fusion), channel_id=1, source_target_pairs={{0,8},{8,0},{1,9},{9,1},{2,10},{10,2},{3,11},{11,3},{4,12},{12,4},... | collective-permute-start | bytes 36872 | tf_op jit(solution)/shard_map/ppermute | solution.py:223
  18.1 1.4 %collective-permute-done = s32[2,16,96]{2,1,0:T(8,128)S(1)} collective-permute-done((s32[2,16,96]{2,1,0:T(8,128)S(1)}, s32[2,16,96]{2,1,0:T(8,128)S(1)}, u32[]{:S(2)}, u32[]{:S(2)}) %collective-permute-start) | collective-permute-done | bytes 12320 | tf_op jit(solution)/shard_map/ppermute | solution.py:223
  19.6 0.1 reshape.177.lane_ref
  19.7 0.3 copy.20
  20.0 6.3 %all-to-all-done.x_ref = bf16[16,128,256]{2,1,0:T(8,128)(2,1)S(1)} async-done(((bf16[16,128,256]{2,1,0:T(8,128)(2,1)}), bf16[16,128,256]{2,1,0:T(8,128)(2,1)S(1)}, u32[]{:S(2)}, u32[]{:S(2)}) %all-to-all-start) | async-done | bytes 1048608 | tf_op jit(solution)/shard_map/all_to_all | solution.py:219
  26.3 1.4 %shard_map.121 = (bf16[2,1536,256]{2,1,0:T(8,128)(2,1)S(1)}, bf16[2,512,256]{2,1,0:T(8,128)(2,1)S(1)}) custom-call(bf16[16,128,256]{2,1,0:T(8,128)(2,1)S(1)} %all-to-all-done.x_ref, s32[4,1536]{1,0:T(4,128)S(1)} %reshape.177.lane_ref, s32[1536,4]{1,0:T(8,128)S(1)} %bitcast.33), custom_call_target="tpu_custom_call" | custom-call | flops 1006632960 | bytes 2097152 | tf_op jit(solution)/shard_map/pallas_call | solution.py:250
  27.8 2.7 %collective-permute-start.1 = (bf16[2,512,256]{2,1,0:T(8,128)(2,1)S(1)}, bf16[2,512,256]{2,1,0:T(8,128)(2,1)S(1)}, u32[]{:S(2)}, u32[]{:S(2)}) collective-permute-start(bf16[2,512,256]{2,1,0:T(8,128)(2,1)S(1)} %get-tuple-element.17), channel_id=1, source_target_pairs={{0,1},{1,0},{2,3},{3,2},{4,5},{5,4},{6,7},{7,6},{8,9},{9,8},{10,11... | collective-permute-start | bytes 1572872 | tf_op jit(solution)/shard_map/ppermute | solution.py:223
  30.5 1.0 shard_map.122.mine_ref
  31.5 0.0 copy-start
  31.5 0.0 copy-start.1
  31.5 0.0 copy-start.2
  31.5 0.0 copy-start.3
  31.5 0.5 collective-permute-done.1.other_ref
  32.0 0.1 shard_map.123
  32.2 19.8 %all_to_all.25.part_ref = bf16[8,128,256]{2,1,0:T(8,128)(2,1)S(1)} all-to-all(bf16[8,128,256]{2,1,0:T(8,128)(2,1)S(1)} %shard_map.123), channel_id=1, replica_groups=mesh['x'=4,'y'=4,'h'=2,'l'=4,'c'=2] {'l','h'}, dimensions={0} | all-to-all | bytes 1048576 | tf_op jit(solution)/shard_map/all_to_all | solution.py:219
  52.0 0.7 shard_map.124
  52.7 9.8 %all_to_all.26.w_ref = bf16[16,24,256]{2,1,0:T(8,128)(2,1)S(1)} all-to-all(bf16[16,24,256]{2,1,0:T(8,128)(2,1)S(1)} %get-tuple-element.18), channel_id=1, replica_groups=mesh['x'=4,'y'=4,'h'=2,'l'=4,'c'=2] {'y','x'}, dimensions={0} | all-to-all | bytes 393216 | tf_op jit(solution)/shard_map/all_to_all | solution.py:219
  62.5 0.1 shard_map.125
  62.5 23.2 %all_to_all.27.mine_ref = bf16[8,152,256]{2,1,0:T(8,128)(2,1)S(1)} all-to-all(bf16[8,152,256]{2,1,0:T(8,128)(2,1)S(1)} %shard_map.125), channel_id=1, replica_groups=mesh['x'=4,'y'=4,'h'=2,'l'=4,'c'=2] {'l','h'}, dimensions={0} | all-to-all | bytes 1245184 | tf_op jit(solution)/shard_map/all_to_all | solution.py:219
  85.8 3.3 %collective-permute-start.2 = (bf16[8,152,256]{2,1,0:T(8,128)(2,1)S(1)}, bf16[8,152,256]{2,1,0:T(8,128)(2,1)S(1)}, u32[]{:S(2)}, u32[]{:S(2)}) collective-permute-start(bf16[8,152,256]{2,1,0:T(8,128)(2,1)S(1)} %all_to_all.27.mine_ref), channel_id=1, source_target_pairs={{0,1},{1,0},{2,3},{3,2},{4,5},{5,4},{6,7},{7,6},{8,9},{9,8},{10,11... | collective-permute-start | bytes 1867784 | tf_op jit(solution)/shard_map/ppermute | solution.py:223
  89.1 0.1 pad_add_fusion.1.col_ref
  89.2 1.6 %shard_map.126 = (bf16[16,192,256]{2,1,0:T(8,128)(2,1)S(1)}, bf16[128,256]{1,0:T(8,128)(2,1)}) custom-call(bf16[8,152,256]{2,1,0:T(8,128)(2,1)S(1)} %all_to_all.27.mine_ref, s32[1536,4]{1,0:T(8,128)S(1)} %bitcast.34, bf16[128,256]{1,0:T(8,128)(2,1)S(1)} %get-tuple-element.20.act_ref), custom_call_target="tpu_custom_call" | custom-call | flops 805306368 | bytes 2097152 | tf_op jit(solution)/shard_map/pallas_call | solution.py:269
  90.8 1.4 %shard_map.127 = (bf16[16,144,256]{2,1,0:T(8,128)(2,1)S(1)}, f32[1,256]{1,0:T(1,128)S(1)}) custom-call(bf16[16,192,256]{2,1,0:T(8,128)(2,1)S(1)} %get-tuple-element.22.picked_ref, bf16[8,152,256]{2,1,0:T(8,128)(2,1)S(1)} %all_to_all.27.mine_ref, bf16[8,152,256]{2,1,0:T(8,128)(2,1)S(1)} %collective-permute-done.2.other_ref, s32[1536,4]{1,0:T(8,128)S(1)} %bitcast.35, ...), custom_call_target="tpu_custom_call" | custom-call | flops 1006632960 | bytes 2097152 | tf_op jit(solution)/shard_map/pallas_call | solution.py:275
  92.2 20.7 %all_to_all.28.part_ref = bf16[16,144,256]{2,1,0:T(8,128)(2,1)S(1)} all-to-all(bf16[16,144,256]{2,1,0:T(8,128)(2,1)S(1)} %get-tuple-element.23), channel_id=1, replica_groups=mesh['x'=4,'y'=4,'h'=2,'l'=4,'c'=2] {'y','x'}, dimensions={0} | all-to-all | bytes 2359296 | tf_op jit(solution)/shard_map/all_to_all | solution.py:219
  112.8 1.0 shard_map.128
  (29 shorter events, 0.2 us)
Async XLA Ops:
  0.6 9.7 %copy-start.5 = (s32[1,1,32,96]{3,2,1,0:T(8,128)S(1)}, s32[1,1,32,96]{3,2,1,0:T(8,128)}, u32[]{:S(2)}) copy-start(s32[1,1,32,96]{3,2,1,0:T(8,128)} %param.14) | copy-start | bytes 36868
  0.6 9.8 %copy-start.8 = (s32[1,1,32,4]{2,3,1,0:T(4,128)S(1)}, s32[1,1,32,4]{2,3,1,0:T(4,128)}, u32[]{:S(2)}) copy-start(s32[1,1,32,4]{2,3,1,0:T(4,128)} %param.17) | copy-start | bytes 1540
  0.7 10.3 %copy-start.6 = (s32[1,1,32,96]{3,2,1,0:T(8,128)S(1)}, s32[1,1,32,96]{3,2,1,0:T(8,128)}, u32[]{:S(2)}) copy-start(s32[1,1,32,96]{3,2,1,0:T(8,128)} %param.15) | copy-start | bytes 36868
  0.7 10.4 %copy-start.7 = (s32[1,1,32,96]{3,2,1,0:T(8,128)S(1)}, s32[1,1,32,96]{3,2,1,0:T(8,128)}, u32[]{:S(2)}) copy-start(s32[1,1,32,96]{3,2,1,0:T(8,128)} %param.16) | copy-start | bytes 36868
  2.7 23.6 %all-to-all-start = ((bf16[16,128,256]{2,1,0:T(8,128)(2,1)}), bf16[16,128,256]{2,1,0:T(8,128)(2,1)S(1)}, u32[]{:S(2)}, u32[]{:S(2)}) async-start(bf16[16,128,256]{2,1,0:T(8,128)(2,1)} %shard_map.120), calls=%async_computation | async-start | bytes 2097152 | tf_op jit(solution)/shard_map/all_to_all | solution.py:219
  11.1 8.4 %collective-permute-start = (s32[2,16,96]{2,1,0:T(8,128)S(1)}, s32[2,16,96]{2,1,0:T(8,128)S(1)}, u32[]{:S(2)}, u32[]{:S(2)}) collective-permute-start(s32[2,16,96]{2,1,0:T(8,128)S(1)} %dynamic-slice_bitcast_fusion), channel_id=1, source_target_pairs={{0,8},{8,0},{1,9},{9,1},{2,10},{10,2},{3,11},{11,3},{4,12},{12,4},... | collective-permute-start | bytes 36872 | tf_op jit(solution)/shard_map/ppermute | solution.py:223
  27.8 4.2 %collective-permute-start.1 = (bf16[2,512,256]{2,1,0:T(8,128)(2,1)S(1)}, bf16[2,512,256]{2,1,0:T(8,128)(2,1)S(1)}, u32[]{:S(2)}, u32[]{:S(2)}) collective-permute-start(bf16[2,512,256]{2,1,0:T(8,128)(2,1)S(1)} %get-tuple-element.17), channel_id=1, source_target_pairs={{0,1},{1,0},{2,3},{3,2},{4,5},{5,4},{6,7},{7,6},{8,9},{9,8},{10,11... | collective-permute-start | bytes 1572872 | tf_op jit(solution)/shard_map/ppermute | solution.py:223
  31.5 20.5 %copy-start = (bf16[256,256]{1,0:T(8,128)(2,1)S(1)}, bf16[256,256]{1,0:T(8,128)(2,1)}, u32[]{:S(2)}) copy-start(bf16[256,256]{1,0:T(8,128)(2,1)} %w_ref.3) | copy-start | bytes 393220
  31.5 20.5 %copy-start.1 = (bf16[128,256]{1,0:T(8,128)(2,1)S(1)}, bf16[128,256]{1,0:T(8,128)(2,1)}, u32[]{:S(2)}) copy-start(bf16[128,256]{1,0:T(8,128)(2,1)} %x_ref.3) | copy-start | bytes 196612
  31.5 20.5 %copy-start.2 = (bf16[128,256]{1,0:T(8,128)(2,1)S(1)}, bf16[128,256]{1,0:T(8,128)(2,1)}, u32[]{:S(2)}) copy-start(bf16[128,256]{1,0:T(8,128)(2,1)} %ct_ref.1) | copy-start | bytes 196612
  31.5 20.5 %copy-start.3 = (f32[128]{0:T(128)S(1)}, f32[128]{0:T(128)}, u32[]{:S(2)}) copy-start(f32[128]{0:T(128)} %param.12) | copy-start | bytes 1540
  31.5 20.5 %copy-start.4 = (f32[256]{0:T(256)S(1)}, f32[256]{0:T(256)}, u32[]{:S(2)}) copy-start(f32[256]{0:T(256)} %param.11) | copy-start | bytes 3076
  85.8 5.0 %collective-permute-start.2 = (bf16[8,152,256]{2,1,0:T(8,128)(2,1)S(1)}, bf16[8,152,256]{2,1,0:T(8,128)(2,1)S(1)}, u32[]{:S(2)}, u32[]{:S(2)}) collective-permute-start(bf16[8,152,256]{2,1,0:T(8,128)(2,1)S(1)} %all_to_all.27.mine_ref), channel_id=1, source_target_pairs={{0,1},{1,0},{2,3},{3,2},{4,5},{5,4},{6,7},{7,6},{8,9},{9,8},{10,11... | collective-permute-start | bytes 1867784 | tf_op jit(solution)/shard_map/ppermute | solution.py:223
